TPU v7x, 32 devices: a whole 2x2x4 slice. The times are simulated.
32 devices in a mesh: seq: 8 (over z, x), head: 4 (over y, core).
Axes of the slice: x: 2, y: 2, z: 4, core: 2. Of those that a mesh axis runs over, the one named last changes fastest.
Arguments:
- query_rows: bfloat16 [8192, 4096], P('seq', 'head'), may hold values from -6 to 6
- key_rows: bfloat16 [8192, 4096], P('seq', 'head'), may hold values from -6 to 6
- value_rows: bfloat16 [8192, 4096], P('seq', 'head'), may hold values from -6 to 6
- out_grads: bfloat16 [8192, 4096], P(('seq', 'head')), may hold values from -6 to 6
Outputs:
- query_grad: bfloat16 [8192, 4096], P('seq', 'head')
- key_grad: bfloat16 [8192, 4096], P('seq', 'head')
- value_grad: bfloat16 [8192, 4096], P('seq', 'head')
All inputs are finite; a program needn't handle non-finite values.
Results may differ from a plain program's by a relative error of at most 0.01.
Values may be sent and summed in bfloat16 or wider, within the bound.
No kernel may reach another device: no remote copies, remote signals or barrier semaphores. Data moves between devices by JAX's collectives and lax.ppermute only.
A program may use at most 128 MiB of HBM per device.

v0:
```python
import math

import jax
import jax.numpy as jnp
from jax import lax
from jax.sharding import PartitionSpec as P

HEAD_DIM = 128
GROUP = 512


def body(query_rows, key_rows, value_rows, out_grads):
    grad_rows = lax.all_to_all(out_grads, "head", split_axis=1, concat_axis=0, tiled=True)
    row_count = query_rows.shape[0]
    feat_width = query_rows.shape[1]
    head_count = feat_width // HEAD_DIM
    block_count = row_count // GROUP
    total_tokens = row_count * lax.axis_size("seq")
    factor = 1.0 / math.sqrt(HEAD_DIM * total_tokens)

    def split(array):
        return array.reshape(block_count, GROUP, head_count, HEAD_DIM)

    queries, keyset, valueset, grads = (
        split(query_rows),
        split(key_rows),
        split(value_rows),
        split(grad_rows),
    )
    kv_state = jnp.einsum(
        "cthi,cthj->chij", keyset, valueset, preferred_element_type=jnp.float32
    ).astype(jnp.bfloat16)
    grad_state = jnp.einsum(
        "cthi,cthj->chij", queries, grads, preferred_element_type=jnp.float32
    ).astype(jnp.bfloat16)
    all_kv, all_grad = (
        lax.all_gather(kv_state, "seq", axis=0, tiled=True),
        lax.all_gather(grad_state, "seq", axis=0, tiled=True),
    )
    global_ids = lax.axis_index("seq") * block_count + jnp.arange(block_count, dtype=jnp.int32)
    group_ids = jnp.arange(all_kv.shape[0], dtype=jnp.int32)
    before = (group_ids[None, :] < global_ids[:, None]).astype(jnp.bfloat16)
    after = (group_ids[None, :] > global_ids[:, None]).astype(jnp.bfloat16)
    prefix = jnp.einsum("cg,ghij->chij", before, all_kv, preferred_element_type=jnp.float32)
    suffix = jnp.einsum("cg,ghij->chij", after, all_grad, preferred_element_type=jnp.float32)
    prefix_low = prefix.astype(jnp.bfloat16)
    suffix_low = suffix.astype(jnp.bfloat16)
    causal = jnp.tril(jnp.ones((GROUP, GROUP), jnp.bool_))
    fwd_raw = jnp.einsum("cthi,cshi->chts", queries, keyset, preferred_element_type=jnp.float32)
    fwd_scores = jnp.where(causal[None, None], factor * fwd_raw, 0.0).astype(jnp.bfloat16)
    back_raw = jnp.einsum("cthj,cshj->chts", grads, valueset, preferred_element_type=jnp.float32)
    back_scores = jnp.where(causal[None, None], factor * back_raw, 0.0).astype(jnp.bfloat16)
    query_grad = jnp.einsum(
        "chts,cshi->cthi", back_scores, keyset, preferred_element_type=jnp.float32
    )
    query_grad = query_grad + factor * jnp.einsum(
        "cthj,chij->cthi", grads, prefix_low, preferred_element_type=jnp.float32
    )
    key_grad = jnp.einsum(
        "chts,cthi->cshi", back_scores, queries, preferred_element_type=jnp.float32
    )
    key_grad = key_grad + factor * jnp.einsum(
        "cshj,chij->cshi", valueset, suffix_low, preferred_element_type=jnp.float32
    )
    value_grad = jnp.einsum(
        "chts,cthj->cshj", fwd_scores, grads, preferred_element_type=jnp.float32
    )
    value_grad = value_grad + factor * jnp.einsum(
        "cshi,chij->cshj", keyset, suffix_low, preferred_element_type=jnp.float32
    )
    return (
        query_grad.reshape(row_count, feat_width).astype(jnp.bfloat16),
        key_grad.reshape(row_count, feat_width).astype(jnp.bfloat16),
        value_grad.reshape(row_count, feat_width).astype(jnp.bfloat16),
    )


def solution(mesh):
    return jax.shard_map(
        body,
        mesh=mesh,
        in_specs=(P("seq", "head"), P("seq", "head"), P("seq", "head"), P(("seq", "head"), None)),
        out_specs=(P("seq", "head"), P("seq", "head"), P("seq", "head")),
        check_vma=False,
    )
```

profile of v0, /device:TPU:0, one launch (start us, length us, event | category | flops | bytes accessed | tf_op | source)
XLA Modules:
  0.0 208.6 jit_solution(10398035131109611767)
XLA Ops:
  7.2 0.0 all-gather.3.cloned.1.call-start
  7.2 0.0 copy-start.6
  7.2 2.4 %copy.76 = bf16[128,8,8,128]{3,2,1,0:T(8,128)(2,1)S(1)} copy(bf16[128,8,8,128]{3,1,2,0:T(8,128)(2,1)} %bitcast.81) | data formatting | bytes 4194304
  9.6 0.0 copy-done.6
  9.6 0.6 copy.75
  10.2 0.0 copy-start.2
  10.2 1.3 copy-done.2
  11.6 1.9 fusion.34
  13.5 0.0 all-gather.3.cloned.1.call-update
  13.5 3.1 %copy.134 = bf16[32,4,8,1024]{3,2,0,1:T(8,128)(2,1)} copy(bf16[32,4,8,1024]{3,2,1,0:T(8,128)(2,1)} %bitcast.83) | data formatting | bytes 4194304 | tf_op jit(solution)/shard_map/all_to_all | solution.py:13
  16.6 4.5 %all-to-all-start = ((bf16[256,4,1024]{2,0,1:T(8,128)(2,1)}), bf16[256,4,1024]{2,0,1:T(8,128)(2,1)}, u32[]{:S(2)}, u32[]{:S(2)}) async-start(bf16[256,4,1024]{2,0,1:T(8,128)(2,1)} %bitcast.74), calls=%async_computation | async-start | bytes 4194304 | tf_op jit(solution)/shard_map/all_to_all | solution.py:13
  21.1 0.2 all-gather.5.cloned.1.call-start
  21.4 3.6 %copy.78 = bf16[128,8,8,128]{3,2,1,0:T(8,128)(2,1)} copy(bf16[128,8,8,128]{3,1,2,0:T(8,128)(2,1)} %bitcast.84) | data formatting | bytes 4194304
  24.9 22.6 %all-to-all-done = bf16[256,4,1024]{2,0,1:T(8,128)(2,1)} async-done(((bf16[256,4,1024]{2,0,1:T(8,128)(2,1)}), bf16[256,4,1024]{2,0,1:T(8,128)(2,1)}, u32[]{:S(2)}, u32[]{:S(2)}) %all-to-all-start) | async-done | bytes 2097184 | tf_op jit(solution)/shard_map/all_to_all | solution.py:13
  47.5 0.0 copy-start.5
  47.5 2.4 %copy.74 = bf16[128,8,8,128]{3,2,1,0:T(8,128)(2,1)S(1)} copy(bf16[128,8,8,128]{3,1,2,0:T(8,128)(2,1)} %bitcast.16) | data formatting | bytes 4194304
  49.8 0.0 copy-start.4
  49.9 1.3 copy-done.4
  51.2 0.0 copy-done.5
  51.2 1.9 fusion.39
  53.1 0.0 all-gather.5.cloned.1.call-update
  53.1 0.1 iota_compare_fusion
  53.2 8.0 %select_convert_fusion.1 = bf16[2,8,512,512]{3,2,1,0:T(8,128)(2,1)} fusion(pred[512,512]{1,0:T(8,128)(4,1)S(1)} %iota_compare_fusion, bf16[2,512,8,128]{3,2,1,0:T(8,128)(2,1)} %bitcast.68, bf16[2,512,8,128]{3,2,1,0:T(8,128)(2,1)} %bitcast.71), kind=kOutput, calls=%fused_computation.1 | convolution fusion | flops 1086324736 | bytes 12845056 | tf_op jit(solution)/shard_map/cthj,cshj->chts/dot_general | solution.py:51
  61.2 28.5 %all-gather.3.cloned.1.call-done = bf16[16,8,128,128]{3,2,1,0:T(8,128)(2,1)} async-done(((bf16[2,8,128,128]{3,2,1,0:T(8,128)(2,1)}), bf16[16,8,128,128]{3,2,1,0:T(8,128)(2,1)}) %all-gather.3.cloned.1.call-update) | async-done | bytes 4194320 | tf_op jit(solution)/shard_map/all_gather | solution.py:37
  89.7 0.0 copy-start.1
  89.7 4.9 %fusion.44 = bf16[2,8,128,128]{3,0,2,1:T(2,128)(2,1)S(1)} fusion(bf16[16,8,128,128]{3,2,1,0:T(8,128)(2,1)} %all-gather.3.cloned.1.call-done, s32[2]{0:T(128)S(1)} %iota_add_fusion), kind=kOutput, calls=%fused_computation.42 | convolution fusion | flops 8650784 | bytes 4718600 | tf_op jit(solution)/shard_map/cg,ghij->chij/dot_general | solution.py:44
  94.6 2.3 %fusion.31 = f32[2,8,128,512]{2,3,1,0:T(8,128)S(1)} fusion(bf16[2,512,8,128]{3,2,1,0:T(8,128)(2,1)} %bitcast.72, bf16[2,8,128,128]{3,0,2,1:T(2,128)(2,1)S(1)} %fusion.44), kind=kOutput, calls=%fused_computation.37 | convolution fusion | flops 268435456 | bytes 6815744 | tf_op jit(solution)/shard_map/cthj,chij->cthi/dot_general | solution.py:56
  96.9 0.0 copy-done.1
  96.9 2.4 %fusion.8 = bf16[2,512,8,128]{3,1,2,0:T(8,128)(2,1)S(1)} fusion(f32[2,8,128,512]{2,3,1,0:T(8,128)S(1)} %fusion.31, bf16[2,8,512,512]{3,2,1,0:T(8,128)(2,1)S(1)} %copy-done.1, bf16[2,512,8,128]{3,2,1,0:T(8,128)(2,1)S(1)} %bitcast.64), kind=kOutput, calls=%fused_computation.12 | convolution fusion | flops 1076887552 | bytes 16777216 | tf_op jit(solution)/shard_map/chts,cshi->cthi/dot_general | solution.py:53
  99.3 1.4 copy.48
  100.7 2.1 %copy.133 = bf16[128,8,8,128]{3,1,2,0:T(8,128)(2,1)} copy(bf16[128,8,8,128]{3,2,1,0:T(8,128)(2,1)S(1)} %bitcast.75) | data formatting | bytes 4194304
  102.8 60.8 %all-gather.5.cloned.1.call-done = bf16[16,8,128,128]{3,2,1,0:T(8,128)(2,1)} async-done(((bf16[2,8,128,128]{3,2,1,0:T(8,128)(2,1)}), bf16[16,8,128,128]{3,2,1,0:T(8,128)(2,1)}) %all-gather.5.cloned.1.call-update) | async-done | bytes 4194320 | tf_op jit(solution)/shard_map/all_gather | solution.py:38
  163.6 4.7 %fusion.47 = bf16[2,8,128,128]{3,0,2,1:T(2,128)(2,1)S(1)} fusion(bf16[16,8,128,128]{3,2,1,0:T(8,128)(2,1)} %all-gather.5.cloned.1.call-done, s32[2]{0:T(128)S(1)} %iota_add_fusion), kind=kOutput, calls=%fused_computation.43 | convolution fusion | flops 8650784 | bytes 4718600 | tf_op jit(solution)/shard_map/cg,ghij->chij/dot_general | solution.py:45
  168.3 0.5 copy.62
  168.8 0.0 copy-start.3
  168.8 2.7 %fusion.24 = f32[2,8,128,512]{2,3,1,0:T(8,128)} fusion(bf16[2,8,128,128]{2,3,1,0:T(8,128)(2,1)S(1)} %copy.62, bf16[2,512,8,128]{3,2,1,0:T(8,128)(2,1)S(1)} %bitcast.65), kind=kOutput, calls=%fused_computation.31 | convolution fusion | flops 268435456 | bytes 6815744 | tf_op jit(solution)/shard_map/cshi,chij->cshj/dot_general | solution.py:68
  171.5 0.0 copy-done.3
  171.5 2.6 %fusion.18 = f32[2,8,128,512]{2,3,1,0:T(8,128)} fusion(bf16[2,8,128,128]{2,3,1,0:T(8,128)(2,1)S(1)} %copy.62, bf16[2,512,8,128]{3,2,1,0:T(8,128)(2,1)S(1)} %bitcast.69), kind=kOutput, calls=%fused_computation.25 | convolution fusion | flops 268435456 | bytes 6815744 | tf_op jit(solution)/shard_map/cshj,chij->cshi/dot_general | solution.py:62
  174.1 10.1 %fusion.6 = bf16[2,512,8,128]{3,1,2,0:T(8,128)(2,1)} fusion(f32[2,8,128,512]{2,3,1,0:T(8,128)} %fusion.24, pred[512,512]{1,0:T(8,128)(4,1)S(1)} %iota_compare_fusion, bf16[2,512,8,128]{3,2,1,0:T(8,128)(2,1)} %bitcast.78, bf16[2,512,8,128]{3,2,1,0:T(8,128)(2,1)S(1)} %bitcast.66, bf16[2,512,8,128]{3,2,1,0:T(8,128)(2,1)} %bitcast.73), kind=kOutput, calls=%fused_computation.8 | convolution fusion | flops 2163212288 | bytes 12845056 | tf_op jit(solution)/shard_map/chts,cthj->cshj/dot_general | solution.py:65
  184.2 0.0 copy-start
  184.2 3.1 %copy.65 = bf16[2,512,8,128]{3,2,1,0:T(8,128)(2,1)S(1)} copy(bf16[2,512,8,128]{3,1,2,0:T(8,128)(2,1)} %fusion.6) | data formatting | bytes 4194304 | tf_op jit(solution)/shard_map/convert_element_type | solution.py:74
  187.2 0.0 copy-done
  187.3 8.2 %fusion.7 = bf16[2,512,8,128]{3,1,2,0:T(8,128)(2,1)} fusion(f32[2,8,128,512]{2,3,1,0:T(8,128)S(1)} %copy-done, bf16[2,8,512,512]{3,2,1,0:T(8,128)(2,1)} %select_convert_fusion.1, bf16[2,512,8,128]{3,2,1,0:T(8,128)(2,1)} %bitcast.79), kind=kOutput, calls=%fused_computation.10 | convolution fusion | flops 1076887552 | bytes 16777216 | tf_op jit(solution)/shard_map/chts,cthi->cshi/dot_general | solution.py:59
  195.5 2.9 %copy.57 = bf16[2,512,8,128]{3,2,1,0:T(8,128)(2,1)S(1)} copy(bf16[2,512,8,128]{3,1,2,0:T(8,128)(2,1)} %fusion.7) | data formatting | bytes 4194304 | tf_op jit(solution)/shard_map/convert_element_type | solution.py:73
  198.4 3.3 %copy_bitcast_fusion = (bf16[1024,1024]{1,0:T(8,128)(2,1)}, bf16[1024,1024]{1,0:T(8,128)(2,1)}) fusion(bf16[128,8,8,128]{3,2,1,0:T(8,128)(2,1)S(1)} %bitcast.76, bf16[128,8,8,128]{3,2,1,0:T(8,128)(2,1)S(1)} %bitcast.77), kind=kLoop, calls=%fused_computation.17 | loop fusion | bytes 8388608 | tf_op jit(solution)/shard_map/convert_element_type | solution.py:74
  (1 shorter events, 0.0 us)
Async XLA Ops:
  7.2 82.6 %all-gather.3.cloned.1.call-start = ((), (), s32[]{:S(2)}) async-start(), calls=%async_computation.1 | async-start | bytes 4718592 | tf_op jit(solution)/shard_map/all_gather | solution.py:37
  7.2 2.4 %copy-start.6 = (bf16[1024,1024]{1,0:T(8,128)(2,1)S(1)}, bf16[1024,1024]{1,0:T(8,128)(2,1)}, u32[]{:S(2)}) copy-start(bf16[1024,1024]{1,0:T(8,128)(2,1)} %param.6) | copy-start | bytes 6291460
  10.2 1.3 copy-start.2
  16.6 30.8 %all-to-all-start = ((bf16[256,4,1024]{2,0,1:T(8,128)(2,1)}), bf16[256,4,1024]{2,0,1:T(8,128)(2,1)}, u32[]{:S(2)}, u32[]{:S(2)}) async-start(bf16[256,4,1024]{2,0,1:T(8,128)(2,1)} %bitcast.74), calls=%async_computation | async-start | bytes 4194304 | tf_op jit(solution)/shard_map/all_to_all | solution.py:13
  21.1 142.4 %all-gather.5.cloned.1.call-start = ((), (), s32[]{:S(2)}) async-start(), calls=%async_computation.2 | async-start | bytes 4718592 | tf_op jit(solution)/shard_map/all_gather | solution.py:38
  47.5 3.7 %copy-start.5 = (bf16[128,8,8,128]{3,2,1,0:T(8,128)(2,1)S(1)}, bf16[128,8,8,128]{3,2,1,0:T(8,128)(2,1)}, u32[]{:S(2)}) copy-start(bf16[128,8,8,128]{3,2,1,0:T(8,128)(2,1)} %copy.78) | copy-start | bytes 6291460
  49.8 1.3 copy-start.4
  89.7 7.2 %copy-start.1 = (bf16[2,8,512,512]{3,2,1,0:T(8,128)(2,1)S(1)}, bf16[2,8,512,512]{3,2,1,0:T(8,128)(2,1)}, u32[]{:S(2)}) copy-start(bf16[2,8,512,512]{3,2,1,0:T(8,128)(2,1)} %select_convert_fusion.1) | copy-start | bytes 25165828
  168.8 2.7 %copy-start.3 = (bf16[128,8,8,128]{3,2,1,0:T(8,128)(2,1)S(1)}, bf16[128,8,8,128]{3,2,1,0:T(8,128)(2,1)}, u32[]{:S(2)}) copy-start(bf16[128,8,8,128]{3,2,1,0:T(8,128)(2,1)} %copy-done.2) | copy-start | bytes 6291460
  184.2 3.1 %copy-start = (f32[2,8,128,512]{2,3,1,0:T(8,128)S(1)}, f32[2,8,128,512]{2,3,1,0:T(8,128)}, u32[]{:S(2)}) copy-start(f32[2,8,128,512]{2,3,1,0:T(8,128)} %fusion.18) | copy-start | bytes 12582916
Sparse Core Ops, SparseCore 0:
  13.6 76.0 all-gather.2
  91.9 71.6 all-gather.4
where the time goes:
time: 209 us
  waiting for transfers between devices  112 us (54%)
  matrix products  49.7 us (24%)
  local copies, waits for them, and re-layouts  28 us (13%)
  between operations  14.2 us (7%)
  starting transfers between devices  4.74 us (2%)
    all_gather x1, waiting for transfers between devices, body(): lax.all_gather(grad_state, 'seq', axis=0, tiled=True)  60.8 us
    all_gather x1, waiting for transfers between devices, body(): lax.all_gather(kv_state, 'seq', axis=0, tiled=True)  28.5 us
    all_to_all x1, waiting for transfers between devices, body(): lax.all_to_all(out_grads, 'head', split_axis=1, concat_axis=0, tiled=True)  22.6 us
    unnamed x19, local copies, waits for them, and re-layouts  13.7 us
    dot_general x1, matrix products, body(): jnp.einsum('chts,cthj->cshj', fwd_scores, grads, preferred_element_type=j...  10.1 us
    dot_general x1, matrix products, body(): jnp.einsum('chts,cthi->cshi', back_scores, queries, preferred_element_typ...  8.22 us
    dot_general x1, matrix products, body(): jnp.einsum('cthj,cshj->chts', grads, valueset, preferred_element_type=jnp...  8 us
    convert_element_type x2, local copies, waits for them, and re-layouts, body(): value_grad.reshape(row_count, feat_width).astype(jnp.bfloat16)  6.43 us
  transfers between devices with their start and end apart: 3, of which 3 were waited for; matrix products, arithmetic and copies ran while one was open for 15% of the time, Pallas kernels for 0%

commit v1 on v0

v1 whole, which is shorter than its diff:
```python
import functools
import math

import jax
import jax.numpy as jnp
from jax import lax
from jax.experimental import pallas as pl
from jax.experimental.pallas import tpu as pltpu
from jax.sharding import PartitionSpec as P

HEAD_DIM = 128
SPLITS = (4, 2, 2)
F32 = jnp.float32
BF16 = jnp.bfloat16
NN = (((1,), (0,)), ((), ()))
NT = (((1,), (1,)), ((), ()))
TN = (((0,), (0,)), ((), ()))


def dot(a, b, dims):
    return lax.dot_general(a, b, dims, preferred_element_type=F32)


def params(**kw):
    return pltpu.CompilerParams(vmem_limit_bytes=48 * 1024 * 1024, **kw)


def cost(flops, bytes_accessed):
    return pl.CostEstimate(flops=int(flops), bytes_accessed=int(bytes_accessed), transcendentals=0)


def head_cols(h):
    return slice(h * HEAD_DIM, (h + 1) * HEAD_DIM)


def kv_kernel(heads, chunk, k_ref, v_ref, local_ref, total_ref):
    chunks = k_ref.shape[0] // chunk
    for h in range(heads):
        run = jnp.zeros((HEAD_DIM, HEAD_DIM), F32)
        for c in range(chunks):
            rows = slice(c * chunk, (c + 1) * chunk)
            local_ref[c, h] = run.astype(BF16)
            run = run + dot(v_ref[rows, head_cols(h)], k_ref[rows, head_cols(h)], TN)
        total_ref[h] = run.astype(BF16)


def kv_states(key_rows, value_rows, chunk, heads=4):
    rows, width = key_rows.shape
    head_count = width // HEAD_DIM
    chunks = rows // chunk
    spec = pl.BlockSpec((rows, heads * HEAD_DIM), lambda i: (0, i))
    return pl.pallas_call(
        functools.partial(kv_kernel, heads, chunk),
        grid=(head_count // heads,),
        in_specs=[spec, spec],
        out_specs=[
            pl.BlockSpec((chunks, heads, HEAD_DIM, HEAD_DIM), lambda i: (0, i, 0, 0)),
            pl.BlockSpec((heads, HEAD_DIM, HEAD_DIM), lambda i: (i, 0, 0)),
        ],
        out_shape=[
            jax.ShapeDtypeStruct((chunks, head_count, HEAD_DIM, HEAD_DIM), BF16),
            jax.ShapeDtypeStruct((head_count, HEAD_DIM, HEAD_DIM), BF16),
        ],
        compiler_params=params(),
        cost_estimate=cost(2 * rows * width * HEAD_DIM, 4 * rows * width),
        name="kv_states",
    )(key_rows, value_rows)


def intra_kernel(heads, with_state, place_ref, *refs):
    ins, outs = refs[:8], refs[8:]
    size = ins[0].shape[0]
    row = lax.broadcasted_iota(jnp.int32, (size, size), 0)
    col = lax.broadcasted_iota(jnp.int32, (size, size), 1)
    keep = row <= col
    for piece in range(2):
        q_ref, k_ref, v_ref, g_ref = ins[4 * piece : 4 * piece + 4]
        for h in range(heads):
            cols = head_cols(h)
            q, k, v, g = q_ref[:, cols], k_ref[:, cols], v_ref[:, cols], g_ref[:, cols]
            fwd = jnp.where(keep, dot(k, q, NT), 0.0).astype(BF16)
            back = jnp.where(keep, dot(v, g, NT), 0.0).astype(BF16)
            outs[0][piece, :, cols] = dot(back, k, TN).astype(outs[0].dtype)
            outs[1][piece, :, cols] = dot(back, q, NN).astype(outs[1].dtype)
            outs[2][piece, :, cols] = dot(fwd, g, NN).astype(outs[2].dtype)
            if with_state:
                outs[3][piece, h] = dot(q, g, TN).astype(BF16)


def intra(place, piece0, arrays, grads, first_own, head0, head_count, chunk, with_state, heads):
    width = heads * HEAD_DIM
    base = head0 // heads
    full = arrays[0].shape[1] // width

    def rows_spec(piece):
        return pl.BlockSpec((chunk, width), lambda i, place: (place[piece], i + base))

    def grad_spec(own):
        if own:
            return pl.BlockSpec((chunk, width), lambda i, place: (0, place[0] * full + i))
        return pl.BlockSpec((chunk, width), lambda i, place: (0, i))

    in_specs, operands = [], []
    for j in range(2):
        in_specs += [rows_spec(piece0 + j)] * 3 + [grad_spec(first_own and j == 0)]
        operands += list(arrays) + [grads[j]]
    out_specs = [pl.BlockSpec((2, chunk, width), lambda i, place: (0, 0, i))] * 3
    out_shape = [jax.ShapeDtypeStruct((2, chunk, head_count * HEAD_DIM), BF16)] * 3
    if with_state:
        out_specs.append(pl.BlockSpec((2, heads, HEAD_DIM, HEAD_DIM), lambda i, place: (0, i, 0, 0)))
        out_shape.append(jax.ShapeDtypeStruct((2, head_count, HEAD_DIM, HEAD_DIM), BF16))
    return pl.pallas_call(
        functools.partial(intra_kernel, heads, with_state),
        grid_spec=pltpu.PrefetchScalarGridSpec(
            num_scalar_prefetch=1,
            grid=(head_count // heads,),
            in_specs=in_specs,
            out_specs=out_specs,
        ),
        out_shape=out_shape,
        compiler_params=params(),
        cost_estimate=cost(
            2 * head_count * 10 * chunk * chunk * HEAD_DIM, 2 * 14 * chunk * head_count * HEAD_DIM
        ),
        name="intra",
    )(place, *operands)


def grad_state_kernel(heads, place_ref, q0, q1, g0, g1, near_ref, state_ref, total_ref):
    for h in range(heads):
        cols = head_cols(h)
        a = dot(q0[:, cols], g0[:, cols], TN)
        b = dot(q1[:, cols], g1[:, cols], TN)
        state_ref[0, h] = a.astype(BF16)
        state_ref[1, h] = b.astype(BF16)
        total = a + b + near_ref[0, h].astype(F32) + near_ref[1, h].astype(F32)
        total_ref[h] = total.astype(BF16)


def grad_states(place, query_rows, grads, near, head0, head_count, chunk):
    width = head_count * HEAD_DIM
    block = head0 // head_count

    def rows_spec(piece):
        return pl.BlockSpec((chunk, width), lambda i, place: (place[piece], block))

    whole = pl.BlockSpec((chunk, width), lambda i, place: (0, 0))
    return pl.pallas_call(
        functools.partial(grad_state_kernel, head_count),
        grid_spec=pltpu.PrefetchScalarGridSpec(
            num_scalar_prefetch=1,
            grid=(1,),
            in_specs=[
                rows_spec(2),
                rows_spec(3),
                whole,
                whole,
                pl.BlockSpec((2, head_count, HEAD_DIM, HEAD_DIM), lambda i, place: (0, block, 0, 0)),
            ],
            out_specs=[
                pl.BlockSpec((2, head_count, HEAD_DIM, HEAD_DIM), lambda i, place: (0, 0, 0, 0)),
                pl.BlockSpec((head_count, HEAD_DIM, HEAD_DIM), lambda i, place: (0, 0, 0)),
            ],
        ),
        out_shape=[
            jax.ShapeDtypeStruct((2, head_count, HEAD_DIM, HEAD_DIM), BF16),
            jax.ShapeDtypeStruct((head_count, HEAD_DIM, HEAD_DIM), BF16),
        ],
        compiler_params=params(),
        cost_estimate=cost(4 * chunk * width * HEAD_DIM, 8 * chunk * width),
        name="grad_states",
    )(place, query_rows, query_rows, *grads, near)


def finish_kernel(chunk, factor, rounds, aliased, place_ref, *refs):
    refs = list(refs)
    if aliased:
        refs = refs[3:]
    k_ref, v_ref = refs[:2]
    g_refs = refs[2:6]
    near = refs[6:9]
    far = refs[9:12]
    near_state, far_state, local_ref = refs[12:15]
    kv_in = refs[15 : 15 + rounds]
    grad_in = refs[15 + rounds : 15 + 2 * rounds]
    dq_ref, dk_ref, dv_ref = refs[15 + 2 * rounds :]
    odd = place_ref[4].astype(F32)
    prefix = kv_in[0][0].astype(F32) * odd
    suffix = grad_in[0][0].astype(F32) * (1.0 - odd)
    for r in range(1, rounds):
        prefix = prefix + kv_in[r][0].astype(F32)
        suffix = suffix + grad_in[r][0].astype(F32)
    states = [near_state[0, 0], near_state[1, 0], far_state[0, 0], far_state[1, 0]]
    states = [s.astype(F32) for s in states]
    for piece in range(4):
        place = place_ref[piece]
        rows = pl.ds(pl.multiple_of(place * chunk, chunk), chunk)
        part = near if piece < 2 else far
        prefix_low = (prefix + local_ref[place, 0].astype(F32)).astype(BF16)
        after = suffix
        for other in range(4):
            if other != piece:
                later = (place_ref[other] > place).astype(F32)
                after = after + later * states[other]
        after_low = after.astype(BF16)
        out = part[0][piece % 2].astype(F32) + dot(g_refs[piece][...], prefix_low, NN)
        dq_ref[rows, :] = (factor * out).astype(BF16)
        out = part[1][piece % 2].astype(F32) + dot(v_ref[rows, :], after_low, NT)
        dk_ref[rows, :] = (factor * out).astype(BF16)
        out = part[2][piece % 2].astype(F32) + dot(k_ref[rows, :], after_low, NN)
        dv_ref[rows, :] = (factor * out).astype(BF16)


def finish(
    place, key_rows, value_rows, grads, near, far, near_state, far_state, local, kv_in, grad_in,
    head0, head_count, chunk, factor, outs,
):
    rows, feat = key_rows.shape
    full = feat // HEAD_DIM
    rounds = len(kv_in)
    wide = pl.BlockSpec((rows, HEAD_DIM), lambda i, place: (0, i + head0))

    def piece_spec(shift):
        return pl.BlockSpec((chunk, HEAD_DIM), lambda i, place: (0, i + shift))

    def pair_spec(shift):
        return pl.BlockSpec((2, chunk, HEAD_DIM), lambda i, place: (0, 0, i + shift))

    def states_spec(count, shift):
        return pl.BlockSpec(
            (count, 1, HEAD_DIM, HEAD_DIM), lambda i, place: (0, i + shift, 0, 0)
        )

    def state_spec(shift):
        return pl.BlockSpec((1, HEAD_DIM, HEAD_DIM), lambda i, place: (i + shift, 0, 0))

    own = pl.BlockSpec((chunk, HEAD_DIM), lambda i, place: (0, place[0] * full + i + head0))
    in_specs = [wide, wide, own, piece_spec(head0), piece_spec(0), piece_spec(0)]
    in_specs += [pair_spec(head0)] * 3 + [pair_spec(0)] * 3
    in_specs += [states_spec(2, head0), states_spec(2, 0), states_spec(local.shape[0], head0)]
    in_specs += [state_spec(head0)] * rounds + [state_spec(0)] * rounds
    operands = [key_rows, value_rows, *grads, *near, *far, near_state, far_state, local]
    operands += [*kv_in, *grad_in]
    aliases = {}
    if outs is not None:
        in_specs = [pl.BlockSpec(memory_space=pl.ANY)] * 3 + in_specs
        operands = list(outs) + operands
        aliases = {1: 0, 2: 1, 3: 2}
    return pl.pallas_call(
        functools.partial(finish_kernel, chunk, factor, rounds, outs is not None),
        grid_spec=pltpu.PrefetchScalarGridSpec(
            num_scalar_prefetch=1,
            grid=(head_count,),
            in_specs=in_specs,
            out_specs=[wide] * 3,
        ),
        out_shape=[jax.ShapeDtypeStruct((rows, feat), BF16)] * 3,
        input_output_aliases=aliases,
        compiler_params=params(),
        cost_estimate=cost(
            6 * rows * head_count * HEAD_DIM * HEAD_DIM, 18 * rows * head_count * HEAD_DIM
        ),
        name="finish",
    )(place, *operands)


def seq_sums(total, axis, size, sign):
    other = lax.ppermute(total, axis, [(i, i ^ 1) for i in range(size)])
    parts = [other]
    window = total + other
    step = 2
    while step < size:
        pairs = [(i, i + sign * step) for i in range(size) if 0 <= i + sign * step < size]
        got = lax.ppermute(window, axis, pairs)
        parts.append(got)
        step *= 2
        if step < size:
            window = window + got
    return parts


def body(seq_size, head_size, query_rows, key_rows, value_rows, out_grads):
    rows, feat = query_rows.shape
    chunk = rows // head_size
    head_count = feat // HEAD_DIM
    factor = 1.0 / math.sqrt(HEAD_DIM * rows * seq_size)
    rank = lax.axis_index("head")
    odd = lax.axis_index("seq") % 2
    place = jnp.stack([rank, rank ^ 1, rank ^ 2, rank ^ 3, odd]).astype(jnp.int32)

    def exchange(mask, head0, heads):
        start = (rank ^ mask) * feat + head0 * HEAD_DIM
        block = lax.dynamic_slice(out_grads, (0, start), (chunk, heads * HEAD_DIM))
        return lax.ppermute(block, "head", [(i, i ^ mask) for i in range(head_size)])

    arrays = (query_rows, key_rows, value_rows)
    firsts = [sum(SPLITS[:s]) for s in range(len(SPLITS))]
    crossing = [[exchange(2, f, n), exchange(3, f, n)] for f, n in zip(firsts, SPLITS)]
    near_grad = exchange(1, 0, head_count)

    local, kv_total = kv_states(key_rows, value_rows, chunk)
    kv_in = seq_sums(kv_total, "seq", seq_size, 1)
    *near, near_state = intra(
        place, 0, arrays, (out_grads, near_grad), True, 0, head_count, chunk, True, 4
    )
    outs = None
    for f, n, grads in zip(firsts, SPLITS, crossing):
        far_state, total = grad_states(place, query_rows, grads, near_state, f, n, chunk)
        grad_in = seq_sums(total, "seq", seq_size, -1)
        far = intra(place, 2, arrays, grads, False, f, n, chunk, False, 2)
        outs = finish(
            place, key_rows, value_rows, (out_grads, near_grad, *grads), near, far, near_state,
            far_state, local, kv_in, grad_in, f, n, chunk, factor, outs,
        )
    return tuple(outs)


def solution(mesh):
    return jax.shard_map(
        functools.partial(body, mesh.shape["seq"], mesh.shape["head"]),
        mesh=mesh,
        in_specs=(P("seq", "head"), P("seq", "head"), P("seq", "head"), P(("seq", "head"), None)),
        out_specs=(P("seq", "head"), P("seq", "head"), P("seq", "head")),
        check_vma=False,
    )
```

time: 209 us -> 80.2 us (0.38)
  waiting for transfers between devices: 112 us -> 6.69 us
  matrix products: 49.7 us -> 0 us
  Pallas kernels: 0 us -> 35.4 us
  starting transfers between devices: 4.74 us -> 27.8 us
  local copies, waits for them, and re-layouts: 28 us -> 7.82 us
  between operations: 14.2 us -> 0.99 us
    all_gather x2 -> x0, waiting for transfers between devices: 89.3 us -> none  [the longest x1 60.8 us: body(): lax.all_gather(grad_state, 'seq', axis=0, tiled=True)]
    dot_general x11 -> x0, matrix products: 49.7 us -> none  [the longest x1 10.1 us: body(): jnp.einsum('chts,cthj->cshj', fwd_scores, grads, preferred_element_type=j...]
    pallas_call x0 -> x11, Pallas kernels: none -> 35.4 us  [the longest x4 18.8 us: intra(): pl.pallas_call(functools.partial(intra_kernel, heads, with_state), grid_s...]
    ppermute x0 -> x19, starting transfers between devices: none -> 27.8 us  [the longest x8 16.8 us: seq_sums(): got = lax.ppermute(window, axis, pairs)]
    all_to_all x1 -> x0, waiting for transfers between devices: 22.6 us -> none  [body(): lax.all_to_all(out_grads, 'head', split_axis=1, concat_axis=0, tiled=True)]
    convert_element_type x5 -> x0, local copies, waits for them, and re-layouts: 11.2 us -> none  [the longest x2 6.43 us: body(): value_grad.reshape(row_count, feat_width).astype(jnp.bfloat16)]
    unnamed x19 -> x16, local copies, waits for them, and re-layouts: 13.7 us -> 4.45 us
    ppermute x0 -> x19, waiting for transfers between devices: none -> 6.69 us  [the longest x4 5.24 us: seq_sums(): other = lax.ppermute(total, axis, [(i, i ^ 1) for i in range(size)])]
  transfers between devices with their start and end apart: 3 -> 19, of which waited for: 3 -> 4; matrix products, arithmetic and copies ran while one was open for 15% -> 3% of each run, Pallas kernels for 0% -> 40%
where the time goes in v1:
time: 80.2 us; the launch traced here: 79 us
  Pallas kernels  35.4 us (44%)
  starting transfers between devices  27.8 us (35%)
  local copies, waits for them, and re-layouts  7.82 us (10%)
  waiting for transfers between devices  6.69 us (8%)
  between operations  0.99 us (1%)
    pallas_call x4, Pallas kernels, intra(): pl.pallas_call(functools.partial(intra_kernel, heads, with_state), grid_s...  18.8 us
    ppermute x8, starting transfers between devices, seq_sums(): got = lax.ppermute(window, axis, pairs)  16.8 us
    pallas_call x3, Pallas kernels, finish(): pl.pallas_call(functools.partial(finish_kernel, chunk, factor, rounds, ou...  12.6 us
    ppermute x7, starting transfers between devices, exchange(): lax.ppermute(block, 'head', [(i, i ^ mask) for i in range(head_size)])  5.73 us
    ppermute x4, starting transfers between devices, seq_sums(): other = lax.ppermute(total, axis, [(i, i ^ 1) for i in range(size)])  5.28 us
    ppermute x4, waiting for transfers between devices, seq_sums(): other = lax.ppermute(total, axis, [(i, i ^ 1) for i in range(size)])  5.24 us
    unnamed x16, local copies, waits for them, and re-layouts  4.45 us
    dynamic_slice x3, local copies, waits for them, and re-layouts, exchange(): block = lax.dynamic_slice(out_grads, (0, start), (chunk, heads * HEAD_DIM))  3.28 us
  transfers between devices with their start and end apart: 19, of which 4 were waited for; matrix products, arithmetic and copies ran while one was open for 3% of the time, Pallas kernels for 40%

profile of v1, /device:TPU:0, one launch (start us, length us, event | category | flops | bytes accessed | tf_op | source)
XLA Modules:
  0.0 79.0 jit_solution(15006407571071324717)
XLA Ops:
  0.6 1.1 %constant_dynamic-slice_fusion.6 = bf16[256,1024]{1,0:T(8,128)(2,1)S(1)} fusion(bf16[256,4096]{1,0:T(8,128)(2,1)} %refs_5_.11, s32[]{:T(128)S(6)} %select_n.29), kind=kLoop, calls=%fused_computation.6 | loop fusion | bytes 1048580 | tf_op jit(solution)/shard_map/dynamic_slice | solution.py:293
  1.7 0.5 collective-permute-start
  2.2 1.6 %copy-done.1 = bf16[1024,1024]{1,0:T(8,128)(2,1)S(1)} copy-done((bf16[1024,1024]{1,0:T(8,128)(2,1)S(1)}, bf16[1024,1024]{1,0:T(8,128)(2,1)}, u32[]{:S(2)}) %copy-start.1) | copy-done | bytes 2097176
  3.8 1.6 %copy-done.3 = bf16[1024,1024]{1,0:T(8,128)(2,1)S(1)} copy-done((bf16[1024,1024]{1,0:T(8,128)(2,1)S(1)}, bf16[1024,1024]{1,0:T(8,128)(2,1)}, u32[]{:S(2)}) %copy-start.3) | copy-done | bytes 2097176
  5.4 1.3 %kv_states.1 = (bf16[4,8,128,128]{3,2,1,0:T(8,128)(2,1)S(1)}, bf16[8,128,128]{2,1,0:T(8,128)(2,1)S(1)}) custom-call(bf16[1024,1024]{1,0:T(8,128)(2,1)S(1)} %copy-done.1, bf16[1024,1024]{1,0:T(8,128)(2,1)S(1)} %copy-done.3), custom_call_target="tpu_custom_call" | custom-call | flops 268435456 | bytes 4194304 | tf_op jit(solution)/shard_map/kv_states/pallas_call | solution.py:52
  6.7 0.0 copy-start.4
  6.8 1.0 %copy-done.4 = bf16[4,8,128,128]{3,2,1,0:T(8,128)(2,1)} copy-done((bf16[4,8,128,128]{3,2,1,0:T(8,128)(2,1)}, bf16[4,8,128,128]{3,2,1,0:T(8,128)(2,1)S(1)}, u32[]{:S(2)}) %copy-start.4) | copy-done | bytes 1048600
  7.7 2.5 %collective-permute-start.3 = (bf16[8,128,128]{2,1,0:T(8,128)(2,1)S(1)}, bf16[8,128,128]{2,1,0:T(8,128)(2,1)S(1)}, u32[]{:S(2)}, u32[]{:S(2)}) collective-permute-start(bf16[8,128,128]{2,1,0:T(8,128)(2,1)S(1)} %get-tuple-element.39), channel_id=1, source_target_pairs={{0,4},{4,0},{8,12},{12,8},{16,20},{20,16},{24,28},{28,24},{1,5},{5... | collective-permute-start | bytes 786440 | tf_op jit(solution)/shard_map/ppermute | solution.py:268
  10.2 1.1 %constant_dynamic-slice_fusion.4 = (bf16[256,512]{1,0:T(8,128)(2,1)S(1)}, bf16[256,512]{1,0:T(8,128)(2,1)S(1)}) fusion(bf16[256,4096]{1,0:T(8,128)(2,1)} %refs_5_.11, s32[]{:T(128)S(6)} %select_n.31, s32[]{:T(128)S(6)} %select_n.30), kind=kLoop, calls=%fused_computation.4 | loop fusion | bytes 1048584 | tf_op jit(solution)/shard_map/dynamic_slice | solution.py:293
  11.3 1.6 %collective-permute-start.1 = (bf16[256,512]{1,0:T(8,128)(2,1)S(1)}, bf16[256,512]{1,0:T(8,128)(2,1)S(1)}, u32[]{:S(2)}, u32[]{:S(2)}) collective-permute-start(bf16[256,512]{1,0:T(8,128)(2,1)S(1)} %get-tuple-element.62), channel_id=1, source_target_pairs={{0,2},{1,3},{2,0},{3,1},{4,6},{5,7},{6,4},{7,5},{8,10},{9,11},{10,... | collective-permute-start | bytes 786440 | tf_op jit(solution)/shard_map/ppermute | solution.py:294
  12.9 0.0 collective-permute-start.2
  12.9 0.1 stack.23.place_ref
  13.0 4.2 %collective-permute-done.3.refs_15_.refs_18_ = bf16[8,128,128]{2,1,0:T(8,128)(2,1)S(1)} collective-permute-done((bf16[8,128,128]{2,1,0:T(8,128)(2,1)S(1)}, bf16[8,128,128]{2,1,0:T(8,128)(2,1)S(1)}, u32[]{:S(2)}, u32[]{:S(2)}) %collective-permute-start.3) | collective-permute-done | bytes 262176 | tf_op jit(solution)/shard_map/ppermute | solution.py:268
  17.2 0.1 add.73
  17.3 0.0 copy-start
  17.3 3.9 %collective-permute-start.4 = (bf16[8,128,128]{2,1,0:T(8,128)(2,1)S(1)}, bf16[8,128,128]{2,1,0:T(8,128)(2,1)S(1)}, u32[]{:S(2)}, u32[]{:S(2)}) collective-permute-start(bf16[8,128,128]{2,1,0:T(8,128)(2,1)S(1)} %add.73), channel_id=1, source_target_pairs={{0,8},{4,12},{8,16},{12,20},{16,24},{20,28},{1,9},{5,13},{9,17},{1... | collective-permute-start | bytes 786440 | tf_op jit(solution)/shard_map/ppermute | solution.py:274
  21.2 0.0 collective-permute-done.refs_7_.refs_3_.refs_6_
  21.2 7.9 %intra.4 = (bf16[2,256,1024]{2,1,0:T(8,128)(2,1)S(1)}, bf16[2,256,1024]{2,1,0:T(8,128)(2,1)S(1)}, bf16[2,256,1024]{2,1,0:T(8,128)(2,1)S(1)}, bf16[2,8,128,128]{3,2,1,0:T(8,128)(2,1)S(1)}) custom-call(s32[5]{0:T(128)S(1)} %stack.23.place_ref, bf16[1024,1024]{1,0:T(8,128)(2,1)} %q1.5, bf16[1024,1024]{1,0:T(8,128)(2,1)} %refs_3_.5, ...), custom_call_target="tpu_custom_call" | custom-call | flops 1342177280 | bytes 7340032 | tf_op jit(solution)/shard_map/intra/pallas_call | solution.py:112
  29.1 0.0 copy-start.5
  29.1 0.0 collective-permute-done.1.refs_3_.g0.refs_4_
  29.2 0.0 collective-permute-done.2.refs_7_.g1.refs_5_
  29.2 0.0 copy-done
  29.2 0.9 %grad_states.3 = (bf16[2,4,128,128]{3,2,1,0:T(8,128)(2,1)S(1)}, bf16[4,128,128]{2,1,0:T(8,128)(2,1)S(1)}) custom-call(s32[5]{0:T(128)S(1)} %stack.23.place_ref, bf16[1024,1024]{1,0:T(8,128)(2,1)S(1)} %copy-done, bf16[1024,1024]{1,0:T(8,128)(2,1)S(1)} %copy-done, bf16[256,512]{1,0:T(8,128)(2,1)S(1)} %collective-permute-done.1.refs_3_.g0.refs_4_, ...), custom_call_target="tpu_custom_call" | custom-call | flops 67108864 | bytes 1048576 | tf_op jit(solution)/shard_map/grad_states/pallas_call | solution.py:148
  30.1 0.3 copy-done.7
  30.4 1.5 %collective-permute-start.6 = (bf16[4,128,128]{2,1,0:T(8,128)(2,1)S(1)}, bf16[4,128,128]{2,1,0:T(8,128)(2,1)S(1)}, u32[]{:S(2)}, u32[]{:S(2)}) collective-permute-start(bf16[4,128,128]{2,1,0:T(8,128)(2,1)S(1)} %get-tuple-element.40), channel_id=1, source_target_pairs={{0,4},{4,0},{8,12},{12,8},{16,20},{20,16},{24,28},{28,24},{1,5},{5... | collective-permute-start | bytes 393224 | tf_op jit(solution)/shard_map/ppermute | solution.py:268
  31.9 1.1 %constant_dynamic-slice_fusion = (bf16[256,256]{1,0:T(8,128)(2,1)S(1)}, bf16[256,256]{1,0:T(8,128)(2,1)S(1)}, bf16[256,256]{1,0:T(8,128)(2,1)S(1)}, bf16[256,256]{1,0:T(8,128)(2,1)S(1)}) fusion(bf16[256,4096]{1,0:T(8,128)(2,1)} %refs_5_.11, s32[]{:T(128)S(6)} %select_n.35, s32[]{:T(128)S(6)} %select_n.34, s32[]{:T(128)S(6)} %select_n.33, s32[]{:T(128)S(6)} %select_n.32), kind=kLoop, calls=%fused_computation | loop fusion | bytes 1048592 | tf_op jit(solution)/shard_map/dynamic_slice | solution.py:293
  33.1 1.6 %collective-permute-start.9 = (bf16[256,256]{1,0:T(8,128)(2,1)S(1)}, bf16[256,256]{1,0:T(8,128)(2,1)S(1)}, u32[]{:S(2)}, u32[]{:S(2)}) collective-permute-start(bf16[256,256]{1,0:T(8,128)(2,1)S(1)} %get-tuple-element.60), channel_id=1, source_target_pairs={{0,2},{1,3},{2,0},{3,1},{4,6},{5,7},{6,4},{7,5},{8,10},{9,11},{10,... | collective-permute-start | bytes 393224 | tf_op jit(solution)/shard_map/ppermute | solution.py:294
  34.6 0.0 collective-permute-start.10
  34.6 0.6 collective-permute-start.14
  35.2 0.0 collective-permute-done.4.refs_16_.refs_19_
  35.2 1.4 %collective-permute-start.15 = (bf16[256,256]{1,0:T(8,128)(2,1)S(1)}, bf16[256,256]{1,0:T(8,128)(2,1)S(1)}, u32[]{:S(2)}, u32[]{:S(2)}) collective-permute-start(bf16[256,256]{1,0:T(8,128)(2,1)S(1)} %get-tuple-element.57), channel_id=1, source_target_pairs={{0,3},{1,2},{2,1},{3,0},{4,7},{5,6},{6,5},{7,4},{8,11},{9,10},{10,... | collective-permute-start | bytes 393224 | tf_op jit(solution)/shard_map/ppermute | solution.py:294
  36.6 0.1 add.74
  36.7 0.0 collective-permute-done.6.refs_18_
  36.8 1.3 %collective-permute-start.7 = (bf16[4,128,128]{2,1,0:T(8,128)(2,1)S(1)}, bf16[4,128,128]{2,1,0:T(8,128)(2,1)S(1)}, u32[]{:S(2)}, u32[]{:S(2)}) collective-permute-start(bf16[4,128,128]{2,1,0:T(8,128)(2,1)S(1)} %add.75), channel_id=1, source_target_pairs={{8,0},{12,4},{16,8},{20,12},{24,16},{28,20},{9,1},{13,5},{17,9},{2... | collective-permute-start | bytes 393224 | tf_op jit(solution)/shard_map/ppermute | solution.py:274
  38.1 0.5 collective-permute-done.9.refs_3_.g0.refs_7_
  38.6 5.0 %collective-permute-start.5 = (bf16[8,128,128]{2,1,0:T(8,128)(2,1)S(1)}, bf16[8,128,128]{2,1,0:T(8,128)(2,1)S(1)}, u32[]{:S(2)}, u32[]{:S(2)}) collective-permute-start(bf16[8,128,128]{2,1,0:T(8,128)(2,1)S(1)} %add.74), channel_id=1, source_target_pairs={{0,16},{4,20},{8,24},{12,28},{1,17},{5,21},{9,25},{13,29},{2,18},{... | collective-permute-start | bytes 786440 | tf_op jit(solution)/shard_map/ppermute | solution.py:274
  43.6 0.0 collective-permute-done.10.refs_7_.g1.refs_8_
  43.6 0.9 %grad_states.4 = (bf16[2,2,128,128]{3,2,1,0:T(8,128)(2,1)S(1)}, bf16[2,128,128]{2,1,0:T(8,128)(2,1)S(1)}) custom-call(s32[5]{0:T(128)S(1)} %stack.23.place_ref, bf16[1024,1024]{1,0:T(8,128)(2,1)S(1)} %copy-done, bf16[1024,1024]{1,0:T(8,128)(2,1)S(1)} %copy-done, bf16[256,256]{1,0:T(8,128)(2,1)S(1)} %collective-permute-done.9.refs_3_.g0.refs_7_, ...), custom_call_target="tpu_custom_call" | custom-call | flops 33554432 | bytes 524288 | tf_op jit(solution)/shard_map/grad_states/pallas_call | solution.py:148
  44.5 0.0 copy-start.2
  44.5 0.6 collective-permute-start.11
  45.2 0.0 collective-permute-done.14.refs_3_.g0.refs_7_
  45.2 0.9 %collective-permute-done.15.refs_7_.g1.refs_8_ = bf16[256,256]{1,0:T(8,128)(2,1)S(1)} collective-permute-done((bf16[256,256]{1,0:T(8,128)(2,1)S(1)}, bf16[256,256]{1,0:T(8,128)(2,1)S(1)}, u32[]{:S(2)}, u32[]{:S(2)}) %collective-permute-start.15) | collective-permute-done | bytes 131104 | tf_op jit(solution)/shard_map/ppermute | solution.py:294
  46.0 0.9 %grad_states.5 = (bf16[2,2,128,128]{3,2,1,0:T(8,128)(2,1)S(1)}, bf16[2,128,128]{2,1,0:T(8,128)(2,1)S(1)}) custom-call(s32[5]{0:T(128)S(1)} %stack.23.place_ref, bf16[1024,1024]{1,0:T(8,128)(2,1)S(1)} %copy-done, bf16[1024,1024]{1,0:T(8,128)(2,1)S(1)} %copy-done, bf16[256,256]{1,0:T(8,128)(2,1)S(1)} %collective-permute-done.14.refs_3_.g0.refs_7_, ...), custom_call_target="tpu_custom_call" | custom-call | flops 33554432 | bytes 524288 | tf_op jit(solution)/shard_map/grad_states/pallas_call | solution.py:148
  46.9 0.6 collective-permute-start.16
  47.5 0.0 collective-permute-done.7.refs_19_
  47.6 1.3 %collective-permute-start.8 = (bf16[4,128,128]{2,1,0:T(8,128)(2,1)S(1)}, bf16[4,128,128]{2,1,0:T(8,128)(2,1)S(1)}, u32[]{:S(2)}, u32[]{:S(2)}) collective-permute-start(bf16[4,128,128]{2,1,0:T(8,128)(2,1)S(1)} %add.76), channel_id=1, source_target_pairs={{16,0},{20,4},{24,8},{28,12},{17,1},{21,5},{25,9},{29,13},{18,2},{... | collective-permute-start | bytes 393224 | tf_op jit(solution)/shard_map/ppermute | solution.py:274
  48.9 0.0 collective-permute-done.11.refs_21_
  48.9 1.3 %collective-permute-start.12 = (bf16[2,128,128]{2,1,0:T(8,128)(2,1)S(1)}, bf16[2,128,128]{2,1,0:T(8,128)(2,1)S(1)}, u32[]{:S(2)}, u32[]{:S(2)}) collective-permute-start(bf16[2,128,128]{2,1,0:T(8,128)(2,1)S(1)} %add.81), channel_id=1, source_target_pairs={{8,0},{12,4},{16,8},{20,12},{24,16},{28,20},{9,1},{13,5},{17,9},{2... | collective-permute-start | bytes 196616 | tf_op jit(solution)/shard_map/ppermute | solution.py:274
  50.2 1.1 %collective-permute-done.16.refs_21_ = bf16[2,128,128]{2,1,0:T(8,128)(2,1)S(1)} collective-permute-done((bf16[2,128,128]{2,1,0:T(8,128)(2,1)S(1)}, bf16[2,128,128]{2,1,0:T(8,128)(2,1)S(1)}, u32[]{:S(2)}, u32[]{:S(2)}) %collective-permute-start.16) | collective-permute-done | bytes 65568 | tf_op jit(solution)/shard_map/ppermute | solution.py:268
  51.3 1.3 %collective-permute-start.17 = (bf16[2,128,128]{2,1,0:T(8,128)(2,1)S(1)}, bf16[2,128,128]{2,1,0:T(8,128)(2,1)S(1)}, u32[]{:S(2)}, u32[]{:S(2)}) collective-permute-start(bf16[2,128,128]{2,1,0:T(8,128)(2,1)S(1)} %add.87), channel_id=1, source_target_pairs={{8,0},{12,4},{16,8},{20,12},{24,16},{28,20},{9,1},{13,5},{17,9},{2... | collective-permute-start | bytes 196616 | tf_op jit(solution)/shard_map/ppermute | solution.py:274
  52.6 3.0 %intra.6 = (bf16[2,256,256]{2,1,0:T(8,128)(2,1)S(1)}, bf16[2,256,256]{2,1,0:T(8,128)(2,1)S(1)}, bf16[2,256,256]{2,1,0:T(8,128)(2,1)S(1)}) custom-call(s32[5]{0:T(128)S(1)} %stack.23.place_ref, bf16[1024,1024]{1,0:T(8,128)(2,1)S(1)} %copy-done, bf16[1024,1024]{1,0:T(8,128)(2,1)S(1)} %copy-done.2, bf16[1024,1024]{1,0:T(8,128)(2,1)} %refs_4_.11, ...), custom_call_target="tpu_custom_call" | custom-call | flops 335544320 | bytes 1835008 | tf_op jit(solution)/shard_map/intra/pallas_call | solution.py:112
  55.6 3.0 %intra.7 = (bf16[2,256,256]{2,1,0:T(8,128)(2,1)S(1)}, bf16[2,256,256]{2,1,0:T(8,128)(2,1)S(1)}, bf16[2,256,256]{2,1,0:T(8,128)(2,1)S(1)}) custom-call(s32[5]{0:T(128)S(1)} %stack.23.place_ref, bf16[1024,1024]{1,0:T(8,128)(2,1)S(1)} %copy-done, bf16[1024,1024]{1,0:T(8,128)(2,1)S(1)} %copy-done.2, bf16[1024,1024]{1,0:T(8,128)(2,1)} %refs_4_.11, ...), custom_call_target="tpu_custom_call" | custom-call | flops 335544320 | bytes 1835008 | tf_op jit(solution)/shard_map/intra/pallas_call | solution.py:112
  58.7 0.0 collective-permute-done.12.refs_22_
  58.7 1.3 %collective-permute-start.13 = (bf16[2,128,128]{2,1,0:T(8,128)(2,1)S(1)}, bf16[2,128,128]{2,1,0:T(8,128)(2,1)S(1)}, u32[]{:S(2)}, u32[]{:S(2)}) collective-permute-start(bf16[2,128,128]{2,1,0:T(8,128)(2,1)S(1)} %add.82), channel_id=1, source_target_pairs={{16,0},{20,4},{24,8},{28,12},{17,1},{21,5},{25,9},{29,13},{18,2},{... | collective-permute-start | bytes 196616 | tf_op jit(solution)/shard_map/ppermute | solution.py:274
  60.0 0.0 collective-permute-done.17.refs_22_
  60.0 1.5 %collective-permute-start.18 = (bf16[2,128,128]{2,1,0:T(8,128)(2,1)S(1)}, bf16[2,128,128]{2,1,0:T(8,128)(2,1)S(1)}, u32[]{:S(2)}, u32[]{:S(2)}) collective-permute-start(bf16[2,128,128]{2,1,0:T(8,128)(2,1)S(1)} %add.88), channel_id=1, source_target_pairs={{16,0},{20,4},{24,8},{28,12},{17,1},{21,5},{25,9},{29,13},{18,2},{... | collective-permute-start | bytes 196616 | tf_op jit(solution)/shard_map/ppermute | solution.py:274
  61.5 4.8 %intra.5 = (bf16[2,256,512]{2,1,0:T(8,128)(2,1)S(1)}, bf16[2,256,512]{2,1,0:T(8,128)(2,1)S(1)}, bf16[2,256,512]{2,1,0:T(8,128)(2,1)S(1)}) custom-call(s32[5]{0:T(128)S(1)} %stack.23.place_ref, bf16[1024,1024]{1,0:T(8,128)(2,1)S(1)} %copy-done, bf16[1024,1024]{1,0:T(8,128)(2,1)} %refs_3_.5, bf16[1024,1024]{1,0:T(8,128)(2,1)} %refs_4_.11, ...), custom_call_target="tpu_custom_call" | custom-call | flops 671088640 | bytes 3670016 | tf_op jit(solution)/shard_map/intra/pallas_call | solution.py:112
  66.3 0.0 collective-permute-done.5.refs_17_.refs_20_
  66.4 0.0 collective-permute-done.8.refs_20_
  66.4 5.6 %finish.3 = (bf16[1024,1024]{1,0:T(8,128)(2,1)}, bf16[1024,1024]{1,0:T(8,128)(2,1)}, bf16[1024,1024]{1,0:T(8,128)(2,1)}) custom-call(s32[5]{0:T(128)S(1)} %stack.23.place_ref, bf16[1024,1024]{1,0:T(8,128)(2,1)} %refs_3_.5, bf16[1024,1024]{1,0:T(8,128)(2,1)} %refs_4_.11, bf16[256,4096]{1,0:T(8,128)(2,1)} %refs_5_.11, ...), custom_call_target="tpu_custom_call" | custom-call | flops 402653184 | bytes 9437184 | tf_op jit(solution)/shard_map/finish/pallas_call | solution.py:249
  72.0 0.0 collective-permute-done.13.refs_23_
  72.0 3.5 %finish.4 = (bf16[1024,1024]{1,0:T(8,128)(2,1)}, bf16[1024,1024]{1,0:T(8,128)(2,1)}, bf16[1024,1024]{1,0:T(8,128)(2,1)}) custom-call(s32[5]{0:T(128)S(1)} %stack.23.place_ref, bf16[1024,1024]{1,0:T(8,128)(2,1)} %get-tuple-element.41.refs_0_, ...), custom_call_target="tpu_custom_call", output_to_operand_aliasing={{0}: (1, {}), {1}: (2, {}), {2}: (3, {})} | custom-call | flops 201326592 | bytes 4718592 | tf_op jit(solution)/shard_map/finish/pallas_call | solution.py:249
  75.5 0.0 collective-permute-done.18.refs_23_
  75.5 3.5 %finish.5 = (bf16[1024,1024]{1,0:T(8,128)(2,1)}, bf16[1024,1024]{1,0:T(8,128)(2,1)}, bf16[1024,1024]{1,0:T(8,128)(2,1)}) custom-call(s32[5]{0:T(128)S(1)} %stack.23.place_ref, bf16[1024,1024]{1,0:T(8,128)(2,1)} %get-tuple-element.49.refs_0_, ...), custom_call_target="tpu_custom_call", output_to_operand_aliasing={{0}: (1, {}), {1}: (2, {}), {2}: (3, {})} | custom-call | flops 201326592 | bytes 4718592 | tf_op jit(solution)/shard_map/finish/pallas_call | solution.py:249
  (13 shorter events, 0.2 us)
Async XLA Ops:
  1.7 19.4 %collective-permute-start = (bf16[256,1024]{1,0:T(8,128)(2,1)S(1)}, bf16[256,1024]{1,0:T(8,128)(2,1)S(1)}, u32[]{:S(2)}, u32[]{:S(2)}) collective-permute-start(bf16[256,1024]{1,0:T(8,128)(2,1)S(1)} %constant_dynamic-slice_fusion.6), channel_id=1, source_target_pairs={{0,1},{1,0},{2,3},{3,2},{4,5},{5,4},{6,7},{7,6},{8,9},{9,8},{10,11... | collective-permute-start | bytes 1572872 | tf_op jit(solution)/shard_map/ppermute | solution.py:294
  2.2 1.6 %copy-start.1 = (bf16[1024,1024]{1,0:T(8,128)(2,1)S(1)}, bf16[1024,1024]{1,0:T(8,128)(2,1)}, u32[]{:S(2)}) copy-start(bf16[1024,1024]{1,0:T(8,128)(2,1)} %refs_3_.5) | copy-start | bytes 6291460
  3.8 1.6 %copy-start.3 = (bf16[1024,1024]{1,0:T(8,128)(2,1)S(1)}, bf16[1024,1024]{1,0:T(8,128)(2,1)}, u32[]{:S(2)}) copy-start(bf16[1024,1024]{1,0:T(8,128)(2,1)} %refs_4_.11) | copy-start | bytes 6291460
  6.7 1.0 %copy-start.4 = (bf16[4,8,128,128]{3,2,1,0:T(8,128)(2,1)}, bf16[4,8,128,128]{3,2,1,0:T(8,128)(2,1)S(1)}, u32[]{:S(2)}) copy-start(bf16[4,8,128,128]{3,2,1,0:T(8,128)(2,1)S(1)} %get-tuple-element.38.refs_14_.refs_17_) | copy-start | bytes 3145732
  7.7 9.5 %collective-permute-start.3 = (bf16[8,128,128]{2,1,0:T(8,128)(2,1)S(1)}, bf16[8,128,128]{2,1,0:T(8,128)(2,1)S(1)}, u32[]{:S(2)}, u32[]{:S(2)}) collective-permute-start(bf16[8,128,128]{2,1,0:T(8,128)(2,1)S(1)} %get-tuple-element.39), channel_id=1, source_target_pairs={{0,4},{4,0},{8,12},{12,8},{16,20},{20,16},{24,28},{28,24},{1,5},{5... | collective-permute-start | bytes 786440 | tf_op jit(solution)/shard_map/ppermute | solution.py:268
  11.3 17.9 %collective-permute-start.1 = (bf16[256,512]{1,0:T(8,128)(2,1)S(1)}, bf16[256,512]{1,0:T(8,128)(2,1)S(1)}, u32[]{:S(2)}, u32[]{:S(2)}) collective-permute-start(bf16[256,512]{1,0:T(8,128)(2,1)S(1)} %get-tuple-element.62), channel_id=1, source_target_pairs={{0,2},{1,3},{2,0},{3,1},{4,6},{5,7},{6,4},{7,5},{8,10},{9,11},{10,... | collective-permute-start | bytes 786440 | tf_op jit(solution)/shard_map/ppermute | solution.py:294
  12.9 16.3 %collective-permute-start.2 = (bf16[256,512]{1,0:T(8,128)(2,1)S(1)}, bf16[256,512]{1,0:T(8,128)(2,1)S(1)}, u32[]{:S(2)}, u32[]{:S(2)}) collective-permute-start(bf16[256,512]{1,0:T(8,128)(2,1)S(1)} %get-tuple-element.61), channel_id=1, source_target_pairs={{0,3},{1,2},{2,1},{3,0},{4,7},{5,6},{6,5},{7,4},{8,11},{9,10},{10,... | collective-permute-start | bytes 786440 | tf_op jit(solution)/shard_map/ppermute | solution.py:294
  17.3 11.9 %copy-start = (bf16[1024,1024]{1,0:T(8,128)(2,1)S(1)}, bf16[1024,1024]{1,0:T(8,128)(2,1)}, u32[]{:S(2)}) copy-start(bf16[1024,1024]{1,0:T(8,128)(2,1)} %q1.5) | copy-start | bytes 6291460
  17.3 17.9 %collective-permute-start.4 = (bf16[8,128,128]{2,1,0:T(8,128)(2,1)S(1)}, bf16[8,128,128]{2,1,0:T(8,128)(2,1)S(1)}, u32[]{:S(2)}, u32[]{:S(2)}) collective-permute-start(bf16[8,128,128]{2,1,0:T(8,128)(2,1)S(1)} %add.73), channel_id=1, source_target_pairs={{0,8},{4,12},{8,16},{12,20},{16,24},{20,28},{1,9},{5,13},{9,17},{1... | collective-permute-start | bytes 786440 | tf_op jit(solution)/shard_map/ppermute | solution.py:274
  29.1 1.0 %copy-start.5 = (bf16[2,256,1024]{2,1,0:T(8,128)(2,1)}, bf16[2,256,1024]{2,1,0:T(8,128)(2,1)S(1)}, u32[]{:S(2)}) copy-start(bf16[2,256,1024]{2,1,0:T(8,128)(2,1)S(1)} %get-tuple-element.31.refs_7_.refs_10_) | copy-start | bytes 3145732
  29.1 1.3 %copy-start.7 = (bf16[2,256,1024]{2,1,0:T(8,128)(2,1)}, bf16[2,256,1024]{2,1,0:T(8,128)(2,1)S(1)}, u32[]{:S(2)}) copy-start(bf16[2,256,1024]{2,1,0:T(8,128)(2,1)S(1)} %get-tuple-element.32.refs_8_.refs_11_) | copy-start | bytes 3145732
  30.4 6.3 %collective-permute-start.6 = (bf16[4,128,128]{2,1,0:T(8,128)(2,1)S(1)}, bf16[4,128,128]{2,1,0:T(8,128)(2,1)S(1)}, u32[]{:S(2)}, u32[]{:S(2)}) collective-permute-start(bf16[4,128,128]{2,1,0:T(8,128)(2,1)S(1)} %get-tuple-element.40), channel_id=1, source_target_pairs={{0,4},{4,0},{8,12},{12,8},{16,20},{20,16},{24,28},{28,24},{1,5},{5... | collective-permute-start | bytes 393224 | tf_op jit(solution)/shard_map/ppermute | solution.py:268
  33.1 5.6 %collective-permute-start.9 = (bf16[256,256]{1,0:T(8,128)(2,1)S(1)}, bf16[256,256]{1,0:T(8,128)(2,1)S(1)}, u32[]{:S(2)}, u32[]{:S(2)}) collective-permute-start(bf16[256,256]{1,0:T(8,128)(2,1)S(1)} %get-tuple-element.60), channel_id=1, source_target_pairs={{0,2},{1,3},{2,0},{3,1},{4,6},{5,7},{6,4},{7,5},{8,10},{9,11},{10,... | collective-permute-start | bytes 393224 | tf_op jit(solution)/shard_map/ppermute | solution.py:294
  34.6 9.0 %collective-permute-start.10 = (bf16[256,256]{1,0:T(8,128)(2,1)S(1)}, bf16[256,256]{1,0:T(8,128)(2,1)S(1)}, u32[]{:S(2)}, u32[]{:S(2)}) collective-permute-start(bf16[256,256]{1,0:T(8,128)(2,1)S(1)} %get-tuple-element.59), channel_id=1, source_target_pairs={{0,3},{1,2},{2,1},{3,0},{4,7},{5,6},{6,5},{7,4},{8,11},{9,10},{10,... | collective-permute-start | bytes 393224 | tf_op jit(solution)/shard_map/ppermute | solution.py:294
  34.6 10.5 %collective-permute-start.14 = (bf16[256,256]{1,0:T(8,128)(2,1)S(1)}, bf16[256,256]{1,0:T(8,128)(2,1)S(1)}, u32[]{:S(2)}, u32[]{:S(2)}) collective-permute-start(bf16[256,256]{1,0:T(8,128)(2,1)S(1)} %get-tuple-element.58), channel_id=1, source_target_pairs={{0,2},{1,3},{2,0},{3,1},{4,6},{5,7},{6,4},{7,5},{8,10},{9,11},{10,... | collective-permute-start | bytes 393224 | tf_op jit(solution)/shard_map/ppermute | solution.py:294
  35.2 10.8 %collective-permute-start.15 = (bf16[256,256]{1,0:T(8,128)(2,1)S(1)}, bf16[256,256]{1,0:T(8,128)(2,1)S(1)}, u32[]{:S(2)}, u32[]{:S(2)}) collective-permute-start(bf16[256,256]{1,0:T(8,128)(2,1)S(1)} %get-tuple-element.57), channel_id=1, source_target_pairs={{0,3},{1,2},{2,1},{3,0},{4,7},{5,6},{6,5},{7,4},{8,11},{9,10},{10,... | collective-permute-start | bytes 393224 | tf_op jit(solution)/shard_map/ppermute | solution.py:294
  36.8 10.8 %collective-permute-start.7 = (bf16[4,128,128]{2,1,0:T(8,128)(2,1)S(1)}, bf16[4,128,128]{2,1,0:T(8,128)(2,1)S(1)}, u32[]{:S(2)}, u32[]{:S(2)}) collective-permute-start(bf16[4,128,128]{2,1,0:T(8,128)(2,1)S(1)} %add.75), channel_id=1, source_target_pairs={{8,0},{12,4},{16,8},{20,12},{24,16},{28,20},{9,1},{13,5},{17,9},{2... | collective-permute-start | bytes 393224 | tf_op jit(solution)/shard_map/ppermute | solution.py:274
  38.6 27.7 %collective-permute-start.5 = (bf16[8,128,128]{2,1,0:T(8,128)(2,1)S(1)}, bf16[8,128,128]{2,1,0:T(8,128)(2,1)S(1)}, u32[]{:S(2)}, u32[]{:S(2)}) collective-permute-start(bf16[8,128,128]{2,1,0:T(8,128)(2,1)S(1)} %add.74), channel_id=1, source_target_pairs={{0,16},{4,20},{8,24},{12,28},{1,17},{5,21},{9,25},{13,29},{2,18},{... | collective-permute-start | bytes 786440 | tf_op jit(solution)/shard_map/ppermute | solution.py:274
  44.5 8.1 %copy-start.2 = (bf16[1024,1024]{1,0:T(8,128)(2,1)S(1)}, bf16[1024,1024]{1,0:T(8,128)(2,1)}, u32[]{:S(2)}) copy-start(bf16[1024,1024]{1,0:T(8,128)(2,1)} %refs_3_.5) | copy-start | bytes 6291460
  44.5 4.4 %collective-permute-start.11 = (bf16[2,128,128]{2,1,0:T(8,128)(2,1)S(1)}, bf16[2,128,128]{2,1,0:T(8,128)(2,1)S(1)}, u32[]{:S(2)}, u32[]{:S(2)}) collective-permute-start(bf16[2,128,128]{2,1,0:T(8,128)(2,1)S(1)} %get-tuple-element.48), channel_id=1, source_target_pairs={{0,4},{4,0},{8,12},{12,8},{16,20},{20,16},{24,28},{28,24},{1,5},{5... | collective-permute-start | bytes 196616 | tf_op jit(solution)/shard_map/ppermute | solution.py:268
  46.9 4.4 %collective-permute-start.16 = (bf16[2,128,128]{2,1,0:T(8,128)(2,1)S(1)}, bf16[2,128,128]{2,1,0:T(8,128)(2,1)S(1)}, u32[]{:S(2)}, u32[]{:S(2)}) collective-permute-start(bf16[2,128,128]{2,1,0:T(8,128)(2,1)S(1)} %get-tuple-element.56), channel_id=1, source_target_pairs={{0,4},{4,0},{8,12},{12,8},{16,20},{20,16},{24,28},{28,24},{1,5},{5... | collective-permute-start | bytes 196616 | tf_op jit(solution)/shard_map/ppermute | solution.py:268
  47.6 18.8 %collective-permute-start.8 = (bf16[4,128,128]{2,1,0:T(8,128)(2,1)S(1)}, bf16[4,128,128]{2,1,0:T(8,128)(2,1)S(1)}, u32[]{:S(2)}, u32[]{:S(2)}) collective-permute-start(bf16[4,128,128]{2,1,0:T(8,128)(2,1)S(1)} %add.76), channel_id=1, source_target_pairs={{16,0},{20,4},{24,8},{28,12},{17,1},{21,5},{25,9},{29,13},{18,2},{... | collective-permute-start | bytes 393224 | tf_op jit(solution)/shard_map/ppermute | solution.py:274
  48.9 9.7 %collective-permute-start.12 = (bf16[2,128,128]{2,1,0:T(8,128)(2,1)S(1)}, bf16[2,128,128]{2,1,0:T(8,128)(2,1)S(1)}, u32[]{:S(2)}, u32[]{:S(2)}) collective-permute-start(bf16[2,128,128]{2,1,0:T(8,128)(2,1)S(1)} %add.81), channel_id=1, source_target_pairs={{8,0},{12,4},{16,8},{20,12},{24,16},{28,20},{9,1},{13,5},{17,9},{2... | collective-permute-start | bytes 196616 | tf_op jit(solution)/shard_map/ppermute | solution.py:274
  51.3 8.7 %collective-permute-start.17 = (bf16[2,128,128]{2,1,0:T(8,128)(2,1)S(1)}, bf16[2,128,128]{2,1,0:T(8,128)(2,1)S(1)}, u32[]{:S(2)}, u32[]{:S(2)}) collective-permute-start(bf16[2,128,128]{2,1,0:T(8,128)(2,1)S(1)} %add.87), channel_id=1, source_target_pairs={{8,0},{12,4},{16,8},{20,12},{24,16},{28,20},{9,1},{13,5},{17,9},{2... | collective-permute-start | bytes 196616 | tf_op jit(solution)/shard_map/ppermute | solution.py:274
  58.7 13.3 %collective-permute-start.13 = (bf16[2,128,128]{2,1,0:T(8,128)(2,1)S(1)}, bf16[2,128,128]{2,1,0:T(8,128)(2,1)S(1)}, u32[]{:S(2)}, u32[]{:S(2)}) collective-permute-start(bf16[2,128,128]{2,1,0:T(8,128)(2,1)S(1)} %add.82), channel_id=1, source_target_pairs={{16,0},{20,4},{24,8},{28,12},{17,1},{21,5},{25,9},{29,13},{18,2},{... | collective-permute-start | bytes 196616 | tf_op jit(solution)/shard_map/ppermute | solution.py:274
  60.0 15.5 %collective-permute-start.18 = (bf16[2,128,128]{2,1,0:T(8,128)(2,1)S(1)}, bf16[2,128,128]{2,1,0:T(8,128)(2,1)S(1)}, u32[]{:S(2)}, u32[]{:S(2)}) collective-permute-start(bf16[2,128,128]{2,1,0:T(8,128)(2,1)S(1)} %add.88), channel_id=1, source_target_pairs={{16,0},{20,4},{24,8},{28,12},{17,1},{21,5},{25,9},{29,13},{18,2},{... | collective-permute-start | bytes 196616 | tf_op jit(solution)/shard_map/ppermute | solution.py:274
  66.4 5.7 %copy-start.6 = (bf16[2,256,1024]{2,1,0:T(8,128)(2,1)S(1)}, bf16[2,256,1024]{2,1,0:T(8,128)(2,1)}, u32[]{:S(2)}) copy-start(bf16[2,256,1024]{2,1,0:T(8,128)(2,1)} %copy-done.5) | copy-start | bytes 3145732

commit v2 on v0

v2 whole, which is shorter than its diff:
```python
import functools
import math

import jax
import jax.numpy as jnp
from jax import lax
from jax.experimental import pallas as pl
from jax.experimental.pallas import tpu as pltpu
from jax.sharding import PartitionSpec as P

HEAD_DIM = 128
SPLITS = (4, 4)
COST = (10**10, 10**8)
F32 = jnp.float32
BF16 = jnp.bfloat16
NN = (((1,), (0,)), ((), ()))
NT = (((1,), (1,)), ((), ()))
TN = (((0,), (0,)), ((), ()))
VMEM = pl.BlockSpec(memory_space=pltpu.VMEM)
ANY = pl.BlockSpec(memory_space=pl.ANY)


def dot(a, b, dims):
    return lax.dot_general(a, b, dims, preferred_element_type=F32)


def head_cols(h):
    return slice(h * HEAD_DIM, (h + 1) * HEAD_DIM)


def rows_of(place_ref, piece, chunk):
    return pl.ds(pl.multiple_of(place_ref[piece] * chunk, chunk), chunk)


def place_as(array, spec):
    return pltpu.with_memory_space_constraint(array, pltpu.VMEM if spec is VMEM else pltpu.HBM)


class Chain:
    def __init__(self, place):
        self.place = place
        self.token = jnp.zeros((8, 128), F32) + place[0].astype(F32)
        self.waits = []
        self.jobs = []

    def add(self, *sums):
        self.jobs += [one for one in sums if one.more()]

    def wait(self, *arrays):
        self.waits += arrays

    def __call__(self, name, kernel, operands, in_specs, out_shape, out_specs, grid=(), scratch=(), alias=None, cost=COST):
        extra = [self.token, *self.waits]
        jobs, self.waits, self.jobs = self.jobs, [], []
        skip, count = len(extra), len(operands)
        pairs = [array for sums in jobs for array in (sums.window, sums.parts[-1])]
        operands, in_specs = [*operands, *pairs], [*in_specs, *[VMEM] * len(pairs)]
        out_shape = [*[bf16(*sums.window.shape) for sums in jobs], *out_shape]
        out_specs = [*[VMEM] * len(jobs), *out_specs]

        def run(place_ref, *refs):
            ins = refs[skip : skip + count]
            pair_refs = refs[skip + count : skip + len(operands)]
            outs = refs[skip + len(operands) + 1 :]
            for n in range(len(jobs)):
                outs[n][...] = pair_refs[2 * n][...] + pair_refs[2 * n + 1][...]
            kernel(place_ref, *ins, *outs[len(jobs) :])

        aliases = {1: 0}
        for source, target in (alias or {}).items():
            aliases[1 + skip + source] = 1 + len(jobs) + target
        self.token, *outs = pl.pallas_call(
            run,
            grid_spec=pltpu.PrefetchScalarGridSpec(
                num_scalar_prefetch=1,
                grid=grid,
                in_specs=[ANY] * skip + list(in_specs),
                out_specs=[ANY] + list(out_specs),
                scratch_shapes=list(scratch),
            ),
            out_shape=[jax.ShapeDtypeStruct((8, 128), F32)] + list(out_shape),
            input_output_aliases=aliases,
            compiler_params=pltpu.CompilerParams(vmem_limit_bytes=8 * 1024 * 1024),
            cost_estimate=pl.CostEstimate(flops=cost[0], bytes_accessed=cost[1], transcendentals=0),
            name=name,
        )(self.place, *extra, *[place_as(x, s) for x, s in zip(operands, in_specs)])
        for sums, window in zip(jobs, outs):
            sums.window = window
            sums.go()
        return outs[len(jobs) :]


def bf16(*shape):
    return pltpu.VMEM(shape, BF16)


def cut(chain, out_grads, parts):
    chunk = out_grads.shape[0]

    def kernel(place_ref, g_ref, *refs):
        outs, sems = refs[:-1], refs[-1]
        copies = []
        for n, (mask, head0, heads) in enumerate(parts):
            start = place_ref[mask] * place_ref[4] + head0 * HEAD_DIM
            cols = pl.ds(pl.multiple_of(start, HEAD_DIM), heads * HEAD_DIM)
            copies.append(pltpu.make_async_copy(g_ref.at[:, cols], outs[n], sems.at[n]))
        for copy in copies:
            copy.start()
        for copy in copies:
            copy.wait()

    return chain(
        "cut", kernel, [out_grads], [ANY],
        [bf16(chunk, heads * HEAD_DIM) for _, _, heads in parts], [VMEM] * len(parts),
        scratch=[pltpu.SemaphoreType.DMA((len(parts),))],
    )


def kv_states(chain, key_rows, value_rows, chunk):
    rows, width = key_rows.shape
    heads, chunks = width // HEAD_DIM, rows // chunk

    def kernel(place_ref, k_ref, v_ref, local_ref, total_ref):
        for h in range(heads):
            run = jnp.zeros((HEAD_DIM, HEAD_DIM), F32)
            for c in range(chunks):
                at = slice(c * chunk, (c + 1) * chunk)
                local_ref[c, h] = run.astype(BF16)
                run = run + dot(v_ref[at, head_cols(h)], k_ref[at, head_cols(h)], TN)
            total_ref[h] = run.astype(BF16)

    return chain(
        "kv_states", kernel, [key_rows, value_rows], [VMEM] * 2,
        [bf16(chunks, heads, HEAD_DIM, HEAD_DIM), bf16(heads, HEAD_DIM, HEAD_DIM)], [VMEM] * 2,
    )


def intra(chain, pieces, arrays, grads, head0, heads, chunk):
    count = len(pieces)

    def kernel(place_ref, q_ref, k_ref, v_ref, *refs):
        g_refs, outs = refs[:count], refs[count:]
        row = lax.broadcasted_iota(jnp.int32, (chunk, chunk), 0)
        col = lax.broadcasted_iota(jnp.int32, (chunk, chunk), 1)
        upper, lower = row <= col, row >= col
        for n, piece in enumerate(pieces):
            rows = rows_of(place_ref, piece, chunk)
            for h in range(heads):
                cols, own = head_cols(head0 + h), head_cols(h)
                q, k, v, g = q_ref[rows, cols], k_ref[rows, cols], v_ref[rows, cols], g_refs[n][:, own]
                fwd = jnp.where(upper, dot(k, q, NT), 0.0).astype(BF16)
                back = jnp.where(upper, dot(v, g, NT), 0.0).astype(BF16)
                turned = jnp.where(lower, dot(g, v, NT), 0.0).astype(BF16)
                outs[0][n, :, own] = dot(turned, k, NN).astype(BF16)
                outs[1][n, :, own] = dot(back, q, NN).astype(BF16)
                outs[2][n, :, own] = dot(fwd, g, NN).astype(BF16)

    shapes = [bf16(count, chunk, heads * HEAD_DIM)] * 3
    return chain(
        "intra", kernel, [*arrays, *grads], [VMEM] * (3 + count), shapes, [VMEM] * len(shapes)
    )


def near_states(chain, query_rows, grads, chunk):
    heads = query_rows.shape[1] // HEAD_DIM

    def kernel(place_ref, q_ref, g0, g1, state_ref):
        for h in range(heads):
            cols = head_cols(h)
            for n, g_ref in enumerate((g0, g1)):
                q = q_ref[rows_of(place_ref, n, chunk), cols]
                state_ref[n, h] = dot(q, g_ref[:, cols], TN).astype(BF16)

    return chain(
        "near_states", kernel, [query_rows, *grads], [VMEM] * 3,
        [bf16(2, heads, HEAD_DIM, HEAD_DIM)], [VMEM],
    )[0]


def far_states(chain, query_rows, grads, near, head0, heads, chunk):
    def kernel(place_ref, q_ref, g0, g1, near_ref, state_ref, total_ref):
        for h in range(heads):
            cols, own = head_cols(head0 + h), head_cols(h)
            a = dot(q_ref[rows_of(place_ref, 2, chunk), cols], g0[:, own], TN)
            b = dot(q_ref[rows_of(place_ref, 3, chunk), cols], g1[:, own], TN)
            state_ref[0, h] = a.astype(BF16)
            state_ref[1, h] = b.astype(BF16)
            total = a + b + near_ref[0, head0 + h].astype(F32) + near_ref[1, head0 + h].astype(F32)
            total_ref[h] = total.astype(BF16)

    return chain(
        "far_states", kernel, [query_rows, *grads, near], [VMEM] * 4,
        [bf16(2, heads, HEAD_DIM, HEAD_DIM), bf16(heads, HEAD_DIM, HEAD_DIM)], [VMEM] * 2,
    )


def finish(chain, key_rows, value_rows, grads, parts, states, local, kv_in, grad_in, last, head0, heads, chunk, factor, outs):
    rows, feat = key_rows.shape
    rounds = len(kv_in)

    def kernel(place_ref, *refs):
        refs = list(refs)
        if outs is not None:
            refs = refs[3:]

        def take(n):
            got = refs[:n]
            del refs[:n]
            return got

        k_ref, v_ref = take(2)
        g_refs = take(4)
        part_refs = [take(3), take(3), take(3)]
        state_refs = take(2)
        (local_ref,) = take(1)
        kv_refs, grad_refs = take(rounds), take(rounds)
        (last_ref,) = take(1)
        dq_ref, dk_ref, dv_ref = refs
        h = pl.program_id(0)
        bit = place_ref[5 + rounds].astype(F32)
        got = last_ref[h].astype(F32)
        prefix, suffix = got * bit, got * (1.0 - bit)
        for r in range(rounds):
            bit = place_ref[5 + r].astype(F32)
            prefix = prefix + kv_refs[r][head0 + h].astype(F32) * bit
            suffix = suffix + grad_refs[r][h].astype(F32) * (1.0 - bit)
        wide = pl.ds(pl.multiple_of((head0 + h) * HEAD_DIM, HEAD_DIM), HEAD_DIM)
        narrow = pl.ds(pl.multiple_of(h * HEAD_DIM, HEAD_DIM), HEAD_DIM)
        state = [
            state_refs[0][0, head0 + h], state_refs[0][1, head0 + h],
            state_refs[1][0, h], state_refs[1][1, h],
        ]
        state = [s.astype(F32) for s in state]
        for piece in range(4):
            place = place_ref[piece]
            at = rows_of(place_ref, piece, chunk)
            part, slot = part_refs[min(piece, 2)], max(piece - 2, 0)
            cols = wide if piece < 2 else narrow
            before_low = (prefix + local_ref[place, head0 + h].astype(F32)).astype(BF16)
            after = suffix
            for other in range(4):
                if other != piece:
                    later = (place_ref[other] > place).astype(F32)
                    after = after + later * state[other]
            after_low = after.astype(BF16)
            out = part[0][slot, :, cols].astype(F32) + dot(g_refs[piece][:, cols], before_low, NN)
            dq_ref[at, :] = (factor * out).astype(BF16)
            out = part[1][slot, :, cols].astype(F32) + dot(v_ref[at, wide], after_low, NT)
            dk_ref[at, :] = (factor * out).astype(BF16)
            out = part[2][slot, :, cols].astype(F32) + dot(k_ref[at, wide], after_low, NN)
            dv_ref[at, :] = (factor * out).astype(BF16)

    operands = [key_rows, value_rows, *grads]
    for p in parts:
        operands += p
    operands += [*states, local, *kv_in, *grad_in, last]
    in_specs = [VMEM] * len(operands)
    alias = {}
    if outs is not None:
        operands = [*outs, *operands]
        in_specs = [ANY] * 3 + in_specs
        alias = {0: 0, 1: 1, 2: 2}
    return chain(
        "finish", kernel, operands, in_specs, [pltpu.HBM((rows, feat), BF16)] * 3,
        [pl.BlockSpec((rows, HEAD_DIM), lambda i, place: (0, i + head0))] * 3,
        grid=(heads,), alias=alias,
    )


class SeqSums:
    def __init__(self, total, axis, size):
        self.window, self.axis, self.size = total, axis, size
        self.step, self.parts = 1, []

    def swap(self, block):
        got = lax.ppermute(block, self.axis, [(i, i ^ self.step) for i in range(self.size)])
        self.step *= 2
        return got

    def more(self):
        return 2 * self.step < self.size

    def go(self):
        self.parts.append(self.swap(self.window))


def add_only(chain):
    if chain.jobs:
        chain("add", lambda place_ref: None, [], [], [], [])


def last_round(chain, prefix_sums, suffix_sums, head0, heads):
    rounds = len(suffix_sums.parts)

    def kernel(place_ref, kv_a, kv_b, grad_a, grad_b, out_ref):
        upper = place_ref[5 + rounds] == 1

        @pl.when(upper)
        def _():
            out_ref[...] = grad_a[...] + grad_b[...]

        @pl.when(jnp.logical_not(upper))
        def _():
            at = slice(head0, head0 + heads)
            out_ref[...] = kv_a[at] + kv_b[at]

    operands = [prefix_sums.window, prefix_sums.parts[-1], suffix_sums.window, suffix_sums.parts[-1]]
    block = chain("last_round", kernel, operands, [VMEM] * 4, [bf16(heads, HEAD_DIM, HEAD_DIM)], [VMEM])[0]
    return suffix_sums.swap(block)


def body(seq_size, head_size, query_rows, key_rows, value_rows, out_grads):
    rows, feat = query_rows.shape
    chunk = rows // head_size
    head_count = feat // HEAD_DIM
    factor = 1.0 / math.sqrt(HEAD_DIM * rows * seq_size)
    rank = lax.axis_index("head")
    seq = lax.axis_index("seq")
    bits = [(seq >> r) & 1 for r in range(seq_size.bit_length() - 1)]
    place = jnp.stack([rank, rank ^ 1, rank ^ 2, rank ^ 3, jnp.full_like(rank, feat), *bits])
    chain = Chain(place.astype(jnp.int32))
    arrays = (query_rows, key_rows, value_rows)
    firsts = [sum(SPLITS[:s]) for s in range(len(SPLITS))]

    def send(block, mask):
        return lax.ppermute(block, "head", [(i, i ^ mask) for i in range(head_size)])

    f, n = firsts[0], SPLITS[0]
    near_block, *blocks = cut(chain, out_grads, [(1, 0, head_count), (2, f, n), (3, f, n)])
    near_grad = send(near_block, 1)
    crossing = [[send(blocks[0], 2), send(blocks[1], 3)]]
    local, kv_total = kv_states(chain, key_rows, value_rows, chunk)
    kv_sums = SeqSums(kv_total, "seq", seq_size)
    kv_sums.go()
    chain.wait(near_grad)
    f, n = firsts[1], SPLITS[1]
    own_grad, *blocks = cut(chain, out_grads, [(0, 0, head_count), (2, f, n), (3, f, n)])
    crossing.append([send(blocks[0], 2), send(blocks[1], 3)])
    own_part = intra(chain, [0], arrays, [own_grad], 0, head_count, chunk)
    near_state = near_states(chain, query_rows, (own_grad, near_grad), chunk)
    near_part = intra(chain, [1], arrays, [near_grad], 0, head_count, chunk)

    far_state, far_part, sums, lasts = [], [], [], []

    def states(s):
        f, n = firsts[s], SPLITS[s]
        far, total = far_states(chain, query_rows, crossing[s], near_state, f, n, chunk)
        far_state.append(far)
        sums.append(SeqSums(total, "seq", seq_size))
        sums[s].go()

    def settle(one):
        while one.more():
            chain.add(one)
            add_only(chain)

    def inside(s):
        far_part.append(intra(chain, [2, 3], arrays, crossing[s], firsts[s], SPLITS[s], chunk))

    def last(s):
        settle(sums[s])
        lasts.append(last_round(chain, kv_sums, sums[s], firsts[s], SPLITS[s]))

    chain.add(kv_sums)
    states(0)
    inside(0)
    chain.add(sums[0])
    add_only(chain)
    states(1)
    inside(1)
    settle(kv_sums)
    last(0)
    chain.add(sums[1])
    add_only(chain)
    last(1)
    outs = None
    for s, (f, n) in enumerate(zip(firsts, SPLITS)):
        outs = finish(
            chain, key_rows, value_rows, (own_grad, near_grad, *crossing[s]),
            (own_part, near_part, far_part[s]), (near_state, far_state[s]),
            local, kv_sums.parts, sums[s].parts, lasts[s], f, n, chunk, factor, outs,
        )
    return tuple(outs)


def solution(mesh):
    return jax.shard_map(
        functools.partial(body, mesh.shape["seq"], mesh.shape["head"]),
        mesh=mesh,
        in_specs=(P("seq", "head"), P("seq", "head"), P("seq", "head"), P(("seq", "head"), None)),
        out_specs=(P("seq", "head"), P("seq", "head"), P("seq", "head")),
        check_vma=False,
    )
```

time: 209 us -> 56.2 us (0.27)
  waiting for transfers between devices: 112 us -> 7.78 us
  matrix products: 49.7 us -> 0 us
  Pallas kernels: 0 us -> 29.5 us
  local copies, waits for them, and re-layouts: 28 us -> 0.1 us
  between operations: 14.2 us -> 0.79 us
  starting transfers between devices: 4.74 us -> 17.9 us
    all_gather x2 -> x0, waiting for transfers between devices: 89.3 us -> none  [the longest x1 60.8 us: body(): lax.all_gather(grad_state, 'seq', axis=0, tiled=True)]
    dot_general x11 -> x0, matrix products: 49.7 us -> none  [the longest x1 10.1 us: body(): jnp.einsum('chts,cthj->cshj', fwd_scores, grads, preferred_element_type=j...]
    pallas_call x0 -> x16, Pallas kernels: none -> 29.5 us  [__call__(): pl.pallas_call(run, grid_spec=pltpu.PrefetchScalarGridSpec(num_scalar_pre...]
    all_to_all x1 -> x0, waiting for transfers between devices: 22.6 us -> none  [body(): lax.all_to_all(out_grads, 'head', split_axis=1, concat_axis=0, tiled=True)]
    ppermute x0 -> x13, starting transfers between devices: none -> 17.9 us  [the longest x8 13.1 us: swap(): lax.ppermute(block, self.axis, [(i, i ^ self.step) for i in range(self.si...]
    unnamed x19 -> x6, local copies, waits for them, and re-layouts: 13.7 us -> 0.01 us
    convert_element_type x5 -> x0, local copies, waits for them, and re-layouts: 11.2 us -> none  [the longest x2 6.43 us: body(): value_grad.reshape(row_count, feat_width).astype(jnp.bfloat16)]
    ppermute x0 -> x13, waiting for transfers between devices: none -> 7.78 us  [the longest x8 7.77 us: swap(): lax.ppermute(block, self.axis, [(i, i ^ self.step) for i in range(self.si...]
  transfers between devices with their start and end apart: 3 -> 13, of which waited for: 3 -> 5; matrix products, arithmetic and copies ran while one was open for 15% -> 0% of each run, Pallas kernels for 0% -> 41%
where the time goes in v2:
time: 56.2 us; the launch traced here: 56.1 us
  Pallas kernels  29.5 us (52%)
  starting transfers between devices  17.9 us (32%)
  waiting for transfers between devices  7.78 us (14%)
  between operations  0.79 us (1%)
    pallas_call x16, Pallas kernels, __call__(): pl.pallas_call(run, grid_spec=pltpu.PrefetchScalarGridSpec(num_scalar_pre...  29.5 us
    ppermute x8, starting transfers between devices, swap(): lax.ppermute(block, self.axis, [(i, i ^ self.step) for i in range(self.si...  13.1 us
    ppermute x8, waiting for transfers between devices, swap(): lax.ppermute(block, self.axis, [(i, i ^ self.step) for i in range(self.si...  7.77 us
    ppermute x5, starting transfers between devices, send(): lax.ppermute(block, 'head', [(i, i ^ mask) for i in range(head_size)])  4.81 us
  transfers between devices with their start and end apart: 13, of which 5 were waited for; matrix products, arithmetic and copies ran while one was open for 0% of the time, Pallas kernels for 41%

profile of v2, /device:TPU:0, one launch (start us, length us, event | category | flops | bytes accessed | tf_op | source)
XLA Modules:
  0.0 56.1 jit_solution(5742993644525947742)
XLA Ops:
  0.6 0.1 stack.31.place_ref
  0.7 0.0 copy-start.1
  0.7 0.0 copy-start.2
  0.7 2.0 %cut.2 = (f32[8,128]{1,0:T(8,128)S(1)}, bf16[256,1024]{1,0:T(8,128)(2,1)S(1)}, bf16[256,512]{1,0:T(8,128)(2,1)S(1)}, bf16[256,512]{1,0:T(8,128)(2,1)S(1)}) custom-call(s32[8]{0:T(128)S(1)} %stack.31.place_ref, f32[8,128]{1,0:T(8,128)S(1)} %add.5.refs_0_, bf16[256,4096]{1,0:T(8,128)(2,1)} %refs_2_.8), custom_call_target="tpu_custom_call", output_to_operand_aliasing={{0}: (1, {})} | custom-call | flops 10000000000 | bytes 100000000 | tf_op jit(solution)/shard_map/cut/pallas_call | solution.py:72
  2.8 3.0 %collective-permute-start.1 = (bf16[256,512]{1,0:T(8,128)(2,1)S(1)}, bf16[256,512]{1,0:T(8,128)(2,1)S(1)}, u32[]{:S(2)}, u32[]{:S(2)}) collective-permute-start(bf16[256,512]{1,0:T(8,128)(2,1)S(1)} %get-tuple-element.62), channel_id=1, source_target_pairs={{0,2},{1,3},{2,0},{3,1},{4,6},{5,7},{6,4},{7,5},{8,10},{9,11},{10,... | collective-permute-start | bytes 786440 | tf_op jit(solution)/shard_map/ppermute | solution.py:326
  5.8 0.0 collective-permute-start.2
  5.8 0.2 collective-permute-start
  6.0 0.0 copy-done.1
  6.0 0.0 copy-done.2
  6.0 1.6 %kv_states.1 = (f32[8,128]{1,0:T(8,128)S(1)}, bf16[4,8,128,128]{3,2,1,0:T(8,128)(2,1)S(1)}, bf16[8,128,128]{2,1,0:T(8,128)(2,1)S(1)}) custom-call(s32[8]{0:T(128)S(1)} %stack.31.place_ref, f32[8,128]{1,0:T(8,128)S(1)} %get-tuple-element.54.refs_0_, bf16[1024,1024]{1,0:T(8,128)(2,1)S(1)} %copy-done.1, ...), custom_call_target="tpu_custom_call", output_to_operand_aliasing={{0}: (1, {})} | custom-call | flops 10000000000 | bytes 100000000 | tf_op jit(solution)/shard_map/kv_states/pallas_call | solution.py:72
  7.6 2.0 %collective-permute-start.3 = (bf16[8,128,128]{2,1,0:T(8,128)(2,1)S(1)}, bf16[8,128,128]{2,1,0:T(8,128)(2,1)S(1)}, u32[]{:S(2)}, u32[]{:S(2)}) collective-permute-start(bf16[8,128,128]{2,1,0:T(8,128)(2,1)S(1)} %get-tuple-element.65.refs_5_), channel_id=1, source_target_pairs={{0,4},{4,0},{8,12},{12,8},{16,20},{20,16},{24,28},{28,24},{1,5},{5... | collective-permute-start | bytes 786440 | tf_op jit(solution)/shard_map/ppermute | solution.py:276
  9.6 0.0 collective-permute-done.refs_1_.refs_3_.refs_4_.refs_7_
  9.6 0.0 copy-start
  9.6 1.8 %cut.3 = (f32[8,128]{1,0:T(8,128)S(1)}, bf16[256,1024]{1,0:T(8,128)(2,1)S(1)}, bf16[256,512]{1,0:T(8,128)(2,1)S(1)}, bf16[256,512]{1,0:T(8,128)(2,1)S(1)}) custom-call(s32[8]{0:T(128)S(1)} %stack.31.place_ref, f32[8,128]{1,0:T(8,128)S(1)} %get-tuple-element.55.refs_0_, ...), custom_call_target="tpu_custom_call", output_to_operand_aliasing={{0}: (1, {})} | custom-call | flops 10000000000 | bytes 100000000 | tf_op jit(solution)/shard_map/cut/pallas_call | solution.py:72
  11.5 1.6 %collective-permute-start.5 = (bf16[256,512]{1,0:T(8,128)(2,1)S(1)}, bf16[256,512]{1,0:T(8,128)(2,1)S(1)}, u32[]{:S(2)}, u32[]{:S(2)}) collective-permute-start(bf16[256,512]{1,0:T(8,128)(2,1)S(1)} %get-tuple-element.70), channel_id=1, source_target_pairs={{0,2},{1,3},{2,0},{3,1},{4,6},{5,7},{6,4},{7,5},{8,10},{9,11},{10,... | collective-permute-start | bytes 786440 | tf_op jit(solution)/shard_map/ppermute | solution.py:326
  13.1 0.0 collective-permute-start.6
  13.1 0.0 copy-done
  13.1 2.8 %intra.4 = (f32[8,128]{1,0:T(8,128)S(1)}, bf16[1,256,1024]{2,1,0:T(8,128)(2,1)S(1)}, bf16[1,256,1024]{2,1,0:T(8,128)(2,1)S(1)}, bf16[1,256,1024]{2,1,0:T(8,128)(2,1)S(1)}) custom-call(s32[8]{0:T(128)S(1)} %stack.31.place_ref, f32[8,128]{1,0:T(8,128)S(1)} %get-tuple-element.57.refs_0_, ...), custom_call_target="tpu_custom_call", output_to_operand_aliasing={{0}: (1, {})} | custom-call | flops 10000000000 | bytes 100000000 | tf_op jit(solution)/shard_map/intra/pallas_call | solution.py:72
  15.9 1.1 %near_states.1 = (f32[8,128]{1,0:T(8,128)S(1)}, bf16[2,8,128,128]{3,2,1,0:T(8,128)(2,1)S(1)}) custom-call(s32[8]{0:T(128)S(1)} %stack.31.place_ref, f32[8,128]{1,0:T(8,128)S(1)} %get-tuple-element.59.refs_0_, bf16[1024,1024]{1,0:T(8,128)(2,1)S(1)} %copy-done, ...), custom_call_target="tpu_custom_call", output_to_operand_aliasing={{0}: (1, {})} | custom-call | flops 10000000000 | bytes 100000000 | tf_op jit(solution)/shard_map/near_states/pallas_call | solution.py:72
  16.9 2.8 %intra.5 = (f32[8,128]{1,0:T(8,128)S(1)}, bf16[1,256,1024]{2,1,0:T(8,128)(2,1)S(1)}, bf16[1,256,1024]{2,1,0:T(8,128)(2,1)S(1)}, bf16[1,256,1024]{2,1,0:T(8,128)(2,1)S(1)}) custom-call(s32[8]{0:T(128)S(1)} %stack.31.place_ref, f32[8,128]{1,0:T(8,128)S(1)} %get-tuple-element.60.refs_0_, ...), custom_call_target="tpu_custom_call", output_to_operand_aliasing={{0}: (1, {})} | custom-call | flops 10000000000 | bytes 100000000 | tf_op jit(solution)/shard_map/intra/pallas_call | solution.py:72
  19.8 0.0 collective-permute-done.1.refs_2_.refs_4_.refs_5_
  19.8 0.0 collective-permute-done.2.refs_3_.refs_5_.refs_6_
  19.8 0.0 collective-permute-done.3.refs_6_.refs_19_.refs_22_
  19.8 1.0 %far_states.2 = (f32[8,128]{1,0:T(8,128)S(1)}, bf16[8,128,128]{2,1,0:T(8,128)(2,1)S(1)}, bf16[2,4,128,128]{3,2,1,0:T(8,128)(2,1)S(1)}, bf16[4,128,128]{2,1,0:T(8,128)(2,1)S(1)}) custom-call(s32[8]{0:T(128)S(1)} %stack.31.place_ref, f32[8,128]{1,0:T(8,128)S(1)} %get-tuple-element.61.refs_0_, ...), custom_call_target="tpu_custom_call", output_to_operand_aliasing={{0}: (1, {})} | custom-call | flops 10000000000 | bytes 100000000 | tf_op jit(solution)/shard_map/far_states/pallas_call | solution.py:72
  20.8 0.6 %collective-permute-start.4 = (bf16[4,128,128]{2,1,0:T(8,128)(2,1)S(1)}, bf16[4,128,128]{2,1,0:T(8,128)(2,1)S(1)}, u32[]{:S(2)}, u32[]{:S(2)}) collective-permute-start(bf16[4,128,128]{2,1,0:T(8,128)(2,1)S(1)} %get-tuple-element.68.refs_1_), channel_id=1, source_target_pairs={{0,4},{4,0},{8,12},{12,8},{16,20},{20,16},{24,28},{28,24},{1,5},{5... | collective-permute-start | bytes 393224 | tf_op jit(solution)/shard_map/ppermute | solution.py:276
  21.4 1.6 %collective-permute-start.7 = (bf16[8,128,128]{2,1,0:T(8,128)(2,1)S(1)}, bf16[8,128,128]{2,1,0:T(8,128)(2,1)S(1)}, u32[]{:S(2)}, u32[]{:S(2)}) collective-permute-start(bf16[8,128,128]{2,1,0:T(8,128)(2,1)S(1)} %get-tuple-element.74.refs_1_), channel_id=1, source_target_pairs={{0,8},{4,12},{8,0},{12,4},{16,24},{20,28},{24,16},{28,20},{1,9},{5... | collective-permute-start | bytes 786440 | tf_op jit(solution)/shard_map/ppermute | solution.py:276
  23.0 2.8 %intra.6 = (f32[8,128]{1,0:T(8,128)S(1)}, bf16[2,256,512]{2,1,0:T(8,128)(2,1)S(1)}, bf16[2,256,512]{2,1,0:T(8,128)(2,1)S(1)}, bf16[2,256,512]{2,1,0:T(8,128)(2,1)S(1)}) custom-call(s32[8]{0:T(128)S(1)} %stack.31.place_ref, f32[8,128]{1,0:T(8,128)S(1)} %get-tuple-element.66.refs_0_, bf16[1024,1024]{1,0:T(8,128)(2,1)S(1)} %copy-done, ...), custom_call_target="tpu_custom_call", output_to_operand_aliasing={{0}: (1, {})} | custom-call | flops 10000000000 | bytes 100000000 | tf_op jit(solution)/shard_map/intra/pallas_call | solution.py:72
  25.7 1.1 %collective-permute-done.4.refs_2_.refs_21_ = bf16[4,128,128]{2,1,0:T(8,128)(2,1)S(1)} collective-permute-done((bf16[4,128,128]{2,1,0:T(8,128)(2,1)S(1)}, bf16[4,128,128]{2,1,0:T(8,128)(2,1)S(1)}, u32[]{:S(2)}, u32[]{:S(2)}) %collective-permute-start.4) | collective-permute-done | bytes 131104 | tf_op jit(solution)/shard_map/ppermute | solution.py:276
  26.9 0.6 %add.6 = (f32[8,128]{1,0:T(8,128)S(1)}, bf16[4,128,128]{2,1,0:T(8,128)(2,1)S(1)}) custom-call(s32[8]{0:T(128)S(1)} %stack.31.place_ref, f32[8,128]{1,0:T(8,128)S(1)} %get-tuple-element.67.refs_0_, bf16[4,128,128]{2,1,0:T(8,128)(2,1)S(1)} %get-tuple-element.68.refs_1_, ...), custom_call_target="tpu_custom_call", output_to_operand_aliasing={{0}: (1, {})} | custom-call | flops 10000000000 | bytes 100000000 | tf_op jit(solution)/shard_map/add/pallas_call | solution.py:72
  27.4 1.6 %collective-permute-start.8 = (bf16[4,128,128]{2,1,0:T(8,128)(2,1)S(1)}, bf16[4,128,128]{2,1,0:T(8,128)(2,1)S(1)}, u32[]{:S(2)}, u32[]{:S(2)}) collective-permute-start(bf16[4,128,128]{2,1,0:T(8,128)(2,1)S(1)} %get-tuple-element.75.refs_3_), channel_id=1, source_target_pairs={{0,8},{4,12},{8,0},{12,4},{16,24},{20,28},{24,16},{28,20},{1,9},{5... | collective-permute-start | bytes 393224 | tf_op jit(solution)/shard_map/ppermute | solution.py:276
  29.1 0.0 collective-permute-done.5.refs_2_.refs_4_.refs_8_
  29.1 0.0 collective-permute-done.6.refs_3_.refs_5_.refs_9_
  29.1 0.9 %far_states.3 = (f32[8,128]{1,0:T(8,128)S(1)}, bf16[2,4,128,128]{3,2,1,0:T(8,128)(2,1)S(1)}, bf16[4,128,128]{2,1,0:T(8,128)(2,1)S(1)}) custom-call(s32[8]{0:T(128)S(1)} %stack.31.place_ref, f32[8,128]{1,0:T(8,128)S(1)} %get-tuple-element.69.refs_0_, bf16[1024,1024]{1,0:T(8,128)(2,1)S(1)} %copy-done, ...), custom_call_target="tpu_custom_call", output_to_operand_aliasing={{0}: (1, {})} | custom-call | flops 10000000000 | bytes 100000000 | tf_op jit(solution)/shard_map/far_states/pallas_call | solution.py:72
  30.0 0.7 %collective-permute-start.9 = (bf16[4,128,128]{2,1,0:T(8,128)(2,1)S(1)}, bf16[4,128,128]{2,1,0:T(8,128)(2,1)S(1)}, u32[]{:S(2)}, u32[]{:S(2)}) collective-permute-start(bf16[4,128,128]{2,1,0:T(8,128)(2,1)S(1)} %get-tuple-element.77.refs_1_), channel_id=1, source_target_pairs={{0,4},{4,0},{8,12},{12,8},{16,20},{20,16},{24,28},{28,24},{1,5},{5... | collective-permute-start | bytes 393224 | tf_op jit(solution)/shard_map/ppermute | solution.py:276
  30.7 2.8 %intra.7 = (f32[8,128]{1,0:T(8,128)S(1)}, bf16[2,256,512]{2,1,0:T(8,128)(2,1)S(1)}, bf16[2,256,512]{2,1,0:T(8,128)(2,1)S(1)}, bf16[2,256,512]{2,1,0:T(8,128)(2,1)S(1)}) custom-call(s32[8]{0:T(128)S(1)} %stack.31.place_ref, f32[8,128]{1,0:T(8,128)S(1)} %get-tuple-element.72.refs_0_, bf16[1024,1024]{1,0:T(8,128)(2,1)S(1)} %copy-done, ...), custom_call_target="tpu_custom_call", output_to_operand_aliasing={{0}: (1, {})} | custom-call | flops 10000000000 | bytes 100000000 | tf_op jit(solution)/shard_map/intra/pallas_call | solution.py:72
  33.5 0.0 collective-permute-done.7.refs_2_.refs_20_.refs_23_
  33.5 0.0 collective-permute-done.8.refs_4_.refs_22_
  33.5 0.6 %last_round.2 = (f32[8,128]{1,0:T(8,128)S(1)}, bf16[4,128,128]{2,1,0:T(8,128)(2,1)S(1)}) custom-call(s32[8]{0:T(128)S(1)} %stack.31.place_ref, f32[8,128]{1,0:T(8,128)S(1)} %get-tuple-element.73.refs_0_, bf16[8,128,128]{2,1,0:T(8,128)(2,1)S(1)} %get-tuple-element.74.refs_1_, ...), custom_call_target="tpu_custom_call", output_to_operand_aliasing={{0}: (1, {})} | custom-call | flops 10000000000 | bytes 100000000 | tf_op jit(solution)/shard_map/last_round/pallas_call | solution.py:72
  34.1 1.4 %collective-permute-done.9.refs_2_.refs_24_ = bf16[4,128,128]{2,1,0:T(8,128)(2,1)S(1)} collective-permute-done((bf16[4,128,128]{2,1,0:T(8,128)(2,1)S(1)}, bf16[4,128,128]{2,1,0:T(8,128)(2,1)S(1)}, u32[]{:S(2)}, u32[]{:S(2)}) %collective-permute-start.9) | collective-permute-done | bytes 131104 | tf_op jit(solution)/shard_map/ppermute | solution.py:276
  35.5 0.6 %add.7 = (f32[8,128]{1,0:T(8,128)S(1)}, bf16[4,128,128]{2,1,0:T(8,128)(2,1)S(1)}) custom-call(s32[8]{0:T(128)S(1)} %stack.31.place_ref, f32[8,128]{1,0:T(8,128)S(1)} %get-tuple-element.76.refs_0_, bf16[4,128,128]{2,1,0:T(8,128)(2,1)S(1)} %get-tuple-element.77.refs_1_, ...), custom_call_target="tpu_custom_call", output_to_operand_aliasing={{0}: (1, {})} | custom-call | flops 10000000000 | bytes 100000000 | tf_op jit(solution)/shard_map/add/pallas_call | solution.py:72
  36.0 1.7 %collective-permute-start.10 = (bf16[4,128,128]{2,1,0:T(8,128)(2,1)S(1)}, bf16[4,128,128]{2,1,0:T(8,128)(2,1)S(1)}, u32[]{:S(2)}, u32[]{:S(2)}) collective-permute-start(bf16[4,128,128]{2,1,0:T(8,128)(2,1)S(1)} %get-tuple-element.79.refs_3_), channel_id=1, source_target_pairs={{0,8},{4,12},{8,0},{12,4},{16,24},{20,28},{24,16},{28,20},{1,9},{5... | collective-permute-start | bytes 393224 | tf_op jit(solution)/shard_map/ppermute | solution.py:276
  37.7 2.6 %collective-permute-start.11 = (bf16[4,128,128]{2,1,0:T(8,128)(2,1)S(1)}, bf16[4,128,128]{2,1,0:T(8,128)(2,1)S(1)}, u32[]{:S(2)}, u32[]{:S(2)}) collective-permute-start(bf16[4,128,128]{2,1,0:T(8,128)(2,1)S(1)} %get-tuple-element.92), channel_id=1, source_target_pairs={{0,16},{4,20},{8,24},{12,28},{16,0},{20,4},{24,8},{28,12},{1,17},{... | collective-permute-start | bytes 393224 | tf_op jit(solution)/shard_map/ppermute | solution.py:276
  40.3 2.8 %collective-permute-done.10.refs_4_.refs_25_ = bf16[4,128,128]{2,1,0:T(8,128)(2,1)S(1)} collective-permute-done((bf16[4,128,128]{2,1,0:T(8,128)(2,1)S(1)}, bf16[4,128,128]{2,1,0:T(8,128)(2,1)S(1)}, u32[]{:S(2)}, u32[]{:S(2)}) %collective-permute-start.10) | collective-permute-done | bytes 131104 | tf_op jit(solution)/shard_map/ppermute | solution.py:276
  43.1 0.6 %last_round.3 = (f32[8,128]{1,0:T(8,128)S(1)}, bf16[4,128,128]{2,1,0:T(8,128)(2,1)S(1)}) custom-call(s32[8]{0:T(128)S(1)} %stack.31.place_ref, f32[8,128]{1,0:T(8,128)S(1)} %get-tuple-element.78.refs_0_, bf16[8,128,128]{2,1,0:T(8,128)(2,1)S(1)} %get-tuple-element.74.refs_1_, ...), custom_call_target="tpu_custom_call", output_to_operand_aliasing={{0}: (1, {})} | custom-call | flops 10000000000 | bytes 100000000 | tf_op jit(solution)/shard_map/last_round/pallas_call | solution.py:72
  43.6 2.3 %collective-permute-start.12 = (bf16[4,128,128]{2,1,0:T(8,128)(2,1)S(1)}, bf16[4,128,128]{2,1,0:T(8,128)(2,1)S(1)}, u32[]{:S(2)}, u32[]{:S(2)}) collective-permute-start(bf16[4,128,128]{2,1,0:T(8,128)(2,1)S(1)} %get-tuple-element.101), channel_id=1, source_target_pairs={{0,16},{4,20},{8,24},{12,28},{16,0},{20,4},{24,8},{28,12},{1,17},{... | collective-permute-start | bytes 393224 | tf_op jit(solution)/shard_map/ppermute | solution.py:276
  46.0 0.9 %collective-permute-done.11.refs_23_ = bf16[4,128,128]{2,1,0:T(8,128)(2,1)S(1)} collective-permute-done((bf16[4,128,128]{2,1,0:T(8,128)(2,1)S(1)}, bf16[4,128,128]{2,1,0:T(8,128)(2,1)S(1)}, u32[]{:S(2)}, u32[]{:S(2)}) %collective-permute-start.11) | collective-permute-done | bytes 131104 | tf_op jit(solution)/shard_map/ppermute | solution.py:276
  46.9 3.8 %finish.2 = (f32[8,128]{1,0:T(8,128)S(1)}, bf16[1024,1024]{1,0:T(8,128)(2,1)}, bf16[1024,1024]{1,0:T(8,128)(2,1)}, bf16[1024,1024]{1,0:T(8,128)(2,1)}) custom-call(s32[8]{0:T(128)S(1)} %stack.31.place_ref, f32[8,128]{1,0:T(8,128)S(1)} %get-tuple-element.80.refs_0_, bf16[1024,1024]{1,0:T(8,128)(2,1)S(1)} %copy-done.1, ...), custom_call_target="tpu_custom_call", output_to_operand_aliasing={{0}: (1, {})} | custom-call | flops 10000000000 | bytes 100000000 | tf_op jit(solution)/shard_map/finish/pallas_call | solution.py:72
  50.7 1.6 %collective-permute-done.12.refs_26_ = bf16[4,128,128]{2,1,0:T(8,128)(2,1)S(1)} collective-permute-done((bf16[4,128,128]{2,1,0:T(8,128)(2,1)S(1)}, bf16[4,128,128]{2,1,0:T(8,128)(2,1)S(1)}, u32[]{:S(2)}, u32[]{:S(2)}) %collective-permute-start.12) | collective-permute-done | bytes 131104 | tf_op jit(solution)/shard_map/ppermute | solution.py:276
  52.3 3.8 %finish.3 = (f32[8,128]{1,0:T(8,128)S(1)}, bf16[1024,1024]{1,0:T(8,128)(2,1)}, bf16[1024,1024]{1,0:T(8,128)(2,1)}, bf16[1024,1024]{1,0:T(8,128)(2,1)}) custom-call(s32[8]{0:T(128)S(1)} %stack.31.place_ref, f32[8,128]{1,0:T(8,128)S(1)} %get-tuple-element.93.refs_0_, ...), custom_call_target="tpu_custom_call", output_to_operand_aliasing={{0}: (1, {}), {1}: (2, {}), {2}: (3, {}), {3}: (4, {})} | custom-call | flops 10000000000 | bytes 100000000 | tf_op jit(solution)/shard_map/finish/pallas_call | solution.py:72
  (1 shorter events, 0.0 us)
Async XLA Ops:
  0.7 5.3 %copy-start.1 = (bf16[1024,1024]{1,0:T(8,128)(2,1)S(1)}, bf16[1024,1024]{1,0:T(8,128)(2,1)}, u32[]{:S(2)}) copy-start(bf16[1024,1024]{1,0:T(8,128)(2,1)} %refs_4_.1) | copy-start | bytes 6291460
  0.7 5.3 %copy-start.2 = (bf16[1024,1024]{1,0:T(8,128)(2,1)S(1)}, bf16[1024,1024]{1,0:T(8,128)(2,1)}, u32[]{:S(2)}) copy-start(bf16[1024,1024]{1,0:T(8,128)(2,1)} %refs_5_.1) | copy-start | bytes 6291460
  2.8 17.0 %collective-permute-start.1 = (bf16[256,512]{1,0:T(8,128)(2,1)S(1)}, bf16[256,512]{1,0:T(8,128)(2,1)S(1)}, u32[]{:S(2)}, u32[]{:S(2)}) collective-permute-start(bf16[256,512]{1,0:T(8,128)(2,1)S(1)} %get-tuple-element.62), channel_id=1, source_target_pairs={{0,2},{1,3},{2,0},{3,1},{4,6},{5,7},{6,4},{7,5},{8,10},{9,11},{10,... | collective-permute-start | bytes 786440 | tf_op jit(solution)/shard_map/ppermute | solution.py:326
  5.8 14.0 %collective-permute-start.2 = (bf16[256,512]{1,0:T(8,128)(2,1)S(1)}, bf16[256,512]{1,0:T(8,128)(2,1)S(1)}, u32[]{:S(2)}, u32[]{:S(2)}) collective-permute-start(bf16[256,512]{1,0:T(8,128)(2,1)S(1)} %get-tuple-element.63), channel_id=1, source_target_pairs={{0,3},{1,2},{2,1},{3,0},{4,7},{5,6},{6,5},{7,4},{8,11},{9,10},{10,... | collective-permute-start | bytes 786440 | tf_op jit(solution)/shard_map/ppermute | solution.py:326
  5.8 3.8 %collective-permute-start = (bf16[256,1024]{1,0:T(8,128)(2,1)S(1)}, bf16[256,1024]{1,0:T(8,128)(2,1)S(1)}, u32[]{:S(2)}, u32[]{:S(2)}) collective-permute-start(bf16[256,1024]{1,0:T(8,128)(2,1)S(1)} %get-tuple-element.56), channel_id=1, source_target_pairs={{0,1},{1,0},{2,3},{3,2},{4,5},{5,4},{6,7},{7,6},{8,9},{9,8},{10,11... | collective-permute-start | bytes 1572872 | tf_op jit(solution)/shard_map/ppermute | solution.py:326
  7.6 12.2 %collective-permute-start.3 = (bf16[8,128,128]{2,1,0:T(8,128)(2,1)S(1)}, bf16[8,128,128]{2,1,0:T(8,128)(2,1)S(1)}, u32[]{:S(2)}, u32[]{:S(2)}) collective-permute-start(bf16[8,128,128]{2,1,0:T(8,128)(2,1)S(1)} %get-tuple-element.65.refs_5_), channel_id=1, source_target_pairs={{0,4},{4,0},{8,12},{12,8},{16,20},{20,16},{24,28},{28,24},{1,5},{5... | collective-permute-start | bytes 786440 | tf_op jit(solution)/shard_map/ppermute | solution.py:276
  9.6 3.4 %copy-start = (bf16[1024,1024]{1,0:T(8,128)(2,1)S(1)}, bf16[1024,1024]{1,0:T(8,128)(2,1)}, u32[]{:S(2)}) copy-start(bf16[1024,1024]{1,0:T(8,128)(2,1)} %refs_1_.18) | copy-start | bytes 6291460
  11.5 17.6 %collective-permute-start.5 = (bf16[256,512]{1,0:T(8,128)(2,1)S(1)}, bf16[256,512]{1,0:T(8,128)(2,1)S(1)}, u32[]{:S(2)}, u32[]{:S(2)}) collective-permute-start(bf16[256,512]{1,0:T(8,128)(2,1)S(1)} %get-tuple-element.70), channel_id=1, source_target_pairs={{0,2},{1,3},{2,0},{3,1},{4,6},{5,7},{6,4},{7,5},{8,10},{9,11},{10,... | collective-permute-start | bytes 786440 | tf_op jit(solution)/shard_map/ppermute | solution.py:326
  13.1 16.0 %collective-permute-start.6 = (bf16[256,512]{1,0:T(8,128)(2,1)S(1)}, bf16[256,512]{1,0:T(8,128)(2,1)S(1)}, u32[]{:S(2)}, u32[]{:S(2)}) collective-permute-start(bf16[256,512]{1,0:T(8,128)(2,1)S(1)} %get-tuple-element.71), channel_id=1, source_target_pairs={{0,3},{1,2},{2,1},{3,0},{4,7},{5,6},{6,5},{7,4},{8,11},{9,10},{10,... | collective-permute-start | bytes 786440 | tf_op jit(solution)/shard_map/ppermute | solution.py:326
  20.8 6.1 %collective-permute-start.4 = (bf16[4,128,128]{2,1,0:T(8,128)(2,1)S(1)}, bf16[4,128,128]{2,1,0:T(8,128)(2,1)S(1)}, u32[]{:S(2)}, u32[]{:S(2)}) collective-permute-start(bf16[4,128,128]{2,1,0:T(8,128)(2,1)S(1)} %get-tuple-element.68.refs_1_), channel_id=1, source_target_pairs={{0,4},{4,0},{8,12},{12,8},{16,20},{20,16},{24,28},{28,24},{1,5},{5... | collective-permute-start | bytes 393224 | tf_op jit(solution)/shard_map/ppermute | solution.py:276
  21.4 12.1 %collective-permute-start.7 = (bf16[8,128,128]{2,1,0:T(8,128)(2,1)S(1)}, bf16[8,128,128]{2,1,0:T(8,128)(2,1)S(1)}, u32[]{:S(2)}, u32[]{:S(2)}) collective-permute-start(bf16[8,128,128]{2,1,0:T(8,128)(2,1)S(1)} %get-tuple-element.74.refs_1_), channel_id=1, source_target_pairs={{0,8},{4,12},{8,0},{12,4},{16,24},{20,28},{24,16},{28,20},{1,9},{5... | collective-permute-start | bytes 786440 | tf_op jit(solution)/shard_map/ppermute | solution.py:276
  27.4 6.1 %collective-permute-start.8 = (bf16[4,128,128]{2,1,0:T(8,128)(2,1)S(1)}, bf16[4,128,128]{2,1,0:T(8,128)(2,1)S(1)}, u32[]{:S(2)}, u32[]{:S(2)}) collective-permute-start(bf16[4,128,128]{2,1,0:T(8,128)(2,1)S(1)} %get-tuple-element.75.refs_3_), channel_id=1, source_target_pairs={{0,8},{4,12},{8,0},{12,4},{16,24},{20,28},{24,16},{28,20},{1,9},{5... | collective-permute-start | bytes 393224 | tf_op jit(solution)/shard_map/ppermute | solution.py:276
  30.0 5.5 %collective-permute-start.9 = (bf16[4,128,128]{2,1,0:T(8,128)(2,1)S(1)}, bf16[4,128,128]{2,1,0:T(8,128)(2,1)S(1)}, u32[]{:S(2)}, u32[]{:S(2)}) collective-permute-start(bf16[4,128,128]{2,1,0:T(8,128)(2,1)S(1)} %get-tuple-element.77.refs_1_), channel_id=1, source_target_pairs={{0,4},{4,0},{8,12},{12,8},{16,20},{20,16},{24,28},{28,24},{1,5},{5... | collective-permute-start | bytes 393224 | tf_op jit(solution)/shard_map/ppermute | solution.py:276
  36.0 7.0 %collective-permute-start.10 = (bf16[4,128,128]{2,1,0:T(8,128)(2,1)S(1)}, bf16[4,128,128]{2,1,0:T(8,128)(2,1)S(1)}, u32[]{:S(2)}, u32[]{:S(2)}) collective-permute-start(bf16[4,128,128]{2,1,0:T(8,128)(2,1)S(1)} %get-tuple-element.79.refs_3_), channel_id=1, source_target_pairs={{0,8},{4,12},{8,0},{12,4},{16,24},{20,28},{24,16},{28,20},{1,9},{5... | collective-permute-start | bytes 393224 | tf_op jit(solution)/shard_map/ppermute | solution.py:276
  37.7 9.2 %collective-permute-start.11 = (bf16[4,128,128]{2,1,0:T(8,128)(2,1)S(1)}, bf16[4,128,128]{2,1,0:T(8,128)(2,1)S(1)}, u32[]{:S(2)}, u32[]{:S(2)}) collective-permute-start(bf16[4,128,128]{2,1,0:T(8,128)(2,1)S(1)} %get-tuple-element.92), channel_id=1, source_target_pairs={{0,16},{4,20},{8,24},{12,28},{16,0},{20,4},{24,8},{28,12},{1,17},{... | collective-permute-start | bytes 393224 | tf_op jit(solution)/shard_map/ppermute | solution.py:276
  43.6 8.7 %collective-permute-start.12 = (bf16[4,128,128]{2,1,0:T(8,128)(2,1)S(1)}, bf16[4,128,128]{2,1,0:T(8,128)(2,1)S(1)}, u32[]{:S(2)}, u32[]{:S(2)}) collective-permute-start(bf16[4,128,128]{2,1,0:T(8,128)(2,1)S(1)} %get-tuple-element.101), channel_id=1, source_target_pairs={{0,16},{4,20},{8,24},{12,28},{16,0},{20,4},{24,8},{28,12},{1,17},{... | collective-permute-start | bytes 393224 | tf_op jit(solution)/shard_map/ppermute | solution.py:276

commit v3 on v2

--- a/solution.py
+++ b/solution.py
@@ -9,7 +9,8 @@
 from jax.sharding import PartitionSpec as P
 
 HEAD_DIM = 128
-SPLITS = (4, 4)
+SPLITS = (4, 2, 2)
+ORDER = "S0 I0 K A0 S1 I1 S2 A1 L0 I2 A2 L1 L2 F0 F1 F2"
 COST = (10**10, 10**8)
 F32 = jnp.float32
 BF16 = jnp.bfloat16
@@ -28,8 +29,8 @@
     return slice(h * HEAD_DIM, (h + 1) * HEAD_DIM)
 
 
-def rows_of(place_ref, piece, chunk):
-    return pl.ds(pl.multiple_of(place_ref[piece] * chunk, chunk), chunk)
+def rows_of(here, piece, chunk):
+    return pl.ds(pl.multiple_of(here[0][piece] * chunk, chunk), chunk)
 
 
 def place_as(array, spec):
@@ -37,14 +38,15 @@
 
 
 class Chain:
-    def __init__(self, place):
-        self.place = place
-        self.token = jnp.zeros((8, 128), F32) + place[0].astype(F32)
+    def __init__(self, token, head_size, seq_size):
+        self.token = token
+        self.head_size, self.seq_bits = head_size, seq_size.bit_length() - 1
         self.waits = []
         self.jobs = []
+        self.through = []
 
     def add(self, *sums):
-        self.jobs += [one for one in sums if one.more()]
+        self.jobs += [one for one in sums if not one.closed]
 
     def wait(self, *arrays):
         self.waits += arrays
@@ -53,41 +55,50 @@
         extra = [self.token, *self.waits]
         jobs, self.waits, self.jobs = self.jobs, [], []
         skip, count = len(extra), len(operands)
+        through, self.through = self.through, []
         pairs = [array for sums in jobs for array in (sums.window, sums.parts[-1])]
         operands, in_specs = [*operands, *pairs], [*in_specs, *[VMEM] * len(pairs)]
         out_shape = [*[bf16(*sums.window.shape) for sums in jobs], *out_shape]
-        out_specs = [*[VMEM] * len(jobs), *out_specs]
-
-        def run(place_ref, *refs):
+        out_specs = [*[VMEM] * len(jobs), *out_specs, *[VMEM] * len(through)]
+        out_shape += [bf16(*array.shape) for array in through]
+        operands, in_specs = [*operands, *through], [*in_specs, *[VMEM] * len(through)]
+
+        def run(*refs):
+            rank, seq = lax.axis_index("head"), lax.axis_index("seq")
+            place = [rank ^ mask for mask in range(self.head_size)]
+            bits = [lax.shift_right_logical(seq, r) & 1 for r in range(self.seq_bits)]
             ins = refs[skip : skip + count]
-            pair_refs = refs[skip + count : skip + len(operands)]
+            pair_refs = refs[skip + count : skip + count + len(pairs)]
             outs = refs[skip + len(operands) + 1 :]
             for n in range(len(jobs)):
                 outs[n][...] = pair_refs[2 * n][...] + pair_refs[2 * n + 1][...]
-            kernel(place_ref, *ins, *outs[len(jobs) :])
-
-        aliases = {1: 0}
+            kernel((place, bits), *ins, *outs[len(jobs) : len(outs) - len(through)])
+
+        aliases = {0: 0}
+        for n in range(len(through)):
+            aliases[skip + len(operands) - 1 - n] = len(out_shape) - n
         for source, target in (alias or {}).items():
-            aliases[1 + skip + source] = 1 + len(jobs) + target
+            aliases[skip + source] = 1 + len(jobs) + target
         self.token, *outs = pl.pallas_call(
             run,
-            grid_spec=pltpu.PrefetchScalarGridSpec(
-                num_scalar_prefetch=1,
-                grid=grid,
-                in_specs=[ANY] * skip + list(in_specs),
-                out_specs=[ANY] + list(out_specs),
-                scratch_shapes=list(scratch),
-            ),
+            grid=grid,
+            in_specs=[ANY] * skip + list(in_specs),
+            out_specs=[ANY] + list(out_specs),
+            scratch_shapes=list(scratch),
             out_shape=[jax.ShapeDtypeStruct((8, 128), F32)] + list(out_shape),
             input_output_aliases=aliases,
             compiler_params=pltpu.CompilerParams(vmem_limit_bytes=8 * 1024 * 1024),
             cost_estimate=pl.CostEstimate(flops=cost[0], bytes_accessed=cost[1], transcendentals=0),
             name=name,
-        )(self.place, *extra, *[place_as(x, s) for x, s in zip(operands, in_specs)])
+        )(*extra, *[place_as(x, s) for x, s in zip(operands, in_specs)])
         for sums, window in zip(jobs, outs):
             sums.window = window
-            sums.go()
-        return outs[len(jobs) :]
+            if sums.more():
+                sums.go()
+            else:
+                sums.closed = True
+        self.passed = outs[len(outs) - len(through) :]
+        return outs[len(jobs) : len(outs) - len(through)]
 
 
 def bf16(*shape):
@@ -96,12 +107,13 @@
 
 def cut(chain, out_grads, parts):
     chunk = out_grads.shape[0]
-
-    def kernel(place_ref, g_ref, *refs):
+    width = out_grads.shape[1] // chain.head_size
+
+    def kernel(here, g_ref, *refs):
         outs, sems = refs[:-1], refs[-1]
         copies = []
         for n, (mask, head0, heads) in enumerate(parts):
-            start = place_ref[mask] * place_ref[4] + head0 * HEAD_DIM
+            start = here[0][mask] * width + head0 * HEAD_DIM
             cols = pl.ds(pl.multiple_of(start, HEAD_DIM), heads * HEAD_DIM)
             copies.append(pltpu.make_async_copy(g_ref.at[:, cols], outs[n], sems.at[n]))
         for copy in copies:
@@ -120,7 +132,7 @@
     rows, width = key_rows.shape
     heads, chunks = width // HEAD_DIM, rows // chunk
 
-    def kernel(place_ref, k_ref, v_ref, local_ref, total_ref):
+    def kernel(here, k_ref, v_ref, local_ref, total_ref):
         for h in range(heads):
             run = jnp.zeros((HEAD_DIM, HEAD_DIM), F32)
             for c in range(chunks):
@@ -138,13 +150,13 @@
 def intra(chain, pieces, arrays, grads, head0, heads, chunk):
     count = len(pieces)
 
-    def kernel(place_ref, q_ref, k_ref, v_ref, *refs):
+    def kernel(here, q_ref, k_ref, v_ref, *refs):
         g_refs, outs = refs[:count], refs[count:]
         row = lax.broadcasted_iota(jnp.int32, (chunk, chunk), 0)
         col = lax.broadcasted_iota(jnp.int32, (chunk, chunk), 1)
         upper, lower = row <= col, row >= col
         for n, piece in enumerate(pieces):
-            rows = rows_of(place_ref, piece, chunk)
+            rows = rows_of(here, piece, chunk)
             for h in range(heads):
                 cols, own = head_cols(head0 + h), head_cols(h)
                 q, k, v, g = q_ref[rows, cols], k_ref[rows, cols], v_ref[rows, cols], g_refs[n][:, own]
@@ -164,11 +176,11 @@
 def near_states(chain, query_rows, grads, chunk):
     heads = query_rows.shape[1] // HEAD_DIM
 
-    def kernel(place_ref, q_ref, g0, g1, state_ref):
+    def kernel(here, q_ref, g0, g1, state_ref):
         for h in range(heads):
             cols = head_cols(h)
             for n, g_ref in enumerate((g0, g1)):
-                q = q_ref[rows_of(place_ref, n, chunk), cols]
+                q = q_ref[rows_of(here, n, chunk), cols]
                 state_ref[n, h] = dot(q, g_ref[:, cols], TN).astype(BF16)
 
     return chain(
@@ -178,11 +190,11 @@
 
 
 def far_states(chain, query_rows, grads, near, head0, heads, chunk):
-    def kernel(place_ref, q_ref, g0, g1, near_ref, state_ref, total_ref):
+    def kernel(here, q_ref, g0, g1, near_ref, state_ref, total_ref):
         for h in range(heads):
             cols, own = head_cols(head0 + h), head_cols(h)
-            a = dot(q_ref[rows_of(place_ref, 2, chunk), cols], g0[:, own], TN)
-            b = dot(q_ref[rows_of(place_ref, 3, chunk), cols], g1[:, own], TN)
+            a = dot(q_ref[rows_of(here, 2, chunk), cols], g0[:, own], TN)
+            b = dot(q_ref[rows_of(here, 3, chunk), cols], g1[:, own], TN)
             state_ref[0, h] = a.astype(BF16)
             state_ref[1, h] = b.astype(BF16)
             total = a + b + near_ref[0, head0 + h].astype(F32) + near_ref[1, head0 + h].astype(F32)
@@ -198,7 +210,7 @@
     rows, feat = key_rows.shape
     rounds = len(kv_in)
 
-    def kernel(place_ref, *refs):
+    def kernel(here, *refs):
         refs = list(refs)
         if outs is not None:
             refs = refs[3:]
@@ -217,11 +229,11 @@
         (last_ref,) = take(1)
         dq_ref, dk_ref, dv_ref = refs
         h = pl.program_id(0)
-        bit = place_ref[5 + rounds].astype(F32)
+        bit = here[1][rounds].astype(F32)
         got = last_ref[h].astype(F32)
         prefix, suffix = got * bit, got * (1.0 - bit)
         for r in range(rounds):
-            bit = place_ref[5 + r].astype(F32)
+            bit = here[1][r].astype(F32)
             prefix = prefix + kv_refs[r][head0 + h].astype(F32) * bit
             suffix = suffix + grad_refs[r][h].astype(F32) * (1.0 - bit)
         wide = pl.ds(pl.multiple_of((head0 + h) * HEAD_DIM, HEAD_DIM), HEAD_DIM)
@@ -232,15 +244,15 @@
         ]
         state = [s.astype(F32) for s in state]
         for piece in range(4):
-            place = place_ref[piece]
-            at = rows_of(place_ref, piece, chunk)
+            place = here[0][piece]
+            at = rows_of(here, piece, chunk)
             part, slot = part_refs[min(piece, 2)], max(piece - 2, 0)
             cols = wide if piece < 2 else narrow
             before_low = (prefix + local_ref[place, head0 + h].astype(F32)).astype(BF16)
             after = suffix
             for other in range(4):
                 if other != piece:
-                    later = (place_ref[other] > place).astype(F32)
+                    later = (here[0][other] > place).astype(F32)
                     after = after + later * state[other]
             after_low = after.astype(BF16)
             out = part[0][slot, :, cols].astype(F32) + dot(g_refs[piece][:, cols], before_low, NN)
@@ -262,7 +274,7 @@
         alias = {0: 0, 1: 1, 2: 2}
     return chain(
         "finish", kernel, operands, in_specs, [pltpu.HBM((rows, feat), BF16)] * 3,
-        [pl.BlockSpec((rows, HEAD_DIM), lambda i, place: (0, i + head0))] * 3,
+        [pl.BlockSpec((rows, HEAD_DIM), lambda i: (0, i + head0))] * 3,
         grid=(heads,), alias=alias,
     )
 
@@ -270,7 +282,7 @@
 class SeqSums:
     def __init__(self, total, axis, size):
         self.window, self.axis, self.size = total, axis, size
-        self.step, self.parts = 1, []
+        self.step, self.parts, self.closed = 1, [], False
 
     def swap(self, block):
         got = lax.ppermute(block, self.axis, [(i, i ^ self.step) for i in range(self.size)])
@@ -286,14 +298,14 @@
 
 def add_only(chain):
     if chain.jobs:
-        chain("add", lambda place_ref: None, [], [], [], [])
+        chain("add", lambda here: None, [], [], [], [])
 
 
 def last_round(chain, prefix_sums, suffix_sums, head0, heads):
     rounds = len(suffix_sums.parts)
 
-    def kernel(place_ref, kv_a, kv_b, grad_a, grad_b, out_ref):
-        upper = place_ref[5 + rounds] == 1
+    def kernel(here, kv_ref, grad_a, grad_b, out_ref):
+        upper = here[1][rounds] == 1
 
         @pl.when(upper)
         def _():
@@ -301,11 +313,10 @@
 
         @pl.when(jnp.logical_not(upper))
         def _():
-            at = slice(head0, head0 + heads)
-            out_ref[...] = kv_a[at] + kv_b[at]
-
-    operands = [prefix_sums.window, prefix_sums.parts[-1], suffix_sums.window, suffix_sums.parts[-1]]
-    block = chain("last_round", kernel, operands, [VMEM] * 4, [bf16(heads, HEAD_DIM, HEAD_DIM)], [VMEM])[0]
+            out_ref[...] = kv_ref[head0 : head0 + heads]
+
+    operands = [prefix_sums.window, suffix_sums.window, suffix_sums.parts[-1]]
+    block = chain("last_round", kernel, operands, [VMEM] * 3, [bf16(heads, HEAD_DIM, HEAD_DIM)], [VMEM])[0]
     return suffix_sums.swap(block)
 
 
@@ -314,11 +325,7 @@
     chunk = rows // head_size
     head_count = feat // HEAD_DIM
     factor = 1.0 / math.sqrt(HEAD_DIM * rows * seq_size)
-    rank = lax.axis_index("head")
-    seq = lax.axis_index("seq")
-    bits = [(seq >> r) & 1 for r in range(seq_size.bit_length() - 1)]
-    place = jnp.stack([rank, rank ^ 1, rank ^ 2, rank ^ 3, jnp.full_like(rank, feat), *bits])
-    chain = Chain(place.astype(jnp.int32))
+    chain = Chain(jnp.zeros((8, 128), F32), head_size, seq_size)
     arrays = (query_rows, key_rows, value_rows)
     firsts = [sum(SPLITS[:s]) for s in range(len(SPLITS))]
 
@@ -333,19 +340,27 @@
     kv_sums = SeqSums(kv_total, "seq", seq_size)
     kv_sums.go()
     chain.wait(near_grad)
-    f, n = firsts[1], SPLITS[1]
-    own_grad, *blocks = cut(chain, out_grads, [(0, 0, head_count), (2, f, n), (3, f, n)])
+    wanted = [(0, 0, head_count)]
+    for f, n in zip(firsts[1:], SPLITS[1:]):
+        wanted += [(2, f, n), (3, f, n)]
+    own_grad, *blocks = cut(chain, out_grads, wanted)
     crossing.append([send(blocks[0], 2), send(blocks[1], 3)])
+    later = blocks[2:]
     own_part = intra(chain, [0], arrays, [own_grad], 0, head_count, chunk)
+    chain.add(kv_sums)
     near_state = near_states(chain, query_rows, (own_grad, near_grad), chunk)
     near_part = intra(chain, [1], arrays, [near_grad], 0, head_count, chunk)
 
-    far_state, far_part, sums, lasts = [], [], [], []
+    far_state, far_part, sums, lasts, outs = [], [], [], [], None
 
     def states(s):
         f, n = firsts[s], SPLITS[s]
+        if s + 2 < len(SPLITS):
+            chain.through = later[2 * s : 2 * s + 2]
         far, total = far_states(chain, query_rows, crossing[s], near_state, f, n, chunk)
         far_state.append(far)
+        if s + 2 < len(SPLITS):
+            crossing.append([send(chain.passed[0], 2), send(chain.passed[1], 3)])
         sums.append(SeqSums(total, "seq", seq_size))
         sums[s].go()
 
@@ -354,32 +369,29 @@
             chain.add(one)
             add_only(chain)
 
-    def inside(s):
-        far_part.append(intra(chain, [2, 3], arrays, crossing[s], firsts[s], SPLITS[s], chunk))
-
-    def last(s):
-        settle(sums[s])
-        lasts.append(last_round(chain, kv_sums, sums[s], firsts[s], SPLITS[s]))
-
-    chain.add(kv_sums)
-    states(0)
-    inside(0)
-    chain.add(sums[0])
-    add_only(chain)
-    states(1)
-    inside(1)
-    settle(kv_sums)
-    last(0)
-    chain.add(sums[1])
-    add_only(chain)
-    last(1)
-    outs = None
-    for s, (f, n) in enumerate(zip(firsts, SPLITS)):
-        outs = finish(
-            chain, key_rows, value_rows, (own_grad, near_grad, *crossing[s]),
-            (own_part, near_part, far_part[s]), (near_state, far_state[s]),
-            local, kv_sums.parts, sums[s].parts, lasts[s], f, n, chunk, factor, outs,
-        )
+    for step in ORDER.split():
+        s = int(step[1:] or 0)
+        if step[0] == "K":
+            chain.add(kv_sums)
+        elif step[0] == "S":
+            states(s)
+        elif step[0] == "I":
+            far_part.append(intra(chain, [2, 3], arrays, crossing[s], firsts[s], SPLITS[s], chunk))
+        elif step[0] == "A":
+            chain.add(sums[s])
+            add_only(chain)
+        elif step[0] == "L":
+            settle(sums[s])
+            while not kv_sums.closed:
+                chain.add(kv_sums)
+                add_only(chain)
+            lasts.append(last_round(chain, kv_sums, sums[s], firsts[s], SPLITS[s]))
+        else:
+            outs = finish(
+                chain, key_rows, value_rows, (own_grad, near_grad, *crossing[s]),
+                (own_part, near_part, far_part[s]), (near_state, far_state[s]),
+                local, kv_sums.parts, sums[s].parts, lasts[s], firsts[s], SPLITS[s], chunk, factor, outs,
+            )
     return tuple(outs)
 
 

time: 56.2 us -> 51 us (0.907)
  Pallas kernels: 29.5 us -> 21.8 us
  starting transfers between devices: 17.9 us -> 23.2 us
  waiting for transfers between devices: 7.78 us -> 5.02 us
    pallas_call x16 -> x21, Pallas kernels: 29.5 us -> 21.8 us  [__call__(): pl.pallas_call(run, grid=grid, in_specs=[ANY] * skip + list(in_specs), ou...]
    ppermute x8 -> x11, waiting for transfers between devices: 7.77 us -> 3.86 us  [swap(): lax.ppermute(block, self.axis, [(i, i ^ self.step) for i in range(self.si...]
    ppermute x8 -> x11, starting transfers between devices: 13.1 us -> 16.8 us  [swap(): lax.ppermute(block, self.axis, [(i, i ^ self.step) for i in range(self.si...]
    ppermute x5 -> x7, starting transfers between devices: 4.81 us -> 6.41 us  [send(): lax.ppermute(block, 'head', [(i, i ^ mask) for i in range(head_size)])]
    ppermute x5 -> x7, waiting for transfers between devices: 0.01 us -> 1.17 us  [send(): lax.ppermute(block, 'head', [(i, i ^ mask) for i in range(head_size)])]
  transfers between devices with their start and end apart: 13 -> 18, of which waited for: 5 -> 4; matrix products, arithmetic and copies ran while one was open for 0% -> 0% of each run, Pallas kernels for 41% -> 37%
where the time goes in v3:
time: 51 us; the launch traced here: 50.8 us
  starting transfers between devices  23.2 us (45%)
  Pallas kernels  21.8 us (43%)
  waiting for transfers between devices  5.02 us (10%)
  between operations  0.8 us (2%)
    pallas_call x21, Pallas kernels, __call__(): pl.pallas_call(run, grid=grid, in_specs=[ANY] * skip + list(in_specs), ou...  21.8 us
    ppermute x11, starting transfers between devices, swap(): lax.ppermute(block, self.axis, [(i, i ^ self.step) for i in range(self.si...  16.8 us
    ppermute x7, starting transfers between devices, send(): lax.ppermute(block, 'head', [(i, i ^ mask) for i in range(head_size)])  6.41 us
    ppermute x11, waiting for transfers between devices, swap(): lax.ppermute(block, self.axis, [(i, i ^ self.step) for i in range(self.si...  3.86 us
    ppermute x7, waiting for transfers between devices, send(): lax.ppermute(block, 'head', [(i, i ^ mask) for i in range(head_size)])  1.17 us
  transfers between devices with their start and end apart: 18, of which 4 were waited for; matrix products, arithmetic and copies ran while one was open for 0% of the time, Pallas kernels for 37%

profile of v3, /device:TPU:0, one launch (start us, length us, event | category | flops | bytes accessed | tf_op | source)
XLA Modules:
  0.0 50.8 jit_solution(9516353988744695829)
XLA Ops:
  0.6 0.0 copy-start.1
  0.7 0.0 copy-start.2
  0.7 1.4 %cut.2 = (f32[8,128]{1,0:T(8,128)S(1)}, bf16[256,1024]{1,0:T(8,128)(2,1)S(1)}, bf16[256,512]{1,0:T(8,128)(2,1)S(1)}, bf16[256,512]{1,0:T(8,128)(2,1)S(1)}) custom-call(f32[8,128]{1,0:T(8,128)S(1)} %broadcast_in_dim.3.refs_0_, bf16[256,4096]{1,0:T(8,128)(2,1)} %refs_2_.9), custom_call_target="tpu_custom_call", output_to_operand_aliasing={{0}: (0, {})} | custom-call | flops 10000000000 | bytes 100000000 | tf_op jit(solution)/shard_map/cut/pallas_call | solution.py:82
  2.0 3.0 %collective-permute-start.2 = (bf16[256,512]{1,0:T(8,128)(2,1)S(1)}, bf16[256,512]{1,0:T(8,128)(2,1)S(1)}, u32[]{:S(2)}, u32[]{:S(2)}) collective-permute-start(bf16[256,512]{1,0:T(8,128)(2,1)S(1)} %get-tuple-element.83), channel_id=1, source_target_pairs={{0,2},{1,3},{2,0},{3,1},{4,6},{5,7},{6,4},{7,5},{8,10},{9,11},{10,... | collective-permute-start | bytes 786440 | tf_op jit(solution)/shard_map/ppermute | solution.py:333
  5.1 0.0 collective-permute-start.3
  5.1 0.2 collective-permute-start
  5.3 0.0 copy-done.1
  5.3 0.0 copy-done.2
  5.3 1.1 %kv_states.1 = (f32[8,128]{1,0:T(8,128)S(1)}, bf16[4,8,128,128]{3,2,1,0:T(8,128)(2,1)S(1)}, bf16[8,128,128]{2,1,0:T(8,128)(2,1)S(1)}) custom-call(f32[8,128]{1,0:T(8,128)S(1)} %get-tuple-element.74.refs_0_, bf16[1024,1024]{1,0:T(8,128)(2,1)S(1)} %copy-done.1, bf16[1024,1024]{1,0:T(8,128)(2,1)S(1)} %copy-done.2), custom_call_target="tpu_custom_call", output_to_operand_aliasing={{0}: (0, {})} | custom-call | flops 10000000000 | bytes 100000000 | tf_op jit(solution)/shard_map/kv_states/pallas_call | solution.py:82
  6.4 2.0 %collective-permute-start.1 = (bf16[8,128,128]{2,1,0:T(8,128)(2,1)S(1)}, bf16[8,128,128]{2,1,0:T(8,128)(2,1)S(1)}, u32[]{:S(2)}, u32[]{:S(2)}) collective-permute-start(bf16[8,128,128]{2,1,0:T(8,128)(2,1)S(1)} %get-tuple-element.80.refs_4_), channel_id=1, source_target_pairs={{0,4},{4,0},{8,12},{12,8},{16,20},{20,16},{24,28},{28,24},{1,5},{5... | collective-permute-start | bytes 786440 | tf_op jit(solution)/shard_map/ppermute | solution.py:288
  8.3 0.0 collective-permute-done.refs_1_.refs_3_.refs_4_.refs_7_
  8.3 0.0 copy-start
  8.4 1.4 %cut.3 = (f32[8,128]{1,0:T(8,128)S(1)}, bf16[256,1024]{1,0:T(8,128)(2,1)S(1)}, bf16[256,256]{1,0:T(8,128)(2,1)S(1)}, bf16[256,256]{1,0:T(8,128)(2,1)S(1)}, bf16[...) custom-call(f32[8,128]{1,0:T(8,128)S(1)} %get-tuple-element.75.refs_0_, ...), custom_call_target="tpu_custom_call", output_to_operand_aliasing={{0}: (0, {})} | custom-call | flops 10000000000 | bytes 100000000 | tf_op jit(solution)/shard_map/cut/pallas_call | solution.py:82
  9.7 1.6 %collective-permute-start.6 = (bf16[256,256]{1,0:T(8,128)(2,1)S(1)}, bf16[256,256]{1,0:T(8,128)(2,1)S(1)}, u32[]{:S(2)}, u32[]{:S(2)}) collective-permute-start(bf16[256,256]{1,0:T(8,128)(2,1)S(1)} %get-tuple-element.93), channel_id=1, source_target_pairs={{0,2},{1,3},{2,0},{3,1},{4,6},{5,7},{6,4},{7,5},{8,10},{9,11},{10,... | collective-permute-start | bytes 393224 | tf_op jit(solution)/shard_map/ppermute | solution.py:333
  11.3 0.0 collective-permute-start.7
  11.3 0.0 copy-done
  11.3 2.3 %intra.5 = (f32[8,128]{1,0:T(8,128)S(1)}, bf16[1,256,1024]{2,1,0:T(8,128)(2,1)S(1)}, bf16[1,256,1024]{2,1,0:T(8,128)(2,1)S(1)}, bf16[1,256,1024]{2,1,0:T(8,128)(2,1)S(1)}) custom-call(f32[8,128]{1,0:T(8,128)S(1)} %get-tuple-element.77.refs_0_, bf16[1024,1024]{1,0:T(8,128)(2,1)S(1)} %copy-done, ...), custom_call_target="tpu_custom_call", output_to_operand_aliasing={{0}: (0, {})} | custom-call | flops 10000000000 | bytes 100000000 | tf_op jit(solution)/shard_map/intra/pallas_call | solution.py:82
  13.6 1.3 %collective-permute-done.1.refs_5_.refs_19_.refs_22_ = bf16[8,128,128]{2,1,0:T(8,128)(2,1)S(1)} collective-permute-done((bf16[8,128,128]{2,1,0:T(8,128)(2,1)S(1)}, bf16[8,128,128]{2,1,0:T(8,128)(2,1)S(1)}, u32[]{:S(2)}, u32[]{:S(2)}) %collective-permute-start.1) | collective-permute-done | bytes 262176 | tf_op jit(solution)/shard_map/ppermute | solution.py:288
  14.9 0.6 %near_states.1 = (f32[8,128]{1,0:T(8,128)S(1)}, bf16[8,128,128]{2,1,0:T(8,128)(2,1)S(1)}, bf16[2,8,128,128]{3,2,1,0:T(8,128)(2,1)S(1)}) custom-call(f32[8,128]{1,0:T(8,128)S(1)} %get-tuple-element.79.refs_0_, bf16[1024,1024]{1,0:T(8,128)(2,1)S(1)} %copy-done, ...), custom_call_target="tpu_custom_call", output_to_operand_aliasing={{0}: (0, {})} | custom-call | flops 10000000000 | bytes 100000000 | tf_op jit(solution)/shard_map/near_states/pallas_call | solution.py:82
  15.5 1.8 %collective-permute-start.4 = (bf16[8,128,128]{2,1,0:T(8,128)(2,1)S(1)}, bf16[8,128,128]{2,1,0:T(8,128)(2,1)S(1)}, u32[]{:S(2)}, u32[]{:S(2)}) collective-permute-start(bf16[8,128,128]{2,1,0:T(8,128)(2,1)S(1)} %get-tuple-element.90.refs_1_), channel_id=1, source_target_pairs={{0,8},{4,12},{8,0},{12,4},{16,24},{20,28},{24,16},{28,20},{1,9},{5... | collective-permute-start | bytes 786440 | tf_op jit(solution)/shard_map/ppermute | solution.py:288
  17.3 2.3 %intra.6 = (f32[8,128]{1,0:T(8,128)S(1)}, bf16[1,256,1024]{2,1,0:T(8,128)(2,1)S(1)}, bf16[1,256,1024]{2,1,0:T(8,128)(2,1)S(1)}, bf16[1,256,1024]{2,1,0:T(8,128)(2,1)S(1)}) custom-call(f32[8,128]{1,0:T(8,128)S(1)} %get-tuple-element.81.refs_0_, bf16[1024,1024]{1,0:T(8,128)(2,1)S(1)} %copy-done, ...), custom_call_target="tpu_custom_call", output_to_operand_aliasing={{0}: (0, {})} | custom-call | flops 10000000000 | bytes 100000000 | tf_op jit(solution)/shard_map/intra/pallas_call | solution.py:82
  19.5 0.0 collective-permute-done.2.refs_2_.refs_4_.refs_5_
  19.6 0.0 collective-permute-done.3.refs_3_.refs_5_.refs_6_
  19.6 0.4 far_states.3
  19.9 1.6 %collective-permute-start.8 = (bf16[256,256]{1,0:T(8,128)(2,1)S(1)}, bf16[256,256]{1,0:T(8,128)(2,1)S(1)}, u32[]{:S(2)}, u32[]{:S(2)}) collective-permute-start(bf16[256,256]{1,0:T(8,128)(2,1)S(1)} %get-tuple-element.97), channel_id=1, source_target_pairs={{0,2},{1,3},{2,0},{3,1},{4,6},{5,7},{6,4},{7,5},{8,10},{9,11},{10,... | collective-permute-start | bytes 393224 | tf_op jit(solution)/shard_map/ppermute | solution.py:333
  21.5 1.5 %collective-permute-start.5 = (bf16[4,128,128]{2,1,0:T(8,128)(2,1)S(1)}, bf16[4,128,128]{2,1,0:T(8,128)(2,1)S(1)}, u32[]{:S(2)}, u32[]{:S(2)}) collective-permute-start(bf16[4,128,128]{2,1,0:T(8,128)(2,1)S(1)} %get-tuple-element.91.refs_3_), channel_id=1, source_target_pairs={{0,4},{4,0},{8,12},{12,8},{16,20},{20,16},{24,28},{28,24},{1,5},{5... | collective-permute-start | bytes 393224 | tf_op jit(solution)/shard_map/ppermute | solution.py:288
  23.0 2.3 %intra.7 = (f32[8,128]{1,0:T(8,128)S(1)}, bf16[2,256,512]{2,1,0:T(8,128)(2,1)S(1)}, bf16[2,256,512]{2,1,0:T(8,128)(2,1)S(1)}, bf16[2,256,512]{2,1,0:T(8,128)(2,1)S(1)}) custom-call(f32[8,128]{1,0:T(8,128)S(1)} %get-tuple-element.88.refs_0_, bf16[1024,1024]{1,0:T(8,128)(2,1)S(1)} %copy-done, ...), custom_call_target="tpu_custom_call", output_to_operand_aliasing={{0}: (0, {})} | custom-call | flops 10000000000 | bytes 100000000 | tf_op jit(solution)/shard_map/intra/pallas_call | solution.py:82
  25.3 1.2 %collective-permute-done.5.refs_4_.refs_21_ = bf16[4,128,128]{2,1,0:T(8,128)(2,1)S(1)} collective-permute-done((bf16[4,128,128]{2,1,0:T(8,128)(2,1)S(1)}, bf16[4,128,128]{2,1,0:T(8,128)(2,1)S(1)}, u32[]{:S(2)}, u32[]{:S(2)}) %collective-permute-start.5) | collective-permute-done | bytes 131104 | tf_op jit(solution)/shard_map/ppermute | solution.py:288
  26.5 0.0 collective-permute-start.9
  26.5 0.0 collective-permute-done.4.refs_2_.refs_20_.refs_23_
  26.5 0.1 add.3
  26.6 0.5 collective-permute-start.11
  27.1 0.0 collective-permute-done.6.refs_2_.refs_4_.refs_8_
  27.1 0.0 collective-permute-done.7.refs_3_.refs_5_.refs_9_
  27.1 0.3 far_states.4
  27.4 1.6 %collective-permute-start.10 = (bf16[2,128,128]{2,1,0:T(8,128)(2,1)S(1)}, bf16[2,128,128]{2,1,0:T(8,128)(2,1)S(1)}, u32[]{:S(2)}, u32[]{:S(2)}) collective-permute-start(bf16[2,128,128]{2,1,0:T(8,128)(2,1)S(1)} %get-tuple-element.100.refs_1_), channel_id=1, source_target_pairs={{0,4},{4,0},{8,12},{12,8},{16,20},{20,16},{24,28},{28,24},{1,5},{5... | collective-permute-start | bytes 196616 | tf_op jit(solution)/shard_map/ppermute | solution.py:288
  29.0 1.2 %intra.8 = (f32[8,128]{1,0:T(8,128)S(1)}, bf16[2,256,256]{2,1,0:T(8,128)(2,1)S(1)}, bf16[2,256,256]{2,1,0:T(8,128)(2,1)S(1)}, bf16[2,256,256]{2,1,0:T(8,128)(2,1)S(1)}) custom-call(f32[8,128]{1,0:T(8,128)S(1)} %get-tuple-element.95.refs_0_, bf16[1024,1024]{1,0:T(8,128)(2,1)S(1)} %copy-done, ...), custom_call_target="tpu_custom_call", output_to_operand_aliasing={{0}: (0, {})} | custom-call | flops 10000000000 | bytes 100000000 | tf_op jit(solution)/shard_map/intra/pallas_call | solution.py:82
  30.2 0.0 collective-permute-done.8.refs_2_.refs_4_.refs_8_
  30.2 1.1 %collective-permute-done.9.refs_3_.refs_5_.refs_9_ = bf16[256,256]{1,0:T(8,128)(2,1)S(1)} collective-permute-done((bf16[256,256]{1,0:T(8,128)(2,1)S(1)}, bf16[256,256]{1,0:T(8,128)(2,1)S(1)}, u32[]{:S(2)}, u32[]{:S(2)}) %collective-permute-start.9) | collective-permute-done | bytes 131104 | tf_op jit(solution)/shard_map/ppermute | solution.py:333
  31.3 0.3 far_states.5
  31.6 1.6 %collective-permute-start.12 = (bf16[2,128,128]{2,1,0:T(8,128)(2,1)S(1)}, bf16[2,128,128]{2,1,0:T(8,128)(2,1)S(1)}, u32[]{:S(2)}, u32[]{:S(2)}) collective-permute-start(bf16[2,128,128]{2,1,0:T(8,128)(2,1)S(1)} %get-tuple-element.106.refs_1_), channel_id=1, source_target_pairs={{0,4},{4,0},{8,12},{12,8},{16,20},{20,16},{24,28},{28,24},{1,5},{5... | collective-permute-start | bytes 196616 | tf_op jit(solution)/shard_map/ppermute | solution.py:288
  33.2 0.0 collective-permute-done.10.refs_2_.refs_24_
  33.2 0.5 %collective-permute-start.13 = (bf16[2,128,128]{2,1,0:T(8,128)(2,1)S(1)}, bf16[2,128,128]{2,1,0:T(8,128)(2,1)S(1)}, u32[]{:S(2)}, u32[]{:S(2)}) collective-permute-start(bf16[2,128,128]{2,1,0:T(8,128)(2,1)S(1)} %get-tuple-element.108.refs_2_), channel_id=1, source_target_pairs={{0,8},{4,12},{8,0},{12,4},{16,24},{20,28},{24,16},{28,20},{1,9},{5... | collective-permute-start | bytes 196616 | tf_op jit(solution)/shard_map/ppermute | solution.py:288
  33.7 0.0 collective-permute-done.11.refs_3_.refs_22_
  33.7 0.2 last_round.3
  33.9 2.7 %collective-permute-start.15 = (bf16[4,128,128]{2,1,0:T(8,128)(2,1)S(1)}, bf16[4,128,128]{2,1,0:T(8,128)(2,1)S(1)}, u32[]{:S(2)}, u32[]{:S(2)}) collective-permute-start(bf16[4,128,128]{2,1,0:T(8,128)(2,1)S(1)} %get-tuple-element.123), channel_id=1, source_target_pairs={{0,16},{4,20},{8,24},{12,28},{16,0},{20,4},{24,8},{28,12},{1,17},{... | collective-permute-start | bytes 393224 | tf_op jit(solution)/shard_map/ppermute | solution.py:288
  36.6 1.2 %intra.9 = (f32[8,128]{1,0:T(8,128)S(1)}, bf16[2,256,256]{2,1,0:T(8,128)(2,1)S(1)}, bf16[2,256,256]{2,1,0:T(8,128)(2,1)S(1)}, bf16[2,256,256]{2,1,0:T(8,128)(2,1)S(1)}) custom-call(f32[8,128]{1,0:T(8,128)S(1)} %get-tuple-element.104.refs_0_, bf16[1024,1024]{1,0:T(8,128)(2,1)S(1)} %copy-done, ...), custom_call_target="tpu_custom_call", output_to_operand_aliasing={{0}: (0, {})} | custom-call | flops 10000000000 | bytes 100000000 | tf_op jit(solution)/shard_map/intra/pallas_call | solution.py:82
  37.8 0.0 collective-permute-done.12.refs_2_.refs_24_
  37.9 1.6 %collective-permute-start.14 = (bf16[2,128,128]{2,1,0:T(8,128)(2,1)S(1)}, bf16[2,128,128]{2,1,0:T(8,128)(2,1)S(1)}, u32[]{:S(2)}, u32[]{:S(2)}) collective-permute-start(bf16[2,128,128]{2,1,0:T(8,128)(2,1)S(1)} %get-tuple-element.110.refs_2_), channel_id=1, source_target_pairs={{0,8},{4,12},{8,0},{12,4},{16,24},{20,28},{24,16},{28,20},{1,9},{5... | collective-permute-start | bytes 196616 | tf_op jit(solution)/shard_map/ppermute | solution.py:288
  39.5 0.0 collective-permute-done.13.refs_3_.refs_25_
  39.5 1.4 %collective-permute-start.16 = (bf16[2,128,128]{2,1,0:T(8,128)(2,1)S(1)}, bf16[2,128,128]{2,1,0:T(8,128)(2,1)S(1)}, u32[]{:S(2)}, u32[]{:S(2)}) collective-permute-start(bf16[2,128,128]{2,1,0:T(8,128)(2,1)S(1)} %get-tuple-element.132), channel_id=1, source_target_pairs={{0,16},{4,20},{8,24},{12,28},{16,0},{20,4},{24,8},{28,12},{1,17},{... | collective-permute-start | bytes 196616 | tf_op jit(solution)/shard_map/ppermute | solution.py:288
  41.0 1.3 %collective-permute-done.14.refs_3_.refs_25_ = bf16[2,128,128]{2,1,0:T(8,128)(2,1)S(1)} collective-permute-done((bf16[2,128,128]{2,1,0:T(8,128)(2,1)S(1)}, bf16[2,128,128]{2,1,0:T(8,128)(2,1)S(1)}, u32[]{:S(2)}, u32[]{:S(2)}) %collective-permute-start.14) | collective-permute-done | bytes 65568 | tf_op jit(solution)/shard_map/ppermute | solution.py:288
  42.2 1.6 %collective-permute-start.17 = (bf16[2,128,128]{2,1,0:T(8,128)(2,1)S(1)}, bf16[2,128,128]{2,1,0:T(8,128)(2,1)S(1)}, u32[]{:S(2)}, u32[]{:S(2)}) collective-permute-start(bf16[2,128,128]{2,1,0:T(8,128)(2,1)S(1)} %get-tuple-element.141), channel_id=1, source_target_pairs={{0,16},{4,20},{8,24},{12,28},{16,0},{20,4},{24,8},{28,12},{1,17},{... | collective-permute-start | bytes 196616 | tf_op jit(solution)/shard_map/ppermute | solution.py:288
  43.9 0.0 collective-permute-done.15.refs_23_
  43.9 3.2 %finish.3 = (f32[8,128]{1,0:T(8,128)S(1)}, bf16[1024,1024]{1,0:T(8,128)(2,1)}, bf16[1024,1024]{1,0:T(8,128)(2,1)}, bf16[1024,1024]{1,0:T(8,128)(2,1)}) custom-call(f32[8,128]{1,0:T(8,128)S(1)} %get-tuple-element.111.refs_0_, bf16[1024,1024]{1,0:T(8,128)(2,1)S(1)} %copy-done.1, bf16[1024,1024]{1,0:T(8,128)(2,1)S(1)} %copy-done.2, ...), custom_call_target="tpu_custom_call", output_to_operand_aliasing={{0}: (0, {})} | custom-call | flops 10000000000 | bytes 100000000 | tf_op jit(solution)/shard_map/finish/pallas_call | solution.py:82
  47.1 0.0 collective-permute-done.16.refs_26_
  47.1 1.9 %finish.4 = (f32[8,128]{1,0:T(8,128)S(1)}, bf16[1024,1024]{1,0:T(8,128)(2,1)}, bf16[1024,1024]{1,0:T(8,128)(2,1)}, bf16[1024,1024]{1,0:T(8,128)(2,1)}) custom-call(f32[8,128]{1,0:T(8,128)S(1)} %get-tuple-element.124.refs_0_, bf16[1024,1024]{1,0:T(8,128)(2,1)} %get-tuple-element.125.refs_1_, ...), custom_call_target="tpu_custom_call", output_to_operand_aliasing={{0}: (0, {}), {1}: (1, {}), {2}: (2, {}), {3}: (3, {})} | custom-call | flops 10000000000 | bytes 100000000 | tf_op jit(solution)/shard_map/finish/pallas_call | solution.py:82
  49.0 0.0 collective-permute-done.17.refs_26_
  49.0 1.9 %finish.5 = (f32[8,128]{1,0:T(8,128)S(1)}, bf16[1024,1024]{1,0:T(8,128)(2,1)}, bf16[1024,1024]{1,0:T(8,128)(2,1)}, bf16[1024,1024]{1,0:T(8,128)(2,1)}) custom-call(f32[8,128]{1,0:T(8,128)S(1)} %get-tuple-element.133.refs_0_, bf16[1024,1024]{1,0:T(8,128)(2,1)} %get-tuple-element.134.refs_1_, ...), custom_call_target="tpu_custom_call", output_to_operand_aliasing={{0}: (0, {}), {1}: (1, {}), {2}: (2, {}), {3}: (3, {})} | custom-call | flops 10000000000 | bytes 100000000 | tf_op jit(solution)/shard_map/finish/pallas_call | solution.py:82
  (5 shorter events, 0.1 us)
Async XLA Ops:
  0.6 4.6 %copy-start.1 = (bf16[1024,1024]{1,0:T(8,128)(2,1)S(1)}, bf16[1024,1024]{1,0:T(8,128)(2,1)}, u32[]{:S(2)}) copy-start(bf16[1024,1024]{1,0:T(8,128)(2,1)} %refs_4_.3) | copy-start | bytes 6291460
  0.7 4.6 %copy-start.2 = (bf16[1024,1024]{1,0:T(8,128)(2,1)S(1)}, bf16[1024,1024]{1,0:T(8,128)(2,1)}, u32[]{:S(2)}) copy-start(bf16[1024,1024]{1,0:T(8,128)(2,1)} %refs_5_.3) | copy-start | bytes 6291460
  2.0 17.5 %collective-permute-start.2 = (bf16[256,512]{1,0:T(8,128)(2,1)S(1)}, bf16[256,512]{1,0:T(8,128)(2,1)S(1)}, u32[]{:S(2)}, u32[]{:S(2)}) collective-permute-start(bf16[256,512]{1,0:T(8,128)(2,1)S(1)} %get-tuple-element.83), channel_id=1, source_target_pairs={{0,2},{1,3},{2,0},{3,1},{4,6},{5,7},{6,4},{7,5},{8,10},{9,11},{10,... | collective-permute-start | bytes 786440 | tf_op jit(solution)/shard_map/ppermute | solution.py:333
  5.1 14.5 %collective-permute-start.3 = (bf16[256,512]{1,0:T(8,128)(2,1)S(1)}, bf16[256,512]{1,0:T(8,128)(2,1)S(1)}, u32[]{:S(2)}, u32[]{:S(2)}) collective-permute-start(bf16[256,512]{1,0:T(8,128)(2,1)S(1)} %get-tuple-element.84), channel_id=1, source_target_pairs={{0,3},{1,2},{2,1},{3,0},{4,7},{5,6},{6,5},{7,4},{8,11},{9,10},{10,... | collective-permute-start | bytes 786440 | tf_op jit(solution)/shard_map/ppermute | solution.py:333
  5.1 3.3 %collective-permute-start = (bf16[256,1024]{1,0:T(8,128)(2,1)S(1)}, bf16[256,1024]{1,0:T(8,128)(2,1)S(1)}, u32[]{:S(2)}, u32[]{:S(2)}) collective-permute-start(bf16[256,1024]{1,0:T(8,128)(2,1)S(1)} %get-tuple-element.76), channel_id=1, source_target_pairs={{0,1},{1,0},{2,3},{3,2},{4,5},{5,4},{6,7},{7,6},{8,9},{9,8},{10,11... | collective-permute-start | bytes 1572872 | tf_op jit(solution)/shard_map/ppermute | solution.py:333
  6.4 8.6 %collective-permute-start.1 = (bf16[8,128,128]{2,1,0:T(8,128)(2,1)S(1)}, bf16[8,128,128]{2,1,0:T(8,128)(2,1)S(1)}, u32[]{:S(2)}, u32[]{:S(2)}) collective-permute-start(bf16[8,128,128]{2,1,0:T(8,128)(2,1)S(1)} %get-tuple-element.80.refs_4_), channel_id=1, source_target_pairs={{0,4},{4,0},{8,12},{12,8},{16,20},{20,16},{24,28},{28,24},{1,5},{5... | collective-permute-start | bytes 786440 | tf_op jit(solution)/shard_map/ppermute | solution.py:288
  8.3 3.0 %copy-start = (bf16[1024,1024]{1,0:T(8,128)(2,1)S(1)}, bf16[1024,1024]{1,0:T(8,128)(2,1)}, u32[]{:S(2)}) copy-start(bf16[1024,1024]{1,0:T(8,128)(2,1)} %refs_1_.22) | copy-start | bytes 6291460
  9.7 17.4 %collective-permute-start.6 = (bf16[256,256]{1,0:T(8,128)(2,1)S(1)}, bf16[256,256]{1,0:T(8,128)(2,1)S(1)}, u32[]{:S(2)}, u32[]{:S(2)}) collective-permute-start(bf16[256,256]{1,0:T(8,128)(2,1)S(1)} %get-tuple-element.93), channel_id=1, source_target_pairs={{0,2},{1,3},{2,0},{3,1},{4,6},{5,7},{6,4},{7,5},{8,10},{9,11},{10,... | collective-permute-start | bytes 393224 | tf_op jit(solution)/shard_map/ppermute | solution.py:333
  11.3 15.8 %collective-permute-start.7 = (bf16[256,256]{1,0:T(8,128)(2,1)S(1)}, bf16[256,256]{1,0:T(8,128)(2,1)S(1)}, u32[]{:S(2)}, u32[]{:S(2)}) collective-permute-start(bf16[256,256]{1,0:T(8,128)(2,1)S(1)} %get-tuple-element.94), channel_id=1, source_target_pairs={{0,3},{1,2},{2,1},{3,0},{4,7},{5,6},{6,5},{7,4},{8,11},{9,10},{10,... | collective-permute-start | bytes 393224 | tf_op jit(solution)/shard_map/ppermute | solution.py:333
  15.5 11.0 %collective-permute-start.4 = (bf16[8,128,128]{2,1,0:T(8,128)(2,1)S(1)}, bf16[8,128,128]{2,1,0:T(8,128)(2,1)S(1)}, u32[]{:S(2)}, u32[]{:S(2)}) collective-permute-start(bf16[8,128,128]{2,1,0:T(8,128)(2,1)S(1)} %get-tuple-element.90.refs_1_), channel_id=1, source_target_pairs={{0,8},{4,12},{8,0},{12,4},{16,24},{20,28},{24,16},{28,20},{1,9},{5... | collective-permute-start | bytes 786440 | tf_op jit(solution)/shard_map/ppermute | solution.py:288
  19.9 10.3 %collective-permute-start.8 = (bf16[256,256]{1,0:T(8,128)(2,1)S(1)}, bf16[256,256]{1,0:T(8,128)(2,1)S(1)}, u32[]{:S(2)}, u32[]{:S(2)}) collective-permute-start(bf16[256,256]{1,0:T(8,128)(2,1)S(1)} %get-tuple-element.97), channel_id=1, source_target_pairs={{0,2},{1,3},{2,0},{3,1},{4,6},{5,7},{6,4},{7,5},{8,10},{9,11},{10,... | collective-permute-start | bytes 393224 | tf_op jit(solution)/shard_map/ppermute | solution.py:333
  21.5 5.0 %collective-permute-start.5 = (bf16[4,128,128]{2,1,0:T(8,128)(2,1)S(1)}, bf16[4,128,128]{2,1,0:T(8,128)(2,1)S(1)}, u32[]{:S(2)}, u32[]{:S(2)}) collective-permute-start(bf16[4,128,128]{2,1,0:T(8,128)(2,1)S(1)} %get-tuple-element.91.refs_3_), channel_id=1, source_target_pairs={{0,4},{4,0},{8,12},{12,8},{16,20},{20,16},{24,28},{28,24},{1,5},{5... | collective-permute-start | bytes 393224 | tf_op jit(solution)/shard_map/ppermute | solution.py:288
  26.5 4.8 %collective-permute-start.9 = (bf16[256,256]{1,0:T(8,128)(2,1)S(1)}, bf16[256,256]{1,0:T(8,128)(2,1)S(1)}, u32[]{:S(2)}, u32[]{:S(2)}) collective-permute-start(bf16[256,256]{1,0:T(8,128)(2,1)S(1)} %get-tuple-element.98), channel_id=1, source_target_pairs={{0,3},{1,2},{2,1},{3,0},{4,7},{5,6},{6,5},{7,4},{8,11},{9,10},{10,... | collective-permute-start | bytes 393224 | tf_op jit(solution)/shard_map/ppermute | solution.py:333
  26.6 7.1 %collective-permute-start.11 = (bf16[4,128,128]{2,1,0:T(8,128)(2,1)S(1)}, bf16[4,128,128]{2,1,0:T(8,128)(2,1)S(1)}, u32[]{:S(2)}, u32[]{:S(2)}) collective-permute-start(bf16[4,128,128]{2,1,0:T(8,128)(2,1)S(1)} %get-tuple-element.103.refs_2_), channel_id=1, source_target_pairs={{0,8},{4,12},{8,0},{12,4},{16,24},{20,28},{24,16},{28,20},{1,9},{5... | collective-permute-start | bytes 393224 | tf_op jit(solution)/shard_map/ppermute | solution.py:288
  27.4 5.8 %collective-permute-start.10 = (bf16[2,128,128]{2,1,0:T(8,128)(2,1)S(1)}, bf16[2,128,128]{2,1,0:T(8,128)(2,1)S(1)}, u32[]{:S(2)}, u32[]{:S(2)}) collective-permute-start(bf16[2,128,128]{2,1,0:T(8,128)(2,1)S(1)} %get-tuple-element.100.refs_1_), channel_id=1, source_target_pairs={{0,4},{4,0},{8,12},{12,8},{16,20},{20,16},{24,28},{28,24},{1,5},{5... | collective-permute-start | bytes 196616 | tf_op jit(solution)/shard_map/ppermute | solution.py:288
  31.6 6.2 %collective-permute-start.12 = (bf16[2,128,128]{2,1,0:T(8,128)(2,1)S(1)}, bf16[2,128,128]{2,1,0:T(8,128)(2,1)S(1)}, u32[]{:S(2)}, u32[]{:S(2)}) collective-permute-start(bf16[2,128,128]{2,1,0:T(8,128)(2,1)S(1)} %get-tuple-element.106.refs_1_), channel_id=1, source_target_pairs={{0,4},{4,0},{8,12},{12,8},{16,20},{20,16},{24,28},{28,24},{1,5},{5... | collective-permute-start | bytes 196616 | tf_op jit(solution)/shard_map/ppermute | solution.py:288
  33.2 6.3 %collective-permute-start.13 = (bf16[2,128,128]{2,1,0:T(8,128)(2,1)S(1)}, bf16[2,128,128]{2,1,0:T(8,128)(2,1)S(1)}, u32[]{:S(2)}, u32[]{:S(2)}) collective-permute-start(bf16[2,128,128]{2,1,0:T(8,128)(2,1)S(1)} %get-tuple-element.108.refs_2_), channel_id=1, source_target_pairs={{0,8},{4,12},{8,0},{12,4},{16,24},{20,28},{24,16},{28,20},{1,9},{5... | collective-permute-start | bytes 196616 | tf_op jit(solution)/shard_map/ppermute | solution.py:288
  33.9 9.9 %collective-permute-start.15 = (bf16[4,128,128]{2,1,0:T(8,128)(2,1)S(1)}, bf16[4,128,128]{2,1,0:T(8,128)(2,1)S(1)}, u32[]{:S(2)}, u32[]{:S(2)}) collective-permute-start(bf16[4,128,128]{2,1,0:T(8,128)(2,1)S(1)} %get-tuple-element.123), channel_id=1, source_target_pairs={{0,16},{4,20},{8,24},{12,28},{16,0},{20,4},{24,8},{28,12},{1,17},{... | collective-permute-start | bytes 393224 | tf_op jit(solution)/shard_map/ppermute | solution.py:288
  37.9 4.3 %collective-permute-start.14 = (bf16[2,128,128]{2,1,0:T(8,128)(2,1)S(1)}, bf16[2,128,128]{2,1,0:T(8,128)(2,1)S(1)}, u32[]{:S(2)}, u32[]{:S(2)}) collective-permute-start(bf16[2,128,128]{2,1,0:T(8,128)(2,1)S(1)} %get-tuple-element.110.refs_2_), channel_id=1, source_target_pairs={{0,8},{4,12},{8,0},{12,4},{16,24},{20,28},{24,16},{28,20},{1,9},{5... | collective-permute-start | bytes 196616 | tf_op jit(solution)/shard_map/ppermute | solution.py:288
  39.5 7.6 %collective-permute-start.16 = (bf16[2,128,128]{2,1,0:T(8,128)(2,1)S(1)}, bf16[2,128,128]{2,1,0:T(8,128)(2,1)S(1)}, u32[]{:S(2)}, u32[]{:S(2)}) collective-permute-start(bf16[2,128,128]{2,1,0:T(8,128)(2,1)S(1)} %get-tuple-element.132), channel_id=1, source_target_pairs={{0,16},{4,20},{8,24},{12,28},{16,0},{20,4},{24,8},{28,12},{1,17},{... | collective-permute-start | bytes 196616 | tf_op jit(solution)/shard_map/ppermute | solution.py:288
  42.2 6.8 %collective-permute-start.17 = (bf16[2,128,128]{2,1,0:T(8,128)(2,1)S(1)}, bf16[2,128,128]{2,1,0:T(8,128)(2,1)S(1)}, u32[]{:S(2)}, u32[]{:S(2)}) collective-permute-start(bf16[2,128,128]{2,1,0:T(8,128)(2,1)S(1)} %get-tuple-element.141), channel_id=1, source_target_pairs={{0,16},{4,20},{8,24},{12,28},{16,0},{20,4},{24,8},{28,12},{1,17},{... | collective-permute-start | bytes 196616 | tf_op jit(solution)/shard_map/ppermute | solution.py:288

commit v4 on v3

--- a/solution.py
+++ b/solution.py
@@ -10,7 +10,11 @@
 
 HEAD_DIM = 128
 SPLITS = (4, 2, 2)
-ORDER = "S0 I0 K A0 S1 I1 S2 A1 L0 I2 A2 L1 L2 F0 F1 F2"
+ORDER = (
+    ("S", 0), ("N", 0), ("K", 0), ("A", 0), ("S", 1), ("I", 0),
+    ("S", 2), ("A", 1), ("L", 0), ("I", 1), ("A", 2), ("I", 2),
+    ("L", 1), ("L", 2), ("F", 0), ("F", 1), ("F", 2),
+)
 COST = (10**10, 10**8)
 F32 = jnp.float32
 BF16 = jnp.bfloat16
@@ -38,8 +42,8 @@
 
 
 class Chain:
-    def __init__(self, token, head_size, seq_size):
-        self.token = token
+    def __init__(self, token, head_size, seq_size, factor):
+        self.token, self.factor = token, factor
         self.head_size, self.seq_bits = head_size, seq_size.bit_length() - 1
         self.waits = []
         self.jobs = []
@@ -56,6 +60,7 @@
         jobs, self.waits, self.jobs = self.jobs, [], []
         skip, count = len(extra), len(operands)
         through, self.through = self.through, []
+        results = len(jobs) + len(out_shape)
         pairs = [array for sums in jobs for array in (sums.window, sums.parts[-1])]
         operands, in_specs = [*operands, *pairs], [*in_specs, *[VMEM] * len(pairs)]
         out_shape = [*[bf16(*sums.window.shape) for sums in jobs], *out_shape]
@@ -72,7 +77,7 @@
             outs = refs[skip + len(operands) + 1 :]
             for n in range(len(jobs)):
                 outs[n][...] = pair_refs[2 * n][...] + pair_refs[2 * n + 1][...]
-            kernel((place, bits), *ins, *outs[len(jobs) : len(outs) - len(through)])
+            kernel((place, bits), *ins, *outs[len(jobs) : results], *outs[results + len(through) :])
 
         aliases = {0: 0}
         for n in range(len(through)):
@@ -138,7 +143,7 @@
             for c in range(chunks):
                 at = slice(c * chunk, (c + 1) * chunk)
                 local_ref[c, h] = run.astype(BF16)
-                run = run + dot(v_ref[at, head_cols(h)], k_ref[at, head_cols(h)], TN)
+                run = run + chain.factor * dot(v_ref[at, head_cols(h)], k_ref[at, head_cols(h)], TN)
             total_ref[h] = run.astype(BF16)
 
     return chain(
@@ -154,15 +159,16 @@
         g_refs, outs = refs[:count], refs[count:]
         row = lax.broadcasted_iota(jnp.int32, (chunk, chunk), 0)
         col = lax.broadcasted_iota(jnp.int32, (chunk, chunk), 1)
-        upper, lower = row <= col, row >= col
+        upper = jnp.where(row <= col, chain.factor, 0.0)
+        lower = jnp.where(row >= col, chain.factor, 0.0)
         for n, piece in enumerate(pieces):
             rows = rows_of(here, piece, chunk)
             for h in range(heads):
                 cols, own = head_cols(head0 + h), head_cols(h)
                 q, k, v, g = q_ref[rows, cols], k_ref[rows, cols], v_ref[rows, cols], g_refs[n][:, own]
-                fwd = jnp.where(upper, dot(k, q, NT), 0.0).astype(BF16)
-                back = jnp.where(upper, dot(v, g, NT), 0.0).astype(BF16)
-                turned = jnp.where(lower, dot(g, v, NT), 0.0).astype(BF16)
+                fwd = (upper * dot(k, q, NT)).astype(BF16)
+                back = (upper * dot(v, g, NT)).astype(BF16)
+                turned = (lower * dot(g, v, NT)).astype(BF16)
                 outs[0][n, :, own] = dot(turned, k, NN).astype(BF16)
                 outs[1][n, :, own] = dot(back, q, NN).astype(BF16)
                 outs[2][n, :, own] = dot(fwd, g, NN).astype(BF16)
@@ -181,7 +187,7 @@
             cols = head_cols(h)
             for n, g_ref in enumerate((g0, g1)):
                 q = q_ref[rows_of(here, n, chunk), cols]
-                state_ref[n, h] = dot(q, g_ref[:, cols], TN).astype(BF16)
+                state_ref[n, h] = (chain.factor * dot(q, g_ref[:, cols], TN)).astype(BF16)
 
     return chain(
         "near_states", kernel, [query_rows, *grads], [VMEM] * 3,
@@ -193,8 +199,8 @@
     def kernel(here, q_ref, g0, g1, near_ref, state_ref, total_ref):
         for h in range(heads):
             cols, own = head_cols(head0 + h), head_cols(h)
-            a = dot(q_ref[rows_of(here, 2, chunk), cols], g0[:, own], TN)
-            b = dot(q_ref[rows_of(here, 3, chunk), cols], g1[:, own], TN)
+            a = chain.factor * dot(q_ref[rows_of(here, 2, chunk), cols], g0[:, own], TN)
+            b = chain.factor * dot(q_ref[rows_of(here, 3, chunk), cols], g1[:, own], TN)
             state_ref[0, h] = a.astype(BF16)
             state_ref[1, h] = b.astype(BF16)
             total = a + b + near_ref[0, head0 + h].astype(F32) + near_ref[1, head0 + h].astype(F32)
@@ -206,7 +212,7 @@
     )
 
 
-def finish(chain, key_rows, value_rows, grads, parts, states, local, kv_in, grad_in, last, head0, heads, chunk, factor, outs):
+def finish(chain, key_rows, value_rows, grads, parts, states, local, kv_in, grad_in, last, head0, heads, chunk, outs):
     rows, feat = key_rows.shape
     rounds = len(kv_in)
 
@@ -227,40 +233,52 @@
         (local_ref,) = take(1)
         kv_refs, grad_refs = take(rounds), take(rounds)
         (last_ref,) = take(1)
-        dq_ref, dk_ref, dv_ref = refs
-        h = pl.program_id(0)
-        bit = here[1][rounds].astype(F32)
-        got = last_ref[h].astype(F32)
-        prefix, suffix = got * bit, got * (1.0 - bit)
-        for r in range(rounds):
-            bit = here[1][r].astype(F32)
-            prefix = prefix + kv_refs[r][head0 + h].astype(F32) * bit
-            suffix = suffix + grad_refs[r][h].astype(F32) * (1.0 - bit)
-        wide = pl.ds(pl.multiple_of((head0 + h) * HEAD_DIM, HEAD_DIM), HEAD_DIM)
-        narrow = pl.ds(pl.multiple_of(h * HEAD_DIM, HEAD_DIM), HEAD_DIM)
-        state = [
-            state_refs[0][0, head0 + h], state_refs[0][1, head0 + h],
-            state_refs[1][0, h], state_refs[1][1, h],
-        ]
-        state = [s.astype(F32) for s in state]
+        out_refs, refs = refs[:3], refs[3:]
+        low_ref, stage_refs, sems = refs[0], refs[1:4], refs[4]
+        for h in range(heads):
+            bit = here[1][rounds].astype(F32)
+            got = last_ref[h].astype(F32)
+            prefix, suffix = got * bit, got * (1.0 - bit)
+            for r in range(rounds):
+                bit = here[1][r].astype(F32)
+                prefix = prefix + kv_refs[r][head0 + h].astype(F32) * bit
+                suffix = suffix + grad_refs[r][h].astype(F32) * (1.0 - bit)
+            state = [
+                state_refs[0][0, head0 + h], state_refs[0][1, head0 + h],
+                state_refs[1][0, h], state_refs[1][1, h],
+            ]
+            state = [s.astype(F32) for s in state]
+            halves = [state[0] + state[1], state[2] + state[3]]
+            for piece in range(4):
+                place = here[0][piece]
+                half = piece // 2
+                far = (here[0][2 - 2 * half] > here[0][2 * half]).astype(F32)
+                near = (here[0][piece ^ 1] > place).astype(F32)
+                low_ref[0, piece, h] = (prefix + local_ref[place, head0 + h].astype(F32)).astype(BF16)
+                low_ref[1, piece, h] = (suffix + far * halves[1 - half] + near * state[piece ^ 1]).astype(BF16)
+        copies = []
+        target = slice(head0 * HEAD_DIM, (head0 + heads) * HEAD_DIM)
         for piece in range(4):
-            place = here[0][piece]
             at = rows_of(here, piece, chunk)
             part, slot = part_refs[min(piece, 2)], max(piece - 2, 0)
-            cols = wide if piece < 2 else narrow
-            before_low = (prefix + local_ref[place, head0 + h].astype(F32)).astype(BF16)
-            after = suffix
-            for other in range(4):
-                if other != piece:
-                    later = (here[0][other] > place).astype(F32)
-                    after = after + later * state[other]
-            after_low = after.astype(BF16)
-            out = part[0][slot, :, cols].astype(F32) + dot(g_refs[piece][:, cols], before_low, NN)
-            dq_ref[at, :] = (factor * out).astype(BF16)
-            out = part[1][slot, :, cols].astype(F32) + dot(v_ref[at, wide], after_low, NT)
-            dk_ref[at, :] = (factor * out).astype(BF16)
-            out = part[2][slot, :, cols].astype(F32) + dot(k_ref[at, wide], after_low, NN)
-            dv_ref[at, :] = (factor * out).astype(BF16)
+            for h in range(heads):
+                wide, narrow = head_cols(head0 + h), head_cols(h)
+                cols = wide if piece < 2 else narrow
+                before_low, after_low = low_ref[0, piece, h], low_ref[1, piece, h]
+                out = part[0][slot, :, cols].astype(F32) + dot(g_refs[piece][:, cols], before_low, NN)
+                stage_refs[0][piece, :, narrow] = out.astype(BF16)
+                out = part[1][slot, :, cols].astype(F32) + dot(v_ref[at, wide], after_low, NT)
+                stage_refs[1][piece, :, narrow] = out.astype(BF16)
+                out = part[2][slot, :, cols].astype(F32) + dot(k_ref[at, wide], after_low, NN)
+                stage_refs[2][piece, :, narrow] = out.astype(BF16)
+            for n in range(3):
+                copy = pltpu.make_async_copy(
+                    stage_refs[n].at[piece], out_refs[n].at[at, target], sems.at[n, piece]
+                )
+                copy.start()
+                copies.append(copy)
+        for copy in copies:
+            copy.wait()
 
     operands = [key_rows, value_rows, *grads]
     for p in parts:
@@ -274,8 +292,12 @@
         alias = {0: 0, 1: 1, 2: 2}
     return chain(
         "finish", kernel, operands, in_specs, [pltpu.HBM((rows, feat), BF16)] * 3,
-        [pl.BlockSpec((rows, HEAD_DIM), lambda i: (0, i + head0))] * 3,
-        grid=(heads,), alias=alias,
+        [ANY] * 3, alias=alias,
+        scratch=[
+            pltpu.VMEM((2, 4, heads, HEAD_DIM, HEAD_DIM), BF16),
+            *[pltpu.VMEM((4, chunk, heads * HEAD_DIM), BF16)] * 3,
+            pltpu.SemaphoreType.DMA((3, 4)),
+        ],
     )
 
 
@@ -325,7 +347,7 @@
     chunk = rows // head_size
     head_count = feat // HEAD_DIM
     factor = 1.0 / math.sqrt(HEAD_DIM * rows * seq_size)
-    chain = Chain(jnp.zeros((8, 128), F32), head_size, seq_size)
+    chain = Chain(jnp.zeros((8, 128), F32), head_size, seq_size, factor)
     arrays = (query_rows, key_rows, value_rows)
     firsts = [sum(SPLITS[:s]) for s in range(len(SPLITS))]
 
@@ -349,18 +371,12 @@
     own_part = intra(chain, [0], arrays, [own_grad], 0, head_count, chunk)
     chain.add(kv_sums)
     near_state = near_states(chain, query_rows, (own_grad, near_grad), chunk)
-    near_part = intra(chain, [1], arrays, [near_grad], 0, head_count, chunk)
-
     far_state, far_part, sums, lasts, outs = [], [], [], [], None
 
     def states(s):
         f, n = firsts[s], SPLITS[s]
-        if s + 2 < len(SPLITS):
-            chain.through = later[2 * s : 2 * s + 2]
         far, total = far_states(chain, query_rows, crossing[s], near_state, f, n, chunk)
         far_state.append(far)
-        if s + 2 < len(SPLITS):
-            crossing.append([send(chain.passed[0], 2), send(chain.passed[1], 3)])
         sums.append(SeqSums(total, "seq", seq_size))
         sums[s].go()
 
@@ -369,18 +385,22 @@
             chain.add(one)
             add_only(chain)
 
-    for step in ORDER.split():
-        s = int(step[1:] or 0)
-        if step[0] == "K":
+    for step, s in ORDER:
+        if step == "K":
             chain.add(kv_sums)
-        elif step[0] == "S":
+        elif step == "N":
+            chain.through = later
+            near_part = intra(chain, [1], arrays, [near_grad], 0, head_count, chunk)
+            for n in range(0, len(later), 2):
+                crossing.append([send(chain.passed[n], 2), send(chain.passed[n + 1], 3)])
+        elif step == "S":
             states(s)
-        elif step[0] == "I":
+        elif step == "I":
             far_part.append(intra(chain, [2, 3], arrays, crossing[s], firsts[s], SPLITS[s], chunk))
-        elif step[0] == "A":
+        elif step == "A":
             chain.add(sums[s])
             add_only(chain)
-        elif step[0] == "L":
+        elif step == "L":
             settle(sums[s])
             while not kv_sums.closed:
                 chain.add(kv_sums)
@@ -390,7 +410,7 @@
             outs = finish(
                 chain, key_rows, value_rows, (own_grad, near_grad, *crossing[s]),
                 (own_part, near_part, far_part[s]), (near_state, far_state[s]),
-                local, kv_sums.parts, sums[s].parts, lasts[s], firsts[s], SPLITS[s], chunk, factor, outs,
+                local, kv_sums.parts, sums[s].parts, lasts[s], firsts[s], SPLITS[s], chunk, outs,
             )
     return tuple(outs)
 

time: 51 us -> 50.8 us (level)
  waiting for transfers between devices: 5.02 us -> 5.86 us
  starting transfers between devices: 23.2 us -> 22.5 us
  Pallas kernels: 21.8 us -> 21.2 us
    ppermute x11, starting transfers between devices: 16.8 us -> 14.9 us  [swap(): lax.ppermute(block, self.axis, [(i, i ^ self.step) for i in range(self.si...]
    ppermute x11, waiting for transfers between devices: 3.86 us -> 5.73 us  [swap(): lax.ppermute(block, self.axis, [(i, i ^ self.step) for i in range(self.si...]
    ppermute x7, starting transfers between devices: 6.41 us -> 7.67 us  [send(): lax.ppermute(block, 'head', [(i, i ^ mask) for i in range(head_size)])]
    ppermute x7, waiting for transfers between devices: 1.17 us -> 0.13 us  [send(): lax.ppermute(block, 'head', [(i, i ^ mask) for i in range(head_size)])]
    pallas_call x21, Pallas kernels: 21.8 us -> 21.2 us  [__call__(): pl.pallas_call(run, grid=grid, in_specs=[ANY] * skip + list(in_specs), ou...]
  transfers between devices with their start and end apart: 18 -> 18, of which waited for: 4 -> 5; matrix products, arithmetic and copies ran while one was open for 0% -> 0% of each run, Pallas kernels for 37% -> 36%
where the time goes in v4:
time: 50.8 us; the launch traced here: 50.6 us
  starting transfers between devices  22.5 us (44%)
  Pallas kernels  21.2 us (42%)
  waiting for transfers between devices  5.86 us (12%)
  between operations  1 us (2%)
    pallas_call x21, Pallas kernels, __call__(): pl.pallas_call(run, grid=grid, in_specs=[ANY] * skip + list(in_specs), ou...  21.2 us
    ppermute x11, starting transfers between devices, swap(): lax.ppermute(block, self.axis, [(i, i ^ self.step) for i in range(self.si...  14.9 us
    ppermute x7, starting transfers between devices, send(): lax.ppermute(block, 'head', [(i, i ^ mask) for i in range(head_size)])  7.67 us
    ppermute x11, waiting for transfers between devices, swap(): lax.ppermute(block, self.axis, [(i, i ^ self.step) for i in range(self.si...  5.73 us
  transfers between devices with their start and end apart: 18, of which 5 were waited for; matrix products, arithmetic and copies ran while one was open for 0% of the time, Pallas kernels for 36%

profile of v4, /device:TPU:0, one launch (start us, length us, event | category | flops | bytes accessed | tf_op | source)
XLA Modules:
  0.0 50.6 jit_solution(4757501929376205177)
XLA Ops:
  0.6 0.0 copy-start.1
  0.7 0.0 copy-start.2
  0.7 1.4 %cut.2 = (f32[8,128]{1,0:T(8,128)S(1)}, bf16[256,1024]{1,0:T(8,128)(2,1)S(1)}, bf16[256,512]{1,0:T(8,128)(2,1)S(1)}, bf16[256,512]{1,0:T(8,128)(2,1)S(1)}) custom-call(f32[8,128]{1,0:T(8,128)S(1)} %broadcast_in_dim.3.refs_0_, bf16[256,4096]{1,0:T(8,128)(2,1)} %refs_2_.9), custom_call_target="tpu_custom_call", output_to_operand_aliasing={{0}: (0, {})} | custom-call | flops 10000000000 | bytes 100000000 | tf_op jit(solution)/shard_map/cut/pallas_call | solution.py:87
  2.0 3.0 %collective-permute-start.2 = (bf16[256,512]{1,0:T(8,128)(2,1)S(1)}, bf16[256,512]{1,0:T(8,128)(2,1)S(1)}, u32[]{:S(2)}, u32[]{:S(2)}) collective-permute-start(bf16[256,512]{1,0:T(8,128)(2,1)S(1)} %get-tuple-element.82), channel_id=1, source_target_pairs={{0,2},{1,3},{2,0},{3,1},{4,6},{5,7},{6,4},{7,5},{8,10},{9,11},{10,... | collective-permute-start | bytes 786440 | tf_op jit(solution)/shard_map/ppermute | solution.py:355
  5.1 0.0 collective-permute-start.3
  5.1 0.2 collective-permute-start
  5.3 0.0 copy-done.1
  5.3 0.0 copy-done.2
  5.3 1.1 %kv_states.1 = (f32[8,128]{1,0:T(8,128)S(1)}, bf16[4,8,128,128]{3,2,1,0:T(8,128)(2,1)S(1)}, bf16[8,128,128]{2,1,0:T(8,128)(2,1)S(1)}) custom-call(f32[8,128]{1,0:T(8,128)S(1)} %get-tuple-element.74.refs_0_, bf16[1024,1024]{1,0:T(8,128)(2,1)S(1)} %copy-done.1, bf16[1024,1024]{1,0:T(8,128)(2,1)S(1)} %copy-done.2), custom_call_target="tpu_custom_call", output_to_operand_aliasing={{0}: (0, {})} | custom-call | flops 10000000000 | bytes 100000000 | tf_op jit(solution)/shard_map/kv_states/pallas_call | solution.py:87
  6.4 2.0 %collective-permute-start.1 = (bf16[8,128,128]{2,1,0:T(8,128)(2,1)S(1)}, bf16[8,128,128]{2,1,0:T(8,128)(2,1)S(1)}, u32[]{:S(2)}, u32[]{:S(2)}) collective-permute-start(bf16[8,128,128]{2,1,0:T(8,128)(2,1)S(1)} %get-tuple-element.80.refs_4_), channel_id=1, source_target_pairs={{0,4},{4,0},{8,12},{12,8},{16,20},{20,16},{24,28},{28,24},{1,5},{5... | collective-permute-start | bytes 786440 | tf_op jit(solution)/shard_map/ppermute | solution.py:310
  8.4 0.0 collective-permute-done.refs_1_.refs_3_.refs_4_.refs_7_
  8.4 0.0 copy-start
  8.4 1.4 %cut.3 = (f32[8,128]{1,0:T(8,128)S(1)}, bf16[256,1024]{1,0:T(8,128)(2,1)S(1)}, bf16[256,256]{1,0:T(8,128)(2,1)S(1)}, bf16[256,256]{1,0:T(8,128)(2,1)S(1)}, bf16[...) custom-call(f32[8,128]{1,0:T(8,128)S(1)} %get-tuple-element.75.refs_0_, ...), custom_call_target="tpu_custom_call", output_to_operand_aliasing={{0}: (0, {})} | custom-call | flops 10000000000 | bytes 100000000 | tf_op jit(solution)/shard_map/cut/pallas_call | solution.py:87
  9.7 1.6 %collective-permute-start.6 = (bf16[256,256]{1,0:T(8,128)(2,1)S(1)}, bf16[256,256]{1,0:T(8,128)(2,1)S(1)}, u32[]{:S(2)}, u32[]{:S(2)}) collective-permute-start(bf16[256,256]{1,0:T(8,128)(2,1)S(1)} %get-tuple-element.92), channel_id=1, source_target_pairs={{0,2},{1,3},{2,0},{3,1},{4,6},{5,7},{6,4},{7,5},{8,10},{9,11},{10,... | collective-permute-start | bytes 393224 | tf_op jit(solution)/shard_map/ppermute | solution.py:355
  11.3 0.0 collective-permute-start.7
  11.3 0.0 copy-done
  11.3 2.3 %intra.5 = (f32[8,128]{1,0:T(8,128)S(1)}, bf16[1,256,1024]{2,1,0:T(8,128)(2,1)S(1)}, bf16[1,256,1024]{2,1,0:T(8,128)(2,1)S(1)}, bf16[1,256,1024]{2,1,0:T(8,128)(2,1)S(1)}) custom-call(f32[8,128]{1,0:T(8,128)S(1)} %get-tuple-element.77.refs_0_, bf16[1024,1024]{1,0:T(8,128)(2,1)S(1)} %copy-done, ...), custom_call_target="tpu_custom_call", output_to_operand_aliasing={{0}: (0, {})} | custom-call | flops 10000000000 | bytes 100000000 | tf_op jit(solution)/shard_map/intra/pallas_call | solution.py:87
  13.6 1.4 %collective-permute-done.1.refs_5_.refs_19_.refs_22_ = bf16[8,128,128]{2,1,0:T(8,128)(2,1)S(1)} collective-permute-done((bf16[8,128,128]{2,1,0:T(8,128)(2,1)S(1)}, bf16[8,128,128]{2,1,0:T(8,128)(2,1)S(1)}, u32[]{:S(2)}, u32[]{:S(2)}) %collective-permute-start.1) | collective-permute-done | bytes 262176 | tf_op jit(solution)/shard_map/ppermute | solution.py:310
  15.0 0.6 %near_states.1 = (f32[8,128]{1,0:T(8,128)S(1)}, bf16[8,128,128]{2,1,0:T(8,128)(2,1)S(1)}, bf16[2,8,128,128]{3,2,1,0:T(8,128)(2,1)S(1)}) custom-call(f32[8,128]{1,0:T(8,128)S(1)} %get-tuple-element.79.refs_0_, bf16[1024,1024]{1,0:T(8,128)(2,1)S(1)} %copy-done, ...), custom_call_target="tpu_custom_call", output_to_operand_aliasing={{0}: (0, {})} | custom-call | flops 10000000000 | bytes 100000000 | tf_op jit(solution)/shard_map/near_states/pallas_call | solution.py:87
  15.5 1.8 %collective-permute-start.4 = (bf16[8,128,128]{2,1,0:T(8,128)(2,1)S(1)}, bf16[8,128,128]{2,1,0:T(8,128)(2,1)S(1)}, u32[]{:S(2)}, u32[]{:S(2)}) collective-permute-start(bf16[8,128,128]{2,1,0:T(8,128)(2,1)S(1)} %get-tuple-element.89.refs_1_), channel_id=1, source_target_pairs={{0,8},{4,12},{8,0},{12,4},{16,24},{20,28},{24,16},{28,20},{1,9},{5... | collective-permute-start | bytes 786440 | tf_op jit(solution)/shard_map/ppermute | solution.py:310
  17.3 0.0 collective-permute-done.2.refs_2_.refs_4_.refs_5_
  17.3 0.1 collective-permute-done.3.refs_3_.refs_5_.refs_6_
  17.4 0.4 far_states.3
  17.8 1.6 %collective-permute-start.5 = (bf16[4,128,128]{2,1,0:T(8,128)(2,1)S(1)}, bf16[4,128,128]{2,1,0:T(8,128)(2,1)S(1)}, u32[]{:S(2)}, u32[]{:S(2)}) collective-permute-start(bf16[4,128,128]{2,1,0:T(8,128)(2,1)S(1)} %get-tuple-element.90.refs_3_), channel_id=1, source_target_pairs={{0,4},{4,0},{8,12},{12,8},{16,20},{20,16},{24,28},{28,24},{1,5},{5... | collective-permute-start | bytes 393224 | tf_op jit(solution)/shard_map/ppermute | solution.py:310
  19.3 2.3 %intra.6 = (f32[8,128]{1,0:T(8,128)S(1)}, bf16[1,256,1024]{2,1,0:T(8,128)(2,1)S(1)}, bf16[1,256,1024]{2,1,0:T(8,128)(2,1)S(1)}, bf16[1,256,1024]{2,1,0:T(8,128)(...) custom-call(f32[8,128]{1,0:T(8,128)S(1)} %get-tuple-element.85.refs_, ...), custom_call_target="tpu_custom_call", output_to_operand_aliasing={{0}: (0, {}), {5}: (6, {}), {4}: (5, {})} | custom-call | flops 10000000000 | bytes 100000000 | tf_op jit(solution)/shard_map/intra/pallas_call | solution.py:87
  21.6 1.5 %collective-permute-start.8 = (bf16[256,256]{1,0:T(8,128)(2,1)S(1)}, bf16[256,256]{1,0:T(8,128)(2,1)S(1)}, u32[]{:S(2)}, u32[]{:S(2)}) collective-permute-start(bf16[256,256]{1,0:T(8,128)(2,1)S(1)} %get-tuple-element.96), channel_id=1, source_target_pairs={{0,2},{1,3},{2,0},{3,1},{4,6},{5,7},{6,4},{7,5},{8,10},{9,11},{10,... | collective-permute-start | bytes 393224 | tf_op jit(solution)/shard_map/ppermute | solution.py:355
  23.1 0.7 %collective-permute-done.5.refs_4_.refs_21_ = bf16[4,128,128]{2,1,0:T(8,128)(2,1)S(1)} collective-permute-done((bf16[4,128,128]{2,1,0:T(8,128)(2,1)S(1)}, bf16[4,128,128]{2,1,0:T(8,128)(2,1)S(1)}, u32[]{:S(2)}, u32[]{:S(2)}) %collective-permute-start.5) | collective-permute-done | bytes 131104 | tf_op jit(solution)/shard_map/ppermute | solution.py:310
  23.8 1.4 %collective-permute-start.9 = (bf16[256,256]{1,0:T(8,128)(2,1)S(1)}, bf16[256,256]{1,0:T(8,128)(2,1)S(1)}, u32[]{:S(2)}, u32[]{:S(2)}) collective-permute-start(bf16[256,256]{1,0:T(8,128)(2,1)S(1)} %get-tuple-element.97), channel_id=1, source_target_pairs={{0,3},{1,2},{2,1},{3,0},{4,7},{5,6},{6,5},{7,4},{8,11},{9,10},{10,... | collective-permute-start | bytes 393224 | tf_op jit(solution)/shard_map/ppermute | solution.py:355
  25.2 0.0 collective-permute-done.4.refs_2_.refs_20_.refs_23_
  25.2 0.1 add.3
  25.3 0.8 %collective-permute-start.11 = (bf16[4,128,128]{2,1,0:T(8,128)(2,1)S(1)}, bf16[4,128,128]{2,1,0:T(8,128)(2,1)S(1)}, u32[]{:S(2)}, u32[]{:S(2)}) collective-permute-start(bf16[4,128,128]{2,1,0:T(8,128)(2,1)S(1)} %get-tuple-element.102.refs_2_), channel_id=1, source_target_pairs={{0,8},{4,12},{8,0},{12,4},{16,24},{20,28},{24,16},{28,20},{1,9},{5... | collective-permute-start | bytes 393224 | tf_op jit(solution)/shard_map/ppermute | solution.py:310
  26.1 0.0 collective-permute-done.6.refs_2_.refs_4_.refs_8_
  26.1 0.0 collective-permute-done.7.refs_3_.refs_5_.refs_9_
  26.1 0.3 far_states.4
  26.4 1.5 %collective-permute-start.10 = (bf16[2,128,128]{2,1,0:T(8,128)(2,1)S(1)}, bf16[2,128,128]{2,1,0:T(8,128)(2,1)S(1)}, u32[]{:S(2)}, u32[]{:S(2)}) collective-permute-start(bf16[2,128,128]{2,1,0:T(8,128)(2,1)S(1)} %get-tuple-element.99.refs_1_), channel_id=1, source_target_pairs={{0,4},{4,0},{8,12},{12,8},{16,20},{20,16},{24,28},{28,24},{1,5},{5... | collective-permute-start | bytes 196616 | tf_op jit(solution)/shard_map/ppermute | solution.py:310
  27.9 2.3 %intra.7 = (f32[8,128]{1,0:T(8,128)S(1)}, bf16[2,256,512]{2,1,0:T(8,128)(2,1)S(1)}, bf16[2,256,512]{2,1,0:T(8,128)(2,1)S(1)}, bf16[2,256,512]{2,1,0:T(8,128)(2,1)S(1)}) custom-call(f32[8,128]{1,0:T(8,128)S(1)} %get-tuple-element.94.refs_0_, bf16[1024,1024]{1,0:T(8,128)(2,1)S(1)} %copy-done, ...), custom_call_target="tpu_custom_call", output_to_operand_aliasing={{0}: (0, {})} | custom-call | flops 10000000000 | bytes 100000000 | tf_op jit(solution)/shard_map/intra/pallas_call | solution.py:87
  30.2 0.0 collective-permute-done.8.refs_2_.refs_4_.refs_8_
  30.2 0.0 collective-permute-done.9.refs_3_.refs_5_.refs_9_
  30.2 0.3 far_states.5
  30.5 1.1 %collective-permute-start.12 = (bf16[2,128,128]{2,1,0:T(8,128)(2,1)S(1)}, bf16[2,128,128]{2,1,0:T(8,128)(2,1)S(1)}, u32[]{:S(2)}, u32[]{:S(2)}) collective-permute-start(bf16[2,128,128]{2,1,0:T(8,128)(2,1)S(1)} %get-tuple-element.105.refs_1_), channel_id=1, source_target_pairs={{0,4},{4,0},{8,12},{12,8},{16,20},{20,16},{24,28},{28,24},{1,5},{5... | collective-permute-start | bytes 196616 | tf_op jit(solution)/shard_map/ppermute | solution.py:310
  31.6 0.0 collective-permute-done.10.refs_2_.refs_24_
  31.6 1.6 %collective-permute-start.13 = (bf16[2,128,128]{2,1,0:T(8,128)(2,1)S(1)}, bf16[2,128,128]{2,1,0:T(8,128)(2,1)S(1)}, u32[]{:S(2)}, u32[]{:S(2)}) collective-permute-start(bf16[2,128,128]{2,1,0:T(8,128)(2,1)S(1)} %get-tuple-element.108.refs_2_), channel_id=1, source_target_pairs={{0,8},{4,12},{8,0},{12,4},{16,24},{20,28},{24,16},{28,20},{1,9},{5... | collective-permute-start | bytes 196616 | tf_op jit(solution)/shard_map/ppermute | solution.py:310
  33.2 0.0 collective-permute-done.11.refs_3_.refs_22_
  33.2 0.2 last_round.3
  33.4 2.7 %collective-permute-start.15 = (bf16[4,128,128]{2,1,0:T(8,128)(2,1)S(1)}, bf16[4,128,128]{2,1,0:T(8,128)(2,1)S(1)}, u32[]{:S(2)}, u32[]{:S(2)}) collective-permute-start(bf16[4,128,128]{2,1,0:T(8,128)(2,1)S(1)} %get-tuple-element.123), channel_id=1, source_target_pairs={{0,16},{4,20},{8,24},{12,28},{16,0},{20,4},{24,8},{28,12},{1,17},{... | collective-permute-start | bytes 393224 | tf_op jit(solution)/shard_map/ppermute | solution.py:310
  36.1 1.2 %intra.8 = (f32[8,128]{1,0:T(8,128)S(1)}, bf16[2,256,256]{2,1,0:T(8,128)(2,1)S(1)}, bf16[2,256,256]{2,1,0:T(8,128)(2,1)S(1)}, bf16[2,256,256]{2,1,0:T(8,128)(2,1)S(1)}) custom-call(f32[8,128]{1,0:T(8,128)S(1)} %get-tuple-element.103.refs_0_, bf16[1024,1024]{1,0:T(8,128)(2,1)S(1)} %copy-done, ...), custom_call_target="tpu_custom_call", output_to_operand_aliasing={{0}: (0, {})} | custom-call | flops 10000000000 | bytes 100000000 | tf_op jit(solution)/shard_map/intra/pallas_call | solution.py:87
  37.3 0.0 collective-permute-done.12.refs_2_.refs_24_
  37.4 0.5 %collective-permute-start.14 = (bf16[2,128,128]{2,1,0:T(8,128)(2,1)S(1)}, bf16[2,128,128]{2,1,0:T(8,128)(2,1)S(1)}, u32[]{:S(2)}, u32[]{:S(2)}) collective-permute-start(bf16[2,128,128]{2,1,0:T(8,128)(2,1)S(1)} %get-tuple-element.110.refs_2_), channel_id=1, source_target_pairs={{0,8},{4,12},{8,0},{12,4},{16,24},{20,28},{24,16},{28,20},{1,9},{5... | collective-permute-start | bytes 196616 | tf_op jit(solution)/shard_map/ppermute | solution.py:310
  37.9 1.2 %intra.9 = (f32[8,128]{1,0:T(8,128)S(1)}, bf16[2,256,256]{2,1,0:T(8,128)(2,1)S(1)}, bf16[2,256,256]{2,1,0:T(8,128)(2,1)S(1)}, bf16[2,256,256]{2,1,0:T(8,128)(2,1)S(1)}) custom-call(f32[8,128]{1,0:T(8,128)S(1)} %get-tuple-element.106.refs_0_, bf16[1024,1024]{1,0:T(8,128)(2,1)S(1)} %copy-done, ...), custom_call_target="tpu_custom_call", output_to_operand_aliasing={{0}: (0, {})} | custom-call | flops 10000000000 | bytes 100000000 | tf_op jit(solution)/shard_map/intra/pallas_call | solution.py:87
  39.1 0.0 collective-permute-done.13.refs_3_.refs_25_
  39.2 1.3 %collective-permute-start.16 = (bf16[2,128,128]{2,1,0:T(8,128)(2,1)S(1)}, bf16[2,128,128]{2,1,0:T(8,128)(2,1)S(1)}, u32[]{:S(2)}, u32[]{:S(2)}) collective-permute-start(bf16[2,128,128]{2,1,0:T(8,128)(2,1)S(1)} %get-tuple-element.132), channel_id=1, source_target_pairs={{0,16},{4,20},{8,24},{12,28},{16,0},{20,4},{24,8},{28,12},{1,17},{... | collective-permute-start | bytes 196616 | tf_op jit(solution)/shard_map/ppermute | solution.py:310
  40.4 3.0 %collective-permute-done.14.refs_3_.refs_25_ = bf16[2,128,128]{2,1,0:T(8,128)(2,1)S(1)} collective-permute-done((bf16[2,128,128]{2,1,0:T(8,128)(2,1)S(1)}, bf16[2,128,128]{2,1,0:T(8,128)(2,1)S(1)}, u32[]{:S(2)}, u32[]{:S(2)}) %collective-permute-start.14) | collective-permute-done | bytes 65568 | tf_op jit(solution)/shard_map/ppermute | solution.py:310
  43.5 0.0 collective-permute-start.17
  43.5 0.0 collective-permute-done.15.refs_23_
  43.5 2.7 %finish.3 = (f32[8,128]{1,0:T(8,128)S(1)}, bf16[1024,1024]{1,0:T(8,128)(2,1)}, bf16[1024,1024]{1,0:T(8,128)(2,1)}, bf16[1024,1024]{1,0:T(8,128)(2,1)}) custom-call(f32[8,128]{1,0:T(8,128)S(1)} %get-tuple-element.111.refs_0_, bf16[1024,1024]{1,0:T(8,128)(2,1)S(1)} %copy-done.1, bf16[1024,1024]{1,0:T(8,128)(2,1)S(1)} %copy-done.2, ...), custom_call_target="tpu_custom_call", output_to_operand_aliasing={{0}: (0, {})} | custom-call | flops 10000000000 | bytes 100000000 | tf_op jit(solution)/shard_map/finish/pallas_call | solution.py:87
  46.2 0.0 collective-permute-done.16.refs_26_
  46.2 1.8 %finish.4 = (f32[8,128]{1,0:T(8,128)S(1)}, bf16[1024,1024]{1,0:T(8,128)(2,1)}, bf16[1024,1024]{1,0:T(8,128)(2,1)}, bf16[1024,1024]{1,0:T(8,128)(2,1)}) custom-call(f32[8,128]{1,0:T(8,128)S(1)} %get-tuple-element.124.refs_0_, bf16[1024,1024]{1,0:T(8,128)(2,1)} %get-tuple-element.125.refs_1_, ...), custom_call_target="tpu_custom_call", output_to_operand_aliasing={{0}: (0, {}), {1}: (1, {}), {2}: (2, {}), {3}: (3, {})} | custom-call | flops 10000000000 | bytes 100000000 | tf_op jit(solution)/shard_map/finish/pallas_call | solution.py:87
  48.0 0.6 %collective-permute-done.17.refs_26_ = bf16[2,128,128]{2,1,0:T(8,128)(2,1)S(1)} collective-permute-done((bf16[2,128,128]{2,1,0:T(8,128)(2,1)S(1)}, bf16[2,128,128]{2,1,0:T(8,128)(2,1)S(1)}, u32[]{:S(2)}, u32[]{:S(2)}) %collective-permute-start.17) | collective-permute-done | bytes 65568 | tf_op jit(solution)/shard_map/ppermute | solution.py:310
  48.6 1.8 %finish.5 = (f32[8,128]{1,0:T(8,128)S(1)}, bf16[1024,1024]{1,0:T(8,128)(2,1)}, bf16[1024,1024]{1,0:T(8,128)(2,1)}, bf16[1024,1024]{1,0:T(8,128)(2,1)}) custom-call(f32[8,128]{1,0:T(8,128)S(1)} %get-tuple-element.133.refs_0_, bf16[1024,1024]{1,0:T(8,128)(2,1)} %get-tuple-element.134.refs_1_, ...), custom_call_target="tpu_custom_call", output_to_operand_aliasing={{0}: (0, {}), {1}: (1, {}), {2}: (2, {}), {3}: (3, {})} | custom-call | flops 10000000000 | bytes 100000000 | tf_op jit(solution)/shard_map/finish/pallas_call | solution.py:87
  (5 shorter events, 0.1 us)
Async XLA Ops:
  0.6 4.6 %copy-start.1 = (bf16[1024,1024]{1,0:T(8,128)(2,1)S(1)}, bf16[1024,1024]{1,0:T(8,128)(2,1)}, u32[]{:S(2)}) copy-start(bf16[1024,1024]{1,0:T(8,128)(2,1)} %refs_4_.3) | copy-start | bytes 6291460
  0.7 4.6 %copy-start.2 = (bf16[1024,1024]{1,0:T(8,128)(2,1)S(1)}, bf16[1024,1024]{1,0:T(8,128)(2,1)}, u32[]{:S(2)}) copy-start(bf16[1024,1024]{1,0:T(8,128)(2,1)} %refs_5_.3) | copy-start | bytes 6291460
  2.0 15.2 %collective-permute-start.2 = (bf16[256,512]{1,0:T(8,128)(2,1)S(1)}, bf16[256,512]{1,0:T(8,128)(2,1)S(1)}, u32[]{:S(2)}, u32[]{:S(2)}) collective-permute-start(bf16[256,512]{1,0:T(8,128)(2,1)S(1)} %get-tuple-element.82), channel_id=1, source_target_pairs={{0,2},{1,3},{2,0},{3,1},{4,6},{5,7},{6,4},{7,5},{8,10},{9,11},{10,... | collective-permute-start | bytes 786440 | tf_op jit(solution)/shard_map/ppermute | solution.py:355
  5.1 12.3 %collective-permute-start.3 = (bf16[256,512]{1,0:T(8,128)(2,1)S(1)}, bf16[256,512]{1,0:T(8,128)(2,1)S(1)}, u32[]{:S(2)}, u32[]{:S(2)}) collective-permute-start(bf16[256,512]{1,0:T(8,128)(2,1)S(1)} %get-tuple-element.83), channel_id=1, source_target_pairs={{0,3},{1,2},{2,1},{3,0},{4,7},{5,6},{6,5},{7,4},{8,11},{9,10},{10,... | collective-permute-start | bytes 786440 | tf_op jit(solution)/shard_map/ppermute | solution.py:355
  5.1 3.3 %collective-permute-start = (bf16[256,1024]{1,0:T(8,128)(2,1)S(1)}, bf16[256,1024]{1,0:T(8,128)(2,1)S(1)}, u32[]{:S(2)}, u32[]{:S(2)}) collective-permute-start(bf16[256,1024]{1,0:T(8,128)(2,1)S(1)} %get-tuple-element.76), channel_id=1, source_target_pairs={{0,1},{1,0},{2,3},{3,2},{4,5},{5,4},{6,7},{7,6},{8,9},{9,8},{10,11... | collective-permute-start | bytes 1572872 | tf_op jit(solution)/shard_map/ppermute | solution.py:355
  6.4 8.6 %collective-permute-start.1 = (bf16[8,128,128]{2,1,0:T(8,128)(2,1)S(1)}, bf16[8,128,128]{2,1,0:T(8,128)(2,1)S(1)}, u32[]{:S(2)}, u32[]{:S(2)}) collective-permute-start(bf16[8,128,128]{2,1,0:T(8,128)(2,1)S(1)} %get-tuple-element.80.refs_4_), channel_id=1, source_target_pairs={{0,4},{4,0},{8,12},{12,8},{16,20},{20,16},{24,28},{28,24},{1,5},{5... | collective-permute-start | bytes 786440 | tf_op jit(solution)/shard_map/ppermute | solution.py:310
  8.4 3.0 %copy-start = (bf16[1024,1024]{1,0:T(8,128)(2,1)S(1)}, bf16[1024,1024]{1,0:T(8,128)(2,1)}, u32[]{:S(2)}) copy-start(bf16[1024,1024]{1,0:T(8,128)(2,1)} %refs_1_.22) | copy-start | bytes 6291460
  9.7 16.3 %collective-permute-start.6 = (bf16[256,256]{1,0:T(8,128)(2,1)S(1)}, bf16[256,256]{1,0:T(8,128)(2,1)S(1)}, u32[]{:S(2)}, u32[]{:S(2)}) collective-permute-start(bf16[256,256]{1,0:T(8,128)(2,1)S(1)} %get-tuple-element.92), channel_id=1, source_target_pairs={{0,2},{1,3},{2,0},{3,1},{4,6},{5,7},{6,4},{7,5},{8,10},{9,11},{10,... | collective-permute-start | bytes 393224 | tf_op jit(solution)/shard_map/ppermute | solution.py:355
  11.3 14.7 %collective-permute-start.7 = (bf16[256,256]{1,0:T(8,128)(2,1)S(1)}, bf16[256,256]{1,0:T(8,128)(2,1)S(1)}, u32[]{:S(2)}, u32[]{:S(2)}) collective-permute-start(bf16[256,256]{1,0:T(8,128)(2,1)S(1)} %get-tuple-element.93), channel_id=1, source_target_pairs={{0,3},{1,2},{2,1},{3,0},{4,7},{5,6},{6,5},{7,4},{8,11},{9,10},{10,... | collective-permute-start | bytes 393224 | tf_op jit(solution)/shard_map/ppermute | solution.py:355
  15.5 9.6 %collective-permute-start.4 = (bf16[8,128,128]{2,1,0:T(8,128)(2,1)S(1)}, bf16[8,128,128]{2,1,0:T(8,128)(2,1)S(1)}, u32[]{:S(2)}, u32[]{:S(2)}) collective-permute-start(bf16[8,128,128]{2,1,0:T(8,128)(2,1)S(1)} %get-tuple-element.89.refs_1_), channel_id=1, source_target_pairs={{0,8},{4,12},{8,0},{12,4},{16,24},{20,28},{24,16},{28,20},{1,9},{5... | collective-permute-start | bytes 786440 | tf_op jit(solution)/shard_map/ppermute | solution.py:310
  17.8 6.0 %collective-permute-start.5 = (bf16[4,128,128]{2,1,0:T(8,128)(2,1)S(1)}, bf16[4,128,128]{2,1,0:T(8,128)(2,1)S(1)}, u32[]{:S(2)}, u32[]{:S(2)}) collective-permute-start(bf16[4,128,128]{2,1,0:T(8,128)(2,1)S(1)} %get-tuple-element.90.refs_3_), channel_id=1, source_target_pairs={{0,4},{4,0},{8,12},{12,8},{16,20},{20,16},{24,28},{28,24},{1,5},{5... | collective-permute-start | bytes 393224 | tf_op jit(solution)/shard_map/ppermute | solution.py:310
  21.6 8.6 %collective-permute-start.8 = (bf16[256,256]{1,0:T(8,128)(2,1)S(1)}, bf16[256,256]{1,0:T(8,128)(2,1)S(1)}, u32[]{:S(2)}, u32[]{:S(2)}) collective-permute-start(bf16[256,256]{1,0:T(8,128)(2,1)S(1)} %get-tuple-element.96), channel_id=1, source_target_pairs={{0,2},{1,3},{2,0},{3,1},{4,6},{5,7},{6,4},{7,5},{8,10},{9,11},{10,... | collective-permute-start | bytes 393224 | tf_op jit(solution)/shard_map/ppermute | solution.py:355
  23.8 6.4 %collective-permute-start.9 = (bf16[256,256]{1,0:T(8,128)(2,1)S(1)}, bf16[256,256]{1,0:T(8,128)(2,1)S(1)}, u32[]{:S(2)}, u32[]{:S(2)}) collective-permute-start(bf16[256,256]{1,0:T(8,128)(2,1)S(1)} %get-tuple-element.97), channel_id=1, source_target_pairs={{0,3},{1,2},{2,1},{3,0},{4,7},{5,6},{6,5},{7,4},{8,11},{9,10},{10,... | collective-permute-start | bytes 393224 | tf_op jit(solution)/shard_map/ppermute | solution.py:355
  25.3 8.0 %collective-permute-start.11 = (bf16[4,128,128]{2,1,0:T(8,128)(2,1)S(1)}, bf16[4,128,128]{2,1,0:T(8,128)(2,1)S(1)}, u32[]{:S(2)}, u32[]{:S(2)}) collective-permute-start(bf16[4,128,128]{2,1,0:T(8,128)(2,1)S(1)} %get-tuple-element.102.refs_2_), channel_id=1, source_target_pairs={{0,8},{4,12},{8,0},{12,4},{16,24},{20,28},{24,16},{28,20},{1,9},{5... | collective-permute-start | bytes 393224 | tf_op jit(solution)/shard_map/ppermute | solution.py:310
  26.4 5.2 %collective-permute-start.10 = (bf16[2,128,128]{2,1,0:T(8,128)(2,1)S(1)}, bf16[2,128,128]{2,1,0:T(8,128)(2,1)S(1)}, u32[]{:S(2)}, u32[]{:S(2)}) collective-permute-start(bf16[2,128,128]{2,1,0:T(8,128)(2,1)S(1)} %get-tuple-element.99.refs_1_), channel_id=1, source_target_pairs={{0,4},{4,0},{8,12},{12,8},{16,20},{20,16},{24,28},{28,24},{1,5},{5... | collective-permute-start | bytes 196616 | tf_op jit(solution)/shard_map/ppermute | solution.py:310
  30.5 6.9 %collective-permute-start.12 = (bf16[2,128,128]{2,1,0:T(8,128)(2,1)S(1)}, bf16[2,128,128]{2,1,0:T(8,128)(2,1)S(1)}, u32[]{:S(2)}, u32[]{:S(2)}) collective-permute-start(bf16[2,128,128]{2,1,0:T(8,128)(2,1)S(1)} %get-tuple-element.105.refs_1_), channel_id=1, source_target_pairs={{0,4},{4,0},{8,12},{12,8},{16,20},{20,16},{24,28},{28,24},{1,5},{5... | collective-permute-start | bytes 196616 | tf_op jit(solution)/shard_map/ppermute | solution.py:310
  31.6 7.5 %collective-permute-start.13 = (bf16[2,128,128]{2,1,0:T(8,128)(2,1)S(1)}, bf16[2,128,128]{2,1,0:T(8,128)(2,1)S(1)}, u32[]{:S(2)}, u32[]{:S(2)}) collective-permute-start(bf16[2,128,128]{2,1,0:T(8,128)(2,1)S(1)} %get-tuple-element.108.refs_2_), channel_id=1, source_target_pairs={{0,8},{4,12},{8,0},{12,4},{16,24},{20,28},{24,16},{28,20},{1,9},{5... | collective-permute-start | bytes 196616 | tf_op jit(solution)/shard_map/ppermute | solution.py:310
  33.4 10.0 %collective-permute-start.15 = (bf16[4,128,128]{2,1,0:T(8,128)(2,1)S(1)}, bf16[4,128,128]{2,1,0:T(8,128)(2,1)S(1)}, u32[]{:S(2)}, u32[]{:S(2)}) collective-permute-start(bf16[4,128,128]{2,1,0:T(8,128)(2,1)S(1)} %get-tuple-element.123), channel_id=1, source_target_pairs={{0,16},{4,20},{8,24},{12,28},{16,0},{20,4},{24,8},{28,12},{1,17},{... | collective-permute-start | bytes 393224 | tf_op jit(solution)/shard_map/ppermute | solution.py:310
  37.4 6.1 %collective-permute-start.14 = (bf16[2,128,128]{2,1,0:T(8,128)(2,1)S(1)}, bf16[2,128,128]{2,1,0:T(8,128)(2,1)S(1)}, u32[]{:S(2)}, u32[]{:S(2)}) collective-permute-start(bf16[2,128,128]{2,1,0:T(8,128)(2,1)S(1)} %get-tuple-element.110.refs_2_), channel_id=1, source_target_pairs={{0,8},{4,12},{8,0},{12,4},{16,24},{20,28},{24,16},{28,20},{1,9},{5... | collective-permute-start | bytes 196616 | tf_op jit(solution)/shard_map/ppermute | solution.py:310
  39.2 7.0 %collective-permute-start.16 = (bf16[2,128,128]{2,1,0:T(8,128)(2,1)S(1)}, bf16[2,128,128]{2,1,0:T(8,128)(2,1)S(1)}, u32[]{:S(2)}, u32[]{:S(2)}) collective-permute-start(bf16[2,128,128]{2,1,0:T(8,128)(2,1)S(1)} %get-tuple-element.132), channel_id=1, source_target_pairs={{0,16},{4,20},{8,24},{12,28},{16,0},{20,4},{24,8},{28,12},{1,17},{... | collective-permute-start | bytes 196616 | tf_op jit(solution)/shard_map/ppermute | solution.py:310
  43.5 5.2 %collective-permute-start.17 = (bf16[2,128,128]{2,1,0:T(8,128)(2,1)S(1)}, bf16[2,128,128]{2,1,0:T(8,128)(2,1)S(1)}, u32[]{:S(2)}, u32[]{:S(2)}) collective-permute-start(bf16[2,128,128]{2,1,0:T(8,128)(2,1)S(1)} %get-tuple-element.141), channel_id=1, source_target_pairs={{0,16},{4,20},{8,24},{12,28},{16,0},{20,4},{24,8},{28,12},{1,17},{... | collective-permute-start | bytes 196616 | tf_op jit(solution)/shard_map/ppermute | solution.py:310

commit v5 on v4

--- a/solution.py
+++ b/solution.py
@@ -15,7 +15,7 @@
     ("S", 2), ("A", 1), ("L", 0), ("I", 1), ("A", 2), ("I", 2),
     ("L", 1), ("L", 2), ("F", 0), ("F", 1), ("F", 2),
 )
-COST = (10**10, 10**8)
+COST = (14 * 10**9, 10**3)
 F32 = jnp.float32
 BF16 = jnp.bfloat16
 NN = (((1,), (0,)), ((), ()))

time: 50.8 us -> 51.3 us (level)
  local copies, waits for them, and re-layouts: 0.02 us -> 1.16 us
  waiting for transfers between devices: 5.86 us -> 5.1 us
    unnamed x6 -> x14, local copies, waits for them, and re-layouts: 0.02 us -> 1.16 us
    ppermute x11, waiting for transfers between devices: 5.73 us -> 5.03 us  [swap(): lax.ppermute(block, self.axis, [(i, i ^ self.step) for i in range(self.si...]
  transfers between devices with their start and end apart: 18 -> 18, of which waited for: 5 -> 4; matrix products, arithmetic and copies ran while one was open for 0% -> 0% of each run, Pallas kernels for 36% -> 35%
where the time goes in v5:
time: 51.3 us; the launch traced here: 51.1 us
  starting transfers between devices  22.6 us (44%)
  Pallas kernels  21.2 us (41%)
  waiting for transfers between devices  5.1 us (10%)
  local copies, waits for them, and re-layouts  1.16 us (2%)
  between operations  1.02 us (2%)
    pallas_call x21, Pallas kernels, __call__(): pl.pallas_call(run, grid=grid, in_specs=[ANY] * skip + list(in_specs), ou...  21.2 us
    ppermute x11, starting transfers between devices, swap(): lax.ppermute(block, self.axis, [(i, i ^ self.step) for i in range(self.si...  14.9 us
    ppermute x7, starting transfers between devices, send(): lax.ppermute(block, 'head', [(i, i ^ mask) for i in range(head_size)])  7.71 us
    ppermute x11, waiting for transfers between devices, swap(): lax.ppermute(block, self.axis, [(i, i ^ self.step) for i in range(self.si...  5.03 us
    unnamed x14, local copies, waits for them, and re-layouts  1.16 us
  transfers between devices with their start and end apart: 18, of which 4 were waited for; matrix products, arithmetic and copies ran while one was open for 0% of the time, Pallas kernels for 35%

profile of v5, /device:TPU:0, one launch (start us, length us, event | category | flops | bytes accessed | tf_op | source)
XLA Modules:
  0.0 51.1 jit_solution(6928008489997169328)
XLA Ops:
  0.6 0.0 copy-start.1
  0.7 0.0 copy-start.2
  0.7 1.4 %cut.2 = (f32[8,128]{1,0:T(8,128)S(1)}, bf16[256,1024]{1,0:T(8,128)(2,1)S(1)}, bf16[256,512]{1,0:T(8,128)(2,1)S(1)}, bf16[256,512]{1,0:T(8,128)(2,1)S(1)}) custom-call(f32[8,128]{1,0:T(8,128)S(1)} %broadcast_in_dim.3.refs_0_, bf16[256,4096]{1,0:T(8,128)(2,1)} %refs_2_.9), custom_call_target="tpu_custom_call", output_to_operand_aliasing={{0}: (0, {})} | custom-call | flops 14000000000 | bytes 1000 | tf_op jit(solution)/shard_map/cut/pallas_call | solution.py:87
  2.0 3.0 %collective-permute-start.2 = (bf16[256,512]{1,0:T(8,128)(2,1)S(1)}, bf16[256,512]{1,0:T(8,128)(2,1)S(1)}, u32[]{:S(2)}, u32[]{:S(2)}) collective-permute-start(bf16[256,512]{1,0:T(8,128)(2,1)S(1)} %get-tuple-element.82), channel_id=1, source_target_pairs={{0,2},{1,3},{2,0},{3,1},{4,6},{5,7},{6,4},{7,5},{8,10},{9,11},{10,... | collective-permute-start | bytes 786440 | tf_op jit(solution)/shard_map/ppermute | solution.py:355
  5.1 0.0 collective-permute-start.3
  5.1 0.2 collective-permute-start
  5.3 0.0 copy-done.1
  5.3 0.0 copy-done.2
  5.3 1.1 %kv_states.1 = (f32[8,128]{1,0:T(8,128)S(1)}, bf16[4,8,128,128]{3,2,1,0:T(8,128)(2,1)S(1)}, bf16[8,128,128]{2,1,0:T(8,128)(2,1)S(1)}) custom-call(f32[8,128]{1,0:T(8,128)S(1)} %get-tuple-element.74.refs_0_, bf16[1024,1024]{1,0:T(8,128)(2,1)S(1)} %copy-done.1, bf16[1024,1024]{1,0:T(8,128)(2,1)S(1)} %copy-done.2), custom_call_target="tpu_custom_call", output_to_operand_aliasing={{0}: (0, {})} | custom-call | flops 14000000000 | bytes 1000 | tf_op jit(solution)/shard_map/kv_states/pallas_call | solution.py:87
  6.4 2.0 %collective-permute-start.1 = (bf16[8,128,128]{2,1,0:T(8,128)(2,1)S(1)}, bf16[8,128,128]{2,1,0:T(8,128)(2,1)S(1)}, u32[]{:S(2)}, u32[]{:S(2)}) collective-permute-start(bf16[8,128,128]{2,1,0:T(8,128)(2,1)S(1)} %get-tuple-element.80.refs_4_), channel_id=1, source_target_pairs={{0,4},{4,0},{8,12},{12,8},{16,20},{20,16},{24,28},{28,24},{1,5},{5... | collective-permute-start | bytes 786440 | tf_op jit(solution)/shard_map/ppermute | solution.py:310
  8.3 0.0 collective-permute-done.refs_1_.refs_3_.refs_4_.refs_7_
  8.4 1.4 %cut.3 = (f32[8,128]{1,0:T(8,128)S(1)}, bf16[256,1024]{1,0:T(8,128)(2,1)S(1)}, bf16[256,256]{1,0:T(8,128)(2,1)S(1)}, bf16[256,256]{1,0:T(8,128)(2,1)S(1)}, bf16[...) custom-call(f32[8,128]{1,0:T(8,128)S(1)} %get-tuple-element.75.refs_0_, ...), custom_call_target="tpu_custom_call", output_to_operand_aliasing={{0}: (0, {})} | custom-call | flops 14000000000 | bytes 1000 | tf_op jit(solution)/shard_map/cut/pallas_call | solution.py:87
  9.7 0.0 copy-start.5
  9.8 1.6 %collective-permute-start.6 = (bf16[256,256]{1,0:T(8,128)(2,1)S(1)}, bf16[256,256]{1,0:T(8,128)(2,1)S(1)}, u32[]{:S(2)}, u32[]{:S(2)}) collective-permute-start(bf16[256,256]{1,0:T(8,128)(2,1)S(1)} %get-tuple-element.92), channel_id=1, source_target_pairs={{0,2},{1,3},{2,0},{3,1},{4,6},{5,7},{6,4},{7,5},{8,10},{9,11},{10,... | collective-permute-start | bytes 393224 | tf_op jit(solution)/shard_map/ppermute | solution.py:355
  11.3 0.0 collective-permute-start.7
  11.3 0.0 copy-done
  11.3 2.3 %intra.5 = (f32[8,128]{1,0:T(8,128)S(1)}, bf16[1,256,1024]{2,1,0:T(8,128)(2,1)S(1)}, bf16[1,256,1024]{2,1,0:T(8,128)(2,1)S(1)}, bf16[1,256,1024]{2,1,0:T(8,128)(2,1)S(1)}) custom-call(f32[8,128]{1,0:T(8,128)S(1)} %get-tuple-element.77.refs_0_, bf16[1024,1024]{1,0:T(8,128)(2,1)S(1)} %copy-done, ...), custom_call_target="tpu_custom_call", output_to_operand_aliasing={{0}: (0, {})} | custom-call | flops 14000000000 | bytes 1000 | tf_op jit(solution)/shard_map/intra/pallas_call | solution.py:87
  13.6 1.3 %collective-permute-done.1.refs_5_.refs_19_.refs_22_ = bf16[8,128,128]{2,1,0:T(8,128)(2,1)S(1)} collective-permute-done((bf16[8,128,128]{2,1,0:T(8,128)(2,1)S(1)}, bf16[8,128,128]{2,1,0:T(8,128)(2,1)S(1)}, u32[]{:S(2)}, u32[]{:S(2)}) %collective-permute-start.1) | collective-permute-done | bytes 262176 | tf_op jit(solution)/shard_map/ppermute | solution.py:310
  15.0 0.0 copy-start.3
  15.0 0.0 copy-done.5
  15.0 0.6 %near_states.1 = (f32[8,128]{1,0:T(8,128)S(1)}, bf16[8,128,128]{2,1,0:T(8,128)(2,1)S(1)}, bf16[2,8,128,128]{3,2,1,0:T(8,128)(2,1)S(1)}) custom-call(f32[8,128]{1,0:T(8,128)S(1)} %get-tuple-element.79.refs_0_, bf16[1024,1024]{1,0:T(8,128)(2,1)S(1)} %copy-done, ...), custom_call_target="tpu_custom_call", output_to_operand_aliasing={{0}: (0, {})} | custom-call | flops 14000000000 | bytes 1000 | tf_op jit(solution)/shard_map/near_states/pallas_call | solution.py:87
  15.5 0.1 copy-done.3
  15.7 1.7 %collective-permute-start.4 = (bf16[8,128,128]{2,1,0:T(8,128)(2,1)S(1)}, bf16[8,128,128]{2,1,0:T(8,128)(2,1)S(1)}, u32[]{:S(2)}, u32[]{:S(2)}) collective-permute-start(bf16[8,128,128]{2,1,0:T(8,128)(2,1)S(1)} %get-tuple-element.89.refs_1_), channel_id=1, source_target_pairs={{0,8},{4,12},{8,0},{12,4},{16,24},{20,28},{24,16},{28,20},{1,9},{5... | collective-permute-start | bytes 786440 | tf_op jit(solution)/shard_map/ppermute | solution.py:310
  17.4 0.0 collective-permute-done.2.refs_2_.refs_4_.refs_5_
  17.4 0.1 collective-permute-done.3.refs_3_.refs_5_.refs_6_
  17.4 0.4 far_states.3
  17.8 1.6 %collective-permute-start.5 = (bf16[4,128,128]{2,1,0:T(8,128)(2,1)S(1)}, bf16[4,128,128]{2,1,0:T(8,128)(2,1)S(1)}, u32[]{:S(2)}, u32[]{:S(2)}) collective-permute-start(bf16[4,128,128]{2,1,0:T(8,128)(2,1)S(1)} %get-tuple-element.90.refs_3_), channel_id=1, source_target_pairs={{0,4},{4,0},{8,12},{12,8},{16,20},{20,16},{24,28},{28,24},{1,5},{5... | collective-permute-start | bytes 393224 | tf_op jit(solution)/shard_map/ppermute | solution.py:310
  19.3 2.3 %intra.6 = (f32[8,128]{1,0:T(8,128)S(1)}, bf16[1,256,1024]{2,1,0:T(8,128)(2,1)S(1)}, bf16[1,256,1024]{2,1,0:T(8,128)(2,1)S(1)}, bf16[1,256,1024]{2,1,0:T(8,128)(...) custom-call(f32[8,128]{1,0:T(8,128)S(1)} %get-tuple-element.85.refs_, ...), custom_call_target="tpu_custom_call", output_to_operand_aliasing={{0}: (0, {}), {5}: (6, {}), {4}: (5, {})} | custom-call | flops 14000000000 | bytes 1000 | tf_op jit(solution)/shard_map/intra/pallas_call | solution.py:87
  21.6 1.5 %collective-permute-start.8 = (bf16[256,256]{1,0:T(8,128)(2,1)S(1)}, bf16[256,256]{1,0:T(8,128)(2,1)S(1)}, u32[]{:S(2)}, u32[]{:S(2)}) collective-permute-start(bf16[256,256]{1,0:T(8,128)(2,1)S(1)} %get-tuple-element.96), channel_id=1, source_target_pairs={{0,2},{1,3},{2,0},{3,1},{4,6},{5,7},{6,4},{7,5},{8,10},{9,11},{10,... | collective-permute-start | bytes 393224 | tf_op jit(solution)/shard_map/ppermute | solution.py:355
  23.1 0.6 %collective-permute-done.5.refs_4_.refs_21_ = bf16[4,128,128]{2,1,0:T(8,128)(2,1)S(1)} collective-permute-done((bf16[4,128,128]{2,1,0:T(8,128)(2,1)S(1)}, bf16[4,128,128]{2,1,0:T(8,128)(2,1)S(1)}, u32[]{:S(2)}, u32[]{:S(2)}) %collective-permute-start.5) | collective-permute-done | bytes 131104 | tf_op jit(solution)/shard_map/ppermute | solution.py:310
  23.8 1.4 %collective-permute-start.9 = (bf16[256,256]{1,0:T(8,128)(2,1)S(1)}, bf16[256,256]{1,0:T(8,128)(2,1)S(1)}, u32[]{:S(2)}, u32[]{:S(2)}) collective-permute-start(bf16[256,256]{1,0:T(8,128)(2,1)S(1)} %get-tuple-element.97), channel_id=1, source_target_pairs={{0,3},{1,2},{2,1},{3,0},{4,7},{5,6},{6,5},{7,4},{8,11},{9,10},{10,... | collective-permute-start | bytes 393224 | tf_op jit(solution)/shard_map/ppermute | solution.py:355
  25.1 0.0 collective-permute-done.4.refs_2_.refs_20_.refs_23_
  25.2 0.1 add.3
  25.2 0.9 %collective-permute-start.11 = (bf16[4,128,128]{2,1,0:T(8,128)(2,1)S(1)}, bf16[4,128,128]{2,1,0:T(8,128)(2,1)S(1)}, u32[]{:S(2)}, u32[]{:S(2)}) collective-permute-start(bf16[4,128,128]{2,1,0:T(8,128)(2,1)S(1)} %get-tuple-element.102.refs_2_), channel_id=1, source_target_pairs={{0,8},{4,12},{8,0},{12,4},{16,24},{20,28},{24,16},{28,20},{1,9},{5... | collective-permute-start | bytes 393224 | tf_op jit(solution)/shard_map/ppermute | solution.py:310
  26.1 0.0 collective-permute-done.6.refs_2_.refs_4_.refs_8_
  26.1 0.0 collective-permute-done.7.refs_3_.refs_5_.refs_9_
  26.1 0.3 far_states.4
  26.4 1.5 %collective-permute-start.10 = (bf16[2,128,128]{2,1,0:T(8,128)(2,1)S(1)}, bf16[2,128,128]{2,1,0:T(8,128)(2,1)S(1)}, u32[]{:S(2)}, u32[]{:S(2)}) collective-permute-start(bf16[2,128,128]{2,1,0:T(8,128)(2,1)S(1)} %get-tuple-element.99.refs_1_), channel_id=1, source_target_pairs={{0,4},{4,0},{8,12},{12,8},{16,20},{20,16},{24,28},{28,24},{1,5},{5... | collective-permute-start | bytes 196616 | tf_op jit(solution)/shard_map/ppermute | solution.py:310
  28.0 2.3 %intra.7 = (f32[8,128]{1,0:T(8,128)S(1)}, bf16[2,256,512]{2,1,0:T(8,128)(2,1)S(1)}, bf16[2,256,512]{2,1,0:T(8,128)(2,1)S(1)}, bf16[2,256,512]{2,1,0:T(8,128)(2,1)S(1)}) custom-call(f32[8,128]{1,0:T(8,128)S(1)} %get-tuple-element.94.refs_0_, bf16[1024,1024]{1,0:T(8,128)(2,1)S(1)} %copy-done, ...), custom_call_target="tpu_custom_call", output_to_operand_aliasing={{0}: (0, {})} | custom-call | flops 14000000000 | bytes 1000 | tf_op jit(solution)/shard_map/intra/pallas_call | solution.py:87
  30.2 0.0 collective-permute-done.8.refs_2_.refs_4_.refs_8_
  30.2 0.0 collective-permute-done.9.refs_3_.refs_5_.refs_9_
  30.3 0.3 far_states.5
  30.6 1.0 %collective-permute-start.12 = (bf16[2,128,128]{2,1,0:T(8,128)(2,1)S(1)}, bf16[2,128,128]{2,1,0:T(8,128)(2,1)S(1)}, u32[]{:S(2)}, u32[]{:S(2)}) collective-permute-start(bf16[2,128,128]{2,1,0:T(8,128)(2,1)S(1)} %get-tuple-element.105.refs_1_), channel_id=1, source_target_pairs={{0,4},{4,0},{8,12},{12,8},{16,20},{20,16},{24,28},{28,24},{1,5},{5... | collective-permute-start | bytes 196616 | tf_op jit(solution)/shard_map/ppermute | solution.py:310
  31.6 0.0 collective-permute-done.10.refs_2_.refs_24_
  31.6 1.6 %collective-permute-start.13 = (bf16[2,128,128]{2,1,0:T(8,128)(2,1)S(1)}, bf16[2,128,128]{2,1,0:T(8,128)(2,1)S(1)}, u32[]{:S(2)}, u32[]{:S(2)}) collective-permute-start(bf16[2,128,128]{2,1,0:T(8,128)(2,1)S(1)} %get-tuple-element.108.refs_2_), channel_id=1, source_target_pairs={{0,8},{4,12},{8,0},{12,4},{16,24},{20,28},{24,16},{28,20},{1,9},{5... | collective-permute-start | bytes 196616 | tf_op jit(solution)/shard_map/ppermute | solution.py:310
  33.2 0.0 collective-permute-done.11.refs_3_.refs_22_
  33.2 0.2 last_round.3
  33.4 2.7 %collective-permute-start.15 = (bf16[4,128,128]{2,1,0:T(8,128)(2,1)S(1)}, bf16[4,128,128]{2,1,0:T(8,128)(2,1)S(1)}, u32[]{:S(2)}, u32[]{:S(2)}) collective-permute-start(bf16[4,128,128]{2,1,0:T(8,128)(2,1)S(1)} %get-tuple-element.123), channel_id=1, source_target_pairs={{0,16},{4,20},{8,24},{12,28},{16,0},{20,4},{24,8},{28,12},{1,17},{... | collective-permute-start | bytes 393224 | tf_op jit(solution)/shard_map/ppermute | solution.py:310
  36.1 1.2 %intra.8 = (f32[8,128]{1,0:T(8,128)S(1)}, bf16[2,256,256]{2,1,0:T(8,128)(2,1)S(1)}, bf16[2,256,256]{2,1,0:T(8,128)(2,1)S(1)}, bf16[2,256,256]{2,1,0:T(8,128)(2,1)S(1)}) custom-call(f32[8,128]{1,0:T(8,128)S(1)} %get-tuple-element.103.refs_0_, bf16[1024,1024]{1,0:T(8,128)(2,1)S(1)} %copy-done, ...), custom_call_target="tpu_custom_call", output_to_operand_aliasing={{0}: (0, {})} | custom-call | flops 14000000000 | bytes 1000 | tf_op jit(solution)/shard_map/intra/pallas_call | solution.py:87
  37.3 0.0 collective-permute-done.12.refs_2_.refs_24_
  37.4 0.5 %collective-permute-start.14 = (bf16[2,128,128]{2,1,0:T(8,128)(2,1)S(1)}, bf16[2,128,128]{2,1,0:T(8,128)(2,1)S(1)}, u32[]{:S(2)}, u32[]{:S(2)}) collective-permute-start(bf16[2,128,128]{2,1,0:T(8,128)(2,1)S(1)} %get-tuple-element.110.refs_2_), channel_id=1, source_target_pairs={{0,8},{4,12},{8,0},{12,4},{16,24},{20,28},{24,16},{28,20},{1,9},{5... | collective-permute-start | bytes 196616 | tf_op jit(solution)/shard_map/ppermute | solution.py:310
  37.9 1.2 %intra.9 = (f32[8,128]{1,0:T(8,128)S(1)}, bf16[2,256,256]{2,1,0:T(8,128)(2,1)S(1)}, bf16[2,256,256]{2,1,0:T(8,128)(2,1)S(1)}, bf16[2,256,256]{2,1,0:T(8,128)(2,1)S(1)}) custom-call(f32[8,128]{1,0:T(8,128)S(1)} %get-tuple-element.106.refs_0_, bf16[1024,1024]{1,0:T(8,128)(2,1)S(1)} %copy-done, ...), custom_call_target="tpu_custom_call", output_to_operand_aliasing={{0}: (0, {})} | custom-call | flops 14000000000 | bytes 1000 | tf_op jit(solution)/shard_map/intra/pallas_call | solution.py:87
  39.1 0.0 collective-permute-done.13.refs_3_.refs_25_
  39.2 1.3 %collective-permute-start.16 = (bf16[2,128,128]{2,1,0:T(8,128)(2,1)S(1)}, bf16[2,128,128]{2,1,0:T(8,128)(2,1)S(1)}, u32[]{:S(2)}, u32[]{:S(2)}) collective-permute-start(bf16[2,128,128]{2,1,0:T(8,128)(2,1)S(1)} %get-tuple-element.132), channel_id=1, source_target_pairs={{0,16},{4,20},{8,24},{12,28},{16,0},{20,4},{24,8},{28,12},{1,17},{... | collective-permute-start | bytes 196616 | tf_op jit(solution)/shard_map/ppermute | solution.py:310
  40.4 3.0 %collective-permute-done.14.refs_3_.refs_25_ = bf16[2,128,128]{2,1,0:T(8,128)(2,1)S(1)} collective-permute-done((bf16[2,128,128]{2,1,0:T(8,128)(2,1)S(1)}, bf16[2,128,128]{2,1,0:T(8,128)(2,1)S(1)}, u32[]{:S(2)}, u32[]{:S(2)}) %collective-permute-start.14) | collective-permute-done | bytes 65568 | tf_op jit(solution)/shard_map/ppermute | solution.py:310
  43.5 0.1 collective-permute-start.17
  43.6 0.0 collective-permute-done.15.refs_23_
  43.6 0.8 %copy-done.4 = bf16[8,128,128]{2,1,0:T(8,128)(2,1)S(1)} copy-done((bf16[8,128,128]{2,1,0:T(8,128)(2,1)S(1)}, bf16[8,128,128]{2,1,0:T(8,128)(2,1)}, u32[]{:S(2)}) %copy-start.4) | copy-done | bytes 262168
  44.4 0.2 copy-done.6
  44.6 2.6 %finish.3 = (f32[8,128]{1,0:T(8,128)S(1)}, bf16[1024,1024]{1,0:T(8,128)(2,1)}, bf16[1024,1024]{1,0:T(8,128)(2,1)}, bf16[1024,1024]{1,0:T(8,128)(2,1)}) custom-call(f32[8,128]{1,0:T(8,128)S(1)} %get-tuple-element.111.refs_0_, bf16[1024,1024]{1,0:T(8,128)(2,1)S(1)} %copy-done.1, bf16[1024,1024]{1,0:T(8,128)(2,1)S(1)} %copy-done.2, ...), custom_call_target="tpu_custom_call", output_to_operand_aliasing={{0}: (0, {})} | custom-call | flops 14000000000 | bytes 1000 | tf_op jit(solution)/shard_map/finish/pallas_call | solution.py:87
  47.2 0.0 collective-permute-done.16.refs_26_
  47.3 1.8 %finish.4 = (f32[8,128]{1,0:T(8,128)S(1)}, bf16[1024,1024]{1,0:T(8,128)(2,1)}, bf16[1024,1024]{1,0:T(8,128)(2,1)}, bf16[1024,1024]{1,0:T(8,128)(2,1)}) custom-call(f32[8,128]{1,0:T(8,128)S(1)} %get-tuple-element.124.refs_0_, bf16[1024,1024]{1,0:T(8,128)(2,1)} %get-tuple-element.125.refs_1_, ...), custom_call_target="tpu_custom_call", output_to_operand_aliasing={{0}: (0, {}), {1}: (1, {}), {2}: (2, {}), {3}: (3, {})} | custom-call | flops 14000000000 | bytes 1000 | tf_op jit(solution)/shard_map/finish/pallas_call | solution.py:87
  49.1 0.0 collective-permute-done.17.refs_26_
  49.1 1.8 %finish.5 = (f32[8,128]{1,0:T(8,128)S(1)}, bf16[1024,1024]{1,0:T(8,128)(2,1)}, bf16[1024,1024]{1,0:T(8,128)(2,1)}, bf16[1024,1024]{1,0:T(8,128)(2,1)}) custom-call(f32[8,128]{1,0:T(8,128)S(1)} %get-tuple-element.133.refs_0_, bf16[1024,1024]{1,0:T(8,128)(2,1)} %get-tuple-element.134.refs_1_, ...), custom_call_target="tpu_custom_call", output_to_operand_aliasing={{0}: (0, {}), {1}: (1, {}), {2}: (2, {}), {3}: (3, {})} | custom-call | flops 14000000000 | bytes 1000 | tf_op jit(solution)/shard_map/finish/pallas_call | solution.py:87
  (8 shorter events, 0.1 us)
Async XLA Ops:
  0.6 4.6 %copy-start.1 = (bf16[1024,1024]{1,0:T(8,128)(2,1)S(1)}, bf16[1024,1024]{1,0:T(8,128)(2,1)}, u32[]{:S(2)}) copy-start(bf16[1024,1024]{1,0:T(8,128)(2,1)} %refs_4_.3) | copy-start | bytes 6291460
  0.7 4.6 %copy-start.2 = (bf16[1024,1024]{1,0:T(8,128)(2,1)S(1)}, bf16[1024,1024]{1,0:T(8,128)(2,1)}, u32[]{:S(2)}) copy-start(bf16[1024,1024]{1,0:T(8,128)(2,1)} %refs_5_.3) | copy-start | bytes 6291460
  2.0 15.3 %collective-permute-start.2 = (bf16[256,512]{1,0:T(8,128)(2,1)S(1)}, bf16[256,512]{1,0:T(8,128)(2,1)S(1)}, u32[]{:S(2)}, u32[]{:S(2)}) collective-permute-start(bf16[256,512]{1,0:T(8,128)(2,1)S(1)} %get-tuple-element.82), channel_id=1, source_target_pairs={{0,2},{1,3},{2,0},{3,1},{4,6},{5,7},{6,4},{7,5},{8,10},{9,11},{10,... | collective-permute-start | bytes 786440 | tf_op jit(solution)/shard_map/ppermute | solution.py:355
  5.1 12.3 %collective-permute-start.3 = (bf16[256,512]{1,0:T(8,128)(2,1)S(1)}, bf16[256,512]{1,0:T(8,128)(2,1)S(1)}, u32[]{:S(2)}, u32[]{:S(2)}) collective-permute-start(bf16[256,512]{1,0:T(8,128)(2,1)S(1)} %get-tuple-element.83), channel_id=1, source_target_pairs={{0,3},{1,2},{2,1},{3,0},{4,7},{5,6},{6,5},{7,4},{8,11},{9,10},{10,... | collective-permute-start | bytes 786440 | tf_op jit(solution)/shard_map/ppermute | solution.py:355
  5.1 3.3 %collective-permute-start = (bf16[256,1024]{1,0:T(8,128)(2,1)S(1)}, bf16[256,1024]{1,0:T(8,128)(2,1)S(1)}, u32[]{:S(2)}, u32[]{:S(2)}) collective-permute-start(bf16[256,1024]{1,0:T(8,128)(2,1)S(1)} %get-tuple-element.76), channel_id=1, source_target_pairs={{0,1},{1,0},{2,3},{3,2},{4,5},{5,4},{6,7},{7,6},{8,9},{9,8},{10,11... | collective-permute-start | bytes 1572872 | tf_op jit(solution)/shard_map/ppermute | solution.py:355
  6.4 8.6 %collective-permute-start.1 = (bf16[8,128,128]{2,1,0:T(8,128)(2,1)S(1)}, bf16[8,128,128]{2,1,0:T(8,128)(2,1)S(1)}, u32[]{:S(2)}, u32[]{:S(2)}) collective-permute-start(bf16[8,128,128]{2,1,0:T(8,128)(2,1)S(1)} %get-tuple-element.80.refs_4_), channel_id=1, source_target_pairs={{0,4},{4,0},{8,12},{12,8},{16,20},{20,16},{24,28},{28,24},{1,5},{5... | collective-permute-start | bytes 786440 | tf_op jit(solution)/shard_map/ppermute | solution.py:310
  8.3 3.0 %copy-start = (bf16[1024,1024]{1,0:T(8,128)(2,1)S(1)}, bf16[1024,1024]{1,0:T(8,128)(2,1)}, u32[]{:S(2)}) copy-start(bf16[1024,1024]{1,0:T(8,128)(2,1)} %refs_1_.22) | copy-start | bytes 6291460
  9.7 5.2 %copy-start.5 = (bf16[256,1024]{1,0:T(8,128)(2,1)}, bf16[256,1024]{1,0:T(8,128)(2,1)S(1)}, u32[]{:S(2)}) copy-start(bf16[256,1024]{1,0:T(8,128)(2,1)S(1)} %get-tuple-element.78.refs_4_.refs_2_.refs_3_.refs_6_) | copy-start | bytes 1572868
  9.8 16.4 %collective-permute-start.6 = (bf16[256,256]{1,0:T(8,128)(2,1)S(1)}, bf16[256,256]{1,0:T(8,128)(2,1)S(1)}, u32[]{:S(2)}, u32[]{:S(2)}) collective-permute-start(bf16[256,256]{1,0:T(8,128)(2,1)S(1)} %get-tuple-element.92), channel_id=1, source_target_pairs={{0,2},{1,3},{2,0},{3,1},{4,6},{5,7},{6,4},{7,5},{8,10},{9,11},{10,... | collective-permute-start | bytes 393224 | tf_op jit(solution)/shard_map/ppermute | solution.py:355
  11.3 14.8 %collective-permute-start.7 = (bf16[256,256]{1,0:T(8,128)(2,1)S(1)}, bf16[256,256]{1,0:T(8,128)(2,1)S(1)}, u32[]{:S(2)}, u32[]{:S(2)}) collective-permute-start(bf16[256,256]{1,0:T(8,128)(2,1)S(1)} %get-tuple-element.93), channel_id=1, source_target_pairs={{0,3},{1,2},{2,1},{3,0},{4,7},{5,6},{6,5},{7,4},{8,11},{9,10},{10,... | collective-permute-start | bytes 393224 | tf_op jit(solution)/shard_map/ppermute | solution.py:355
  15.0 0.7 %copy-start.3 = (bf16[8,128,128]{2,1,0:T(8,128)(2,1)}, bf16[8,128,128]{2,1,0:T(8,128)(2,1)S(1)}, u32[]{:S(2)}) copy-start(bf16[8,128,128]{2,1,0:T(8,128)(2,1)S(1)} %collective-permute-done.1.refs_5_.refs_19_.refs_22_) | copy-start | bytes 786436
  15.7 9.5 %collective-permute-start.4 = (bf16[8,128,128]{2,1,0:T(8,128)(2,1)S(1)}, bf16[8,128,128]{2,1,0:T(8,128)(2,1)S(1)}, u32[]{:S(2)}, u32[]{:S(2)}) collective-permute-start(bf16[8,128,128]{2,1,0:T(8,128)(2,1)S(1)} %get-tuple-element.89.refs_1_), channel_id=1, source_target_pairs={{0,8},{4,12},{8,0},{12,4},{16,24},{20,28},{24,16},{28,20},{1,9},{5... | collective-permute-start | bytes 786440 | tf_op jit(solution)/shard_map/ppermute | solution.py:310
  17.8 6.0 %collective-permute-start.5 = (bf16[4,128,128]{2,1,0:T(8,128)(2,1)S(1)}, bf16[4,128,128]{2,1,0:T(8,128)(2,1)S(1)}, u32[]{:S(2)}, u32[]{:S(2)}) collective-permute-start(bf16[4,128,128]{2,1,0:T(8,128)(2,1)S(1)} %get-tuple-element.90.refs_3_), channel_id=1, source_target_pairs={{0,4},{4,0},{8,12},{12,8},{16,20},{20,16},{24,28},{28,24},{1,5},{5... | collective-permute-start | bytes 393224 | tf_op jit(solution)/shard_map/ppermute | solution.py:310
  21.6 8.6 %collective-permute-start.8 = (bf16[256,256]{1,0:T(8,128)(2,1)S(1)}, bf16[256,256]{1,0:T(8,128)(2,1)S(1)}, u32[]{:S(2)}, u32[]{:S(2)}) collective-permute-start(bf16[256,256]{1,0:T(8,128)(2,1)S(1)} %get-tuple-element.96), channel_id=1, source_target_pairs={{0,2},{1,3},{2,0},{3,1},{4,6},{5,7},{6,4},{7,5},{8,10},{9,11},{10,... | collective-permute-start | bytes 393224 | tf_op jit(solution)/shard_map/ppermute | solution.py:355
  23.8 6.5 %collective-permute-start.9 = (bf16[256,256]{1,0:T(8,128)(2,1)S(1)}, bf16[256,256]{1,0:T(8,128)(2,1)S(1)}, u32[]{:S(2)}, u32[]{:S(2)}) collective-permute-start(bf16[256,256]{1,0:T(8,128)(2,1)S(1)} %get-tuple-element.97), channel_id=1, source_target_pairs={{0,3},{1,2},{2,1},{3,0},{4,7},{5,6},{6,5},{7,4},{8,11},{9,10},{10,... | collective-permute-start | bytes 393224 | tf_op jit(solution)/shard_map/ppermute | solution.py:355
  25.2 8.0 %collective-permute-start.11 = (bf16[4,128,128]{2,1,0:T(8,128)(2,1)S(1)}, bf16[4,128,128]{2,1,0:T(8,128)(2,1)S(1)}, u32[]{:S(2)}, u32[]{:S(2)}) collective-permute-start(bf16[4,128,128]{2,1,0:T(8,128)(2,1)S(1)} %get-tuple-element.102.refs_2_), channel_id=1, source_target_pairs={{0,8},{4,12},{8,0},{12,4},{16,24},{20,28},{24,16},{28,20},{1,9},{5... | collective-permute-start | bytes 393224 | tf_op jit(solution)/shard_map/ppermute | solution.py:310
  26.4 5.1 %collective-permute-start.10 = (bf16[2,128,128]{2,1,0:T(8,128)(2,1)S(1)}, bf16[2,128,128]{2,1,0:T(8,128)(2,1)S(1)}, u32[]{:S(2)}, u32[]{:S(2)}) collective-permute-start(bf16[2,128,128]{2,1,0:T(8,128)(2,1)S(1)} %get-tuple-element.99.refs_1_), channel_id=1, source_target_pairs={{0,4},{4,0},{8,12},{12,8},{16,20},{20,16},{24,28},{28,24},{1,5},{5... | collective-permute-start | bytes 196616 | tf_op jit(solution)/shard_map/ppermute | solution.py:310
  30.6 6.8 %collective-permute-start.12 = (bf16[2,128,128]{2,1,0:T(8,128)(2,1)S(1)}, bf16[2,128,128]{2,1,0:T(8,128)(2,1)S(1)}, u32[]{:S(2)}, u32[]{:S(2)}) collective-permute-start(bf16[2,128,128]{2,1,0:T(8,128)(2,1)S(1)} %get-tuple-element.105.refs_1_), channel_id=1, source_target_pairs={{0,4},{4,0},{8,12},{12,8},{16,20},{20,16},{24,28},{28,24},{1,5},{5... | collective-permute-start | bytes 196616 | tf_op jit(solution)/shard_map/ppermute | solution.py:310
  31.6 7.5 %collective-permute-start.13 = (bf16[2,128,128]{2,1,0:T(8,128)(2,1)S(1)}, bf16[2,128,128]{2,1,0:T(8,128)(2,1)S(1)}, u32[]{:S(2)}, u32[]{:S(2)}) collective-permute-start(bf16[2,128,128]{2,1,0:T(8,128)(2,1)S(1)} %get-tuple-element.108.refs_2_), channel_id=1, source_target_pairs={{0,8},{4,12},{8,0},{12,4},{16,24},{20,28},{24,16},{28,20},{1,9},{5... | collective-permute-start | bytes 196616 | tf_op jit(solution)/shard_map/ppermute | solution.py:310
  33.4 10.1 %collective-permute-start.15 = (bf16[4,128,128]{2,1,0:T(8,128)(2,1)S(1)}, bf16[4,128,128]{2,1,0:T(8,128)(2,1)S(1)}, u32[]{:S(2)}, u32[]{:S(2)}) collective-permute-start(bf16[4,128,128]{2,1,0:T(8,128)(2,1)S(1)} %get-tuple-element.123), channel_id=1, source_target_pairs={{0,16},{4,20},{8,24},{12,28},{16,0},{20,4},{24,8},{28,12},{1,17},{... | collective-permute-start | bytes 393224 | tf_op jit(solution)/shard_map/ppermute | solution.py:310
  37.4 6.1 %collective-permute-start.14 = (bf16[2,128,128]{2,1,0:T(8,128)(2,1)S(1)}, bf16[2,128,128]{2,1,0:T(8,128)(2,1)S(1)}, u32[]{:S(2)}, u32[]{:S(2)}) collective-permute-start(bf16[2,128,128]{2,1,0:T(8,128)(2,1)S(1)} %get-tuple-element.110.refs_2_), channel_id=1, source_target_pairs={{0,8},{4,12},{8,0},{12,4},{16,24},{20,28},{24,16},{28,20},{1,9},{5... | collective-permute-start | bytes 196616 | tf_op jit(solution)/shard_map/ppermute | solution.py:310
  39.2 8.1 %collective-permute-start.16 = (bf16[2,128,128]{2,1,0:T(8,128)(2,1)S(1)}, bf16[2,128,128]{2,1,0:T(8,128)(2,1)S(1)}, u32[]{:S(2)}, u32[]{:S(2)}) collective-permute-start(bf16[2,128,128]{2,1,0:T(8,128)(2,1)S(1)} %get-tuple-element.132), channel_id=1, source_target_pairs={{0,16},{4,20},{8,24},{12,28},{16,0},{20,4},{24,8},{28,12},{1,17},{... | collective-permute-start | bytes 196616 | tf_op jit(solution)/shard_map/ppermute | solution.py:310
  43.5 1.0 %copy-start.4 = (bf16[8,128,128]{2,1,0:T(8,128)(2,1)S(1)}, bf16[8,128,128]{2,1,0:T(8,128)(2,1)}, u32[]{:S(2)}) copy-start(bf16[8,128,128]{2,1,0:T(8,128)(2,1)} %copy-done.3) | copy-start | bytes 786436
  43.5 1.1 %copy-start.6 = (bf16[256,1024]{1,0:T(8,128)(2,1)S(1)}, bf16[256,1024]{1,0:T(8,128)(2,1)}, u32[]{:S(2)}) copy-start(bf16[256,1024]{1,0:T(8,128)(2,1)} %copy-done.5) | copy-start | bytes 1572868
  43.5 5.6 %collective-permute-start.17 = (bf16[2,128,128]{2,1,0:T(8,128)(2,1)S(1)}, bf16[2,128,128]{2,1,0:T(8,128)(2,1)S(1)}, u32[]{:S(2)}, u32[]{:S(2)}) collective-permute-start(bf16[2,128,128]{2,1,0:T(8,128)(2,1)S(1)} %get-tuple-element.141), channel_id=1, source_target_pairs={{0,16},{4,20},{8,24},{12,28},{16,0},{20,4},{24,8},{28,12},{1,17},{... | collective-permute-start | bytes 196616 | tf_op jit(solution)/shard_map/ppermute | solution.py:310
